TPU v7x, 32 devices: a whole 2x2x4 slice. The times are simulated.
32 devices in a mesh: section: 2 (over core), wide: 16 (over z, y, x).
Axes of the slice: x: 2, y: 2, z: 4, core: 2. Of those that a mesh axis runs over, the one named last changes fastest.
Arguments:
- fields: bfloat16 [8, 1024, 512], P(None, 'wide'), may hold values from -6 to 6
- pixel_mask: int32 [8, 1024, 128], P(None, 'wide'), may hold values from 0 to 1
- channel_counts: int32 [8, 8], replicated, may hold values from 1 to 4, as said below
- kernels: bfloat16 [2, 1600], P('section'), may hold values from -0.625 to 0.625
- enc_bias: float32 [16], replicated, may hold values from -3 to 3
- dec_bias: float32 [4], replicated, may hold values from -3 to 3
- cotangent: bfloat16 [8, 1024, 512], P(None, 'wide'), may hold values from -6 to 6
- run_mean: float32 [16], replicated, may hold values from -4 to 4
- run_cov: float32 [16, 16], replicated, may hold values from -4 to 4
Outputs:
- pixels_out: bfloat16 [2, 8, 1024, 512], P('section', None, 'wide')
- kernel_grads: float32 [2, 1600], P('section')
- enc_bias_grad: float32 [16], replicated
- dec_bias_grad: float32 [4], replicated
- new_mean: float32 [16], replicated
- new_cov: float32 [16, 16], replicated
Inputs may be any that keep to these rules, and one draw needn't show every extreme that they name: `channel_counts`: each is 1, 2 or 4; within a micro-batch the counts never fall from one field to the next.
All inputs are finite; a program needn't handle non-finite values.
Results may differ from a plain program's by a relative error of at most 0.0058.
Values may be sent and summed in bfloat16 or wider, within the bound.
No kernel may reach another device: no remote copies, remote signals or barrier semaphores. Data moves between devices by JAX's collectives and lax.ppermute only.
A program may use at most 192 MiB of HBM per device.

v0:
```python
import jax
import jax.numpy as jnp
from jax import lax
from jax.sharding import PartitionSpec as P

CIN = 4
CCODE = 16
KS = 5
HW = 128


decay_rate = 0.9
whiten_weight = 0.25


def shortened(x):

    def short(part):
        return part.astype(jnp.bfloat16) if part.dtype == jnp.float32 else part

    return jax.tree.map(short, x)


def extended(x, sides, width):
    for axis, dim in sides:
        peers, length = (lax.axis_size(axis), x.shape[dim])
        up = [(i, (i + 1) % peers) for i in range(peers - 1)]
        down = [(j, i) for i, j in up]
        last = lax.slice_in_dim(x, length - width, length, axis=dim)
        first = lax.slice_in_dim(x, 0, width, axis=dim)
        before = lax.ppermute(last, axis, up)
        after = lax.ppermute(first, axis, down)
        x = jnp.concatenate([before, x, after], axis=dim)
    return x


def partner(x, axis, stride):
    return lax.ppermute(x, axis, [(i, i ^ 1 << stride) for i in range(lax.axis_size(axis))])


def smooth_unit(values):
    return jnp.where(values > 0, values, jnp.expm1(jnp.minimum(values, 0.0)))


def unit_slope(values):
    return jnp.where(values > 0, 1.0, jnp.exp(jnp.minimum(values, 0.0)))


def moment_parts(layout, weights):
    weights_low = weights.astype(jnp.bfloat16)
    first_part = jnp.einsum("bjcu,bju->c", layout, weights_low, preferred_element_type=jnp.float32)
    second_part = jnp.einsum(
        "bjcu,bjdu->cd",
        layout * weights_low[:, :, None, :],
        layout,
        preferred_element_type=jnp.float32,
    )
    return (first_part, second_part, jnp.sum(weights))


def shards(
    fields, pixel_mask, channel_counts, kernels, enc_bias, dec_bias, cotangent, run_mean, run_cov
):
    section_index = lax.axis_index("section")
    micro_count, band_rows, row_span = fields.shape
    half_rows = band_rows // 2
    coarse_width = CCODE * (HW // 2)
    band_start = lax.axis_index("wide") * band_rows
    field_now = band_start // HW
    top_open = band_start % HW != 0
    bottom_open = (band_start + band_rows) % HW != 0
    selector = jnp.arange(channel_counts.shape[1]) == field_now
    count_now = jnp.sum(jnp.where(selector[None, :], channel_counts, 0), axis=1)
    chan_valid = (jnp.arange(CIN)[None, :] < count_now[:, None]).astype(jnp.float32)
    pixel_valid = pixel_mask.astype(jnp.float32)
    input_mask = (chan_valid[:, None, :, None] * pixel_valid[:, :, None, :]).reshape(
        micro_count, band_rows, row_span
    )
    code_mask = pixel_valid[:, ::2, ::2]
    masked_input = fields * input_mask.astype(jnp.bfloat16)
    encode_bias = jnp.repeat(enc_bias, HW // 2)
    decode_bias = jnp.repeat(dec_bias, HW)

    def trim_edges(widened):
        length = widened.shape[1]
        places = jnp.arange(length)
        keeping = ((places >= 2) | top_open) & ((places < length - 2) | bottom_open)
        return widened * keeping[None, :, None].astype(widened.dtype)

    def strided_conv(widened, kern):
        batch = widened.shape[0]
        shaped = widened.reshape(batch, band_rows + 4, CIN, HW)
        result = lax.conv_general_dilated(
            shaped,
            kern,
            (2, 2),
            ((0, 0), (2, 2)),
            dimension_numbers=("NHCW", "OIHW", "NHCW"),
            preferred_element_type=jnp.float32,
        )
        return result.reshape(batch, half_rows, coarse_width)

    def spread_conv(widened, kern):
        batch = widened.shape[0]
        shaped = widened.reshape(batch, half_rows + 2, CCODE, HW // 2)
        result = lax.conv_general_dilated(
            shaped,
            kern[:, :, ::-1, ::-1],
            (1, 1),
            ((0, 1), (2, 3)),
            lhs_dilation=(2, 2),
            dimension_numbers=("NHCW", "IOHW", "NHCW"),
            preferred_element_type=jnp.float32,
        )
        return result.reshape(batch, band_rows, row_span)

    def kernel_terms(fine_rows, coarse_rows):
        batch = fine_rows.shape[0]
        finer = fine_rows[:, : band_rows + 3].reshape(batch, band_rows + 3, CIN, HW)
        coarser = coarse_rows.reshape(batch, half_rows, CCODE, HW // 2)
        return lax.conv_general_dilated(
            finer,
            coarser,
            (1, 1),
            ((0, 0), (2, 1)),
            rhs_dilation=(2, 2),
            dimension_numbers=("CHNW", "IHOW", "CNHW"),
            preferred_element_type=jnp.float32,
        )

    own_kernel = kernels[0].reshape(CCODE, CIN, KS, KS)
    group_size = 1
    round_count = micro_count // group_size
    received = jnp.zeros((group_size, band_rows, row_span), jnp.bfloat16)
    kept_codes, kept_preacts, kept_inputs, kept_grads, kept_recons = ([], [], [], [], [])
    first_sum = jnp.zeros((CCODE,), jnp.float32)
    second_sum = jnp.zeros((CCODE, CCODE), jnp.float32)
    valid_total = jnp.zeros((), jnp.float32)
    decode_kernel = jnp.zeros((CCODE, CIN, KS, KS), jnp.float32)
    decode_shift = jnp.zeros((CIN,), jnp.float32)
    for turn_index in range(round_count + 1):
        leading = min(turn_index, round_count - 1) * group_size
        trailing = max(turn_index - 1, 0) * group_size
        current = jnp.where(
            section_index == 0, masked_input[leading : leading + group_size], received
        )
        widened = trim_edges(extended(shortened(current), (("wide", 1),), 2).astype(current.dtype))
        incoming = received

        def encode_turn():
            preact = strided_conv(widened, own_kernel) + encode_bias
            codes_now = smooth_unit(preact).astype(jnp.bfloat16)
            layout = codes_now.reshape(group_size, half_rows, CCODE, HW // 2)
            even_rows = ((leading + jnp.arange(group_size)) % 2 == 0).astype(jnp.float32)
            weights_now = code_mask[leading : leading + group_size] * even_rows[:, None, None]
            first_part, second_part, valid_part = moment_parts(layout, weights_now)
            return (
                codes_now.reshape(group_size, band_rows, row_span),
                preact.reshape(group_size, band_rows, row_span),
                first_part,
                second_part,
                valid_part,
            )

        def decode_turn():
            rawact_now = spread_conv(widened, own_kernel) + decode_bias
            mask_now = input_mask[trailing : trailing + group_size]
            recon = smooth_unit(rawact_now) * mask_now
            slope = (
                cotangent[trailing : trailing + group_size].astype(jnp.float32)
                * mask_now
                * unit_slope(rawact_now)
            )
            layout = incoming.reshape(group_size, half_rows, CCODE, HW // 2)
            odd_rows = ((trailing + jnp.arange(group_size)) % 2 == 1).astype(jnp.float32)
            weights_now = code_mask[trailing : trailing + group_size] * odd_rows[:, None, None]
            first_part, second_part, valid_part = moment_parts(layout, weights_now)
            return (slope.astype(jnp.bfloat16), recon, first_part, second_part, valid_part)

        outgoing, kept_now, first_part, second_part, valid_part = lax.cond(
            section_index == 0, encode_turn, decode_turn
        )
        grad_rows = trim_edges(extended(outgoing, (("wide", 1),), 2))

        def decode_back():
            code_grad = (
                strided_conv(grad_rows, own_kernel)
                .astype(jnp.bfloat16)
                .reshape(group_size, band_rows, row_span)
            )
            kernel_part = kernel_terms(
                grad_rows, received.reshape(group_size, half_rows, coarse_width)
            )
            shift_part = jnp.sum(
                outgoing.astype(jnp.float32).reshape(group_size, band_rows, CIN, HW), axis=(0, 1, 3)
            )
            return (code_grad, kernel_part, shift_part)

        def encode_wait():
            return (
                jnp.zeros((group_size, band_rows, row_span), jnp.bfloat16),
                jnp.zeros((CCODE, CIN, KS, KS), jnp.float32),
                jnp.zeros((CIN,), jnp.float32),
            )

        returned, kernel_part, shift_part = lax.cond(section_index == 0, encode_wait, decode_back)
        payload = jnp.where(section_index == 0, outgoing, returned)
        arrived = partner(shortened(payload), "section", 0).astype(payload.dtype)
        part_scale = jnp.where(
            section_index == 0, float(turn_index < round_count), float(turn_index >= 1)
        )
        first_sum = first_sum + part_scale * first_part
        second_sum = second_sum + part_scale * second_part
        valid_total = valid_total + part_scale * valid_part
        if turn_index < round_count:
            kept_codes.append(outgoing)
            kept_preacts.append(kept_now)
            kept_inputs.append(widened)
        if turn_index >= 1:
            kept_grads.append(arrived)
            kept_recons.append(kept_now)
            decode_kernel = decode_kernel + kernel_part
            decode_shift = decode_shift + shift_part
        received = arrived
    all_codes = jnp.concatenate(kept_codes, axis=0)
    all_preacts = jnp.concatenate(kept_preacts, axis=0)
    all_inputs = jnp.concatenate(kept_inputs, axis=0)
    all_grads = jnp.concatenate(kept_grads, axis=0)
    all_recons = jnp.concatenate(kept_recons, axis=0)
    first_sum, second_sum, valid_total = lax.psum(
        (first_sum, second_sum, valid_total), ("section", "wide")
    )
    mean = first_sum / valid_total
    cov = second_sum / valid_total - jnp.outer(mean, mean)
    new_mean = decay_rate * run_mean + (1.0 - decay_rate) * mean
    new_cov = decay_rate * run_cov + (1.0 - decay_rate) * cov
    offset = cov - jnp.eye(CCODE, dtype=jnp.float32)

    def encode_grad():
        layout = all_codes.reshape(micro_count, half_rows, CCODE, HW // 2).astype(jnp.float32)
        centered = layout - mean[None, None, :, None]
        turned = jnp.einsum("cd,bjdu->bjcu", offset, centered, precision=lax.Precision.HIGHEST)
        penalty_grad = (
            whiten_weight * (2.0 * turned + mean[None, None, :, None]) * code_mask[:, :, None, :]
        )
        code_grad = all_grads.astype(jnp.float32).reshape(micro_count, half_rows, coarse_width)
        code_grad = code_grad + penalty_grad.reshape(micro_count, half_rows, coarse_width)
        slope = code_grad * unit_slope(all_preacts.reshape(micro_count, half_rows, coarse_width))
        return slope.astype(jnp.bfloat16).reshape(micro_count, band_rows, row_span)

    def decode_rest():
        return jnp.zeros((micro_count, band_rows, row_span), jnp.bfloat16)

    preact_grad = lax.cond(section_index == 0, encode_grad, decode_rest)
    grad_wide = trim_edges(extended(preact_grad, (("wide", 1),), 2))

    def encode_finish():
        input_grad = (spread_conv(grad_wide, own_kernel) * input_mask).astype(jnp.bfloat16)
        kernel_part = kernel_terms(
            all_inputs, preact_grad.reshape(micro_count, half_rows, coarse_width)
        )
        shift_part = jnp.sum(
            preact_grad.astype(jnp.float32).reshape(micro_count, half_rows, CCODE, HW // 2),
            axis=(0, 1, 3),
        )
        return (input_grad, kernel_part, shift_part)

    def decode_finish():
        return (
            all_recons.astype(jnp.bfloat16),
            jnp.zeros((CCODE, CIN, KS, KS), jnp.float32),
            jnp.zeros((CCODE,), jnp.float32),
        )

    pixel_block, encode_kernel, encode_shift = lax.cond(
        section_index == 0, encode_finish, decode_finish
    )
    pixels = pixel_block[None]
    kernel_total = (encode_kernel + decode_kernel).reshape(1, CCODE * CIN * KS * KS)
    kernel_rows = jnp.where(
        jnp.arange(lax.axis_size("section"))[:, None] == section_index, kernel_total, 0.0
    )
    summed, encode_total, decode_total = lax.psum(
        (kernel_rows, encode_shift, decode_shift), ("section", "wide")
    )
    own_rows = lax.dynamic_slice_in_dim(summed, section_index, 1, 0)
    return (pixels, own_rows, encode_total, decode_total, new_mean, new_cov)


def solution(mesh):
    in_specs = (
        P(None, "wide", None),
        P(None, "wide", None),
        P(),
        P("section", None),
        P(),
        P(),
        P(None, "wide", None),
        P(),
        P(),
    )
    out_specs = (P("section", None, "wide", None), P("section", None), P(), P(), P(), P())
    return jax.shard_map(shards, mesh=mesh, in_specs=in_specs, out_specs=out_specs, check_vma=False)
```

profile of v0, /device:TPU:0, one launch (start us, length us, event | category | flops | bytes accessed | tf_op | source)
XLA Modules:
  0.0 1072.9 jit_solution(10033344770160734635)
XLA Ops:
  4.6 4.8 collective-permute-start
  15.8 15.2 %conditional.29 = (f32[16]{0:T(128)S(1)}, f32[16,16]{1,0:T(8,128)S(1)}, f32[1,32,64]{2,1,0:T(8,128)}, f32[]{:T(128)}, bf16[1,64,512]{2,1,0:T(8,128)(2,1)S(1)}, /*index=5*/f32[1,64,512]{2,1,0:T(8,128)S(1)}) conditional(s32[]{:T(128)} %convert_element_type.531, (bf16[8,64,512]{2,1,0:T(8,128)(2,1)S(1)}, f32[8,64,512]{2,1,0:T(8,128)S(1)}, ...), branch_computations={%region_1.2_spmd, %region_2.3_spmd} | conditional | flops 9568768 | bytes 6055782
  19.5 4.7 fusion.25
  31.6 4.3 collective-permute-start.2
  37.2 4.2 collective-permute-done.3
  42.1 32.6 %collective-permute-start.4 = (bf16[1,64,512]{2,1,0:T(8,128)(2,1)S(1)}, bf16[1,64,512]{2,1,0:T(8,128)(2,1)S(1)}, u32[]{:S(2)}, u32[]{:S(2)}) collective-permute-start(bf16[1,64,512]{2,1,0:T(8,128)(2,1)S(1)} %get-tuple-element.2084), channel_id=1, source_target_pairs={{0,16},{16,0},{1,17},{17,1},{2,18},{18,2},{3,19},{19,3},{4,20},{20... | collective-permute-start | bytes 196616 | tf_op jit(solution)/shard_map/ppermute | solution.py:38
  75.7 4.5 collective-permute-start.5
  81.6 4.2 collective-permute-done.6
  86.5 15.1 %conditional.31 = (f32[16]{0:T(128)S(1)}, f32[16,16]{1,0:T(8,128)S(1)}, f32[1,32,64]{2,1,0:T(8,128)}, f32[]{:T(128)}, f32[1,64,512]{2,1,0:T(8,128)S(1)}, /*index=5*/bf16[1,64,512]{2,1,0:T(8,128)(2,1)S(1)}) conditional(s32[]{:T(128)} %convert_element_type.531, (bf16[8,64,512]{2,1,0:T(8,128)(2,1)S(1)}, f32[8,64,512]{2,1,0:T(8,128)S(1)}, ...), branch_computations={%region_5.6_spmd, %region_6.7_spmd} | conditional | flops 9570816 | bytes 6907750
  90.0 4.7 fusion.69
  101.6 4.7 collective-permute-start.7
  111.8 8.4 conditional.32
  120.9 39.7 %collective-permute-start.9 = (bf16[1,64,512]{2,1,0:T(8,128)(2,1)S(1)}, bf16[1,64,512]{2,1,0:T(8,128)(2,1)S(1)}, u32[]{:S(2)}, u32[]{:S(2)}) collective-permute-start(bf16[1,64,512]{2,1,0:T(8,128)(2,1)S(1)} %get-tuple-element.2082), channel_id=1, source_target_pairs={{0,16},{16,0},{1,17},{17,1},{2,18},{18,2},{3,19},{19,3},{4,20},{20... | collective-permute-start | bytes 196616 | tf_op jit(solution)/shard_map/ppermute | solution.py:38
  162.2 4.5 collective-permute-start.10
  168.0 4.2 collective-permute-done.11
  172.9 20.4 %conditional.33 = (f32[16]{0:T(128)S(1)}, f32[16,16]{1,0:T(8,128)S(1)}, f32[1,32,64]{2,1,0:T(8,128)}, f32[]{:T(128)}, f32[1,64,512]{2,1,0:T(8,128)S(1)}, /*index=5*/bf16[1,64,512]{2,1,0:T(8,128)(2,1)S(1)}) conditional(s32[]{:T(128)} %convert_element_type.531, (bf16[8,64,512]{2,1,0:T(8,128)(2,1)S(1)}, f32[8,64,512]{2,1,0:T(8,128)S(1)}, ...), branch_computations={%region_11.12_spmd, %region_12.13_spmd} | conditional | flops 9568768 | bytes 6940546
  183.0 4.7 fusion.113
  198.7 4.2 collective-permute-done.13
  202.9 8.4 conditional.34
  212.0 35.0 %collective-permute-start.14 = (bf16[1,64,512]{2,1,0:T(8,128)(2,1)S(1)}, bf16[1,64,512]{2,1,0:T(8,128)(2,1)S(1)}, u32[]{:S(2)}, u32[]{:S(2)}) collective-permute-start(bf16[1,64,512]{2,1,0:T(8,128)(2,1)S(1)} %get-tuple-element.2080), channel_id=1, source_target_pairs={{0,16},{16,0},{1,17},{17,1},{2,18},{18,2},{3,19},{19,3},{4,20},{20... | collective-permute-start | bytes 196616 | tf_op jit(solution)/shard_map/ppermute | solution.py:38
  253.8 4.2 collective-permute-done.16
  258.7 20.6 %conditional.35 = (f32[16]{0:T(128)S(1)}, f32[16,16]{1,0:T(8,128)S(1)}, f32[1,32,64]{2,1,0:T(8,128)}, f32[]{:T(128)}, f32[1,64,512]{2,1,0:T(8,128)S(1)}, /*index=5*/bf16[1,64,512]{2,1,0:T(8,128)(2,1)S(1)}) conditional(s32[]{:T(128)} %convert_element_type.531, (bf16[8,64,512]{2,1,0:T(8,128)(2,1)S(1)}, f32[8,64,512]{2,1,0:T(8,128)S(1)}, ...), branch_computations={%region_17.18_spmd, %region_18.19_spmd} | conditional | flops 9570816 | bytes 6940546
  269.0 4.7 fusion.157
  284.7 4.2 collective-permute-done.18
  288.9 8.2 conditional.36
  297.8 34.7 %collective-permute-start.19 = (bf16[1,64,512]{2,1,0:T(8,128)(2,1)S(1)}, bf16[1,64,512]{2,1,0:T(8,128)(2,1)S(1)}, u32[]{:S(2)}, u32[]{:S(2)}) collective-permute-start(bf16[1,64,512]{2,1,0:T(8,128)(2,1)S(1)} %get-tuple-element.2078), channel_id=1, source_target_pairs={{0,16},{16,0},{1,17},{17,1},{2,18},{18,2},{3,19},{19,3},{4,20},{20... | collective-permute-start | bytes 196616 | tf_op jit(solution)/shard_map/ppermute | solution.py:38
  334.1 4.3 collective-permute-start.20
  339.7 4.2 collective-permute-done.21
  344.6 20.6 %conditional.37 = (f32[16]{0:T(128)S(1)}, f32[16,16]{1,0:T(8,128)S(1)}, f32[1,32,64]{2,1,0:T(8,128)}, f32[]{:T(128)}, f32[1,64,512]{2,1,0:T(8,128)S(1)}, /*index=5*/bf16[1,64,512]{2,1,0:T(8,128)(2,1)S(1)}) conditional(s32[]{:T(128)} %convert_element_type.531, (bf16[8,64,512]{2,1,0:T(8,128)(2,1)S(1)}, f32[8,64,512]{2,1,0:T(8,128)S(1)}, ...), branch_computations={%region_23.24_spmd, %region_24.25_spmd} | conditional | flops 9568768 | bytes 6940546
  354.9 4.7 fusion.201
  370.5 4.2 collective-permute-done.23
  374.8 8.5 conditional.38
  383.9 34.6 %collective-permute-start.24 = (bf16[1,64,512]{2,1,0:T(8,128)(2,1)S(1)}, bf16[1,64,512]{2,1,0:T(8,128)(2,1)S(1)}, u32[]{:S(2)}, u32[]{:S(2)}) collective-permute-start(bf16[1,64,512]{2,1,0:T(8,128)(2,1)S(1)} %get-tuple-element.2076), channel_id=1, source_target_pairs={{0,16},{16,0},{1,17},{17,1},{2,18},{18,2},{3,19},{19,3},{4,20},{20... | collective-permute-start | bytes 196616 | tf_op jit(solution)/shard_map/ppermute | solution.py:38
  430.2 20.4 %conditional.39 = (f32[16]{0:T(128)S(1)}, f32[16,16]{1,0:T(8,128)S(1)}, f32[1,32,64]{2,1,0:T(8,128)S(1)}, f32[]{:T(128)}, f32[1,64,512]{2,1,0:T(8,128)S(1)}, /*index=5*/bf16[1,64,512]{2,1,0:T(8,128)(2,1)S(1)}) conditional(s32[]{:T(128)} %convert_element_type.531, (bf16[8,64,512]{2,1,0:T(8,128)(2,1)S(1)}, f32[8,64,512]{2,1,0:T(8,128)S(1)}, ...), branch_computations={%region_29.30_spmd, %region_30.31_spmd} | conditional | flops 9570816 | bytes 6907750
  440.3 4.7 fusion.245
  460.2 8.5 conditional.40
  469.4 34.9 %collective-permute-start.29 = (bf16[1,64,512]{2,1,0:T(8,128)(2,1)S(1)}, bf16[1,64,512]{2,1,0:T(8,128)(2,1)S(1)}, u32[]{:S(2)}, u32[]{:S(2)}) collective-permute-start(bf16[1,64,512]{2,1,0:T(8,128)(2,1)S(1)} %get-tuple-element.2074), channel_id=1, source_target_pairs={{0,16},{16,0},{1,17},{17,1},{2,18},{18,2},{3,19},{19,3},{4,20},{20... | collective-permute-start | bytes 196616 | tf_op jit(solution)/shard_map/ppermute | solution.py:38
  506.5 4.3 collective-permute-start.30
  517.0 20.7 %conditional.41 = (f32[16]{0:T(128)S(1)}, f32[16,16]{1,0:T(8,128)S(1)}, f32[1,32,64]{2,1,0:T(8,128)}, f32[]{:T(128)}, f32[1,64,512]{2,1,0:T(8,128)S(1)}, /*index=5*/bf16[1,64,512]{2,1,0:T(8,128)(2,1)S(1)}) conditional(s32[]{:T(128)} %convert_element_type.531, (bf16[8,64,512]{2,1,0:T(8,128)(2,1)S(1)}, f32[8,64,512]{2,1,0:T(8,128)S(1)}, ...), branch_computations={%region_35.36_spmd, %region_36.37_spmd} | conditional | flops 9568768 | bytes 6940546
  527.4 4.7 fusion.289
  538.3 4.6 collective-permute-start.32
  548.5 8.3 conditional.42
  557.5 35.4 %collective-permute-start.34 = (bf16[1,64,512]{2,1,0:T(8,128)(2,1)S(1)}, bf16[1,64,512]{2,1,0:T(8,128)(2,1)S(1)}, u32[]{:S(2)}, u32[]{:S(2)}) collective-permute-start(bf16[1,64,512]{2,1,0:T(8,128)(2,1)S(1)} %get-tuple-element.2072), channel_id=1, source_target_pairs={{0,16},{16,0},{1,17},{17,1},{2,18},{18,2},{3,19},{19,3},{4,20},{20... | collective-permute-start | bytes 196616 | tf_op jit(solution)/shard_map/ppermute | solution.py:38
  594.4 4.6 collective-permute-start.35
  605.8 20.8 %conditional.43 = (f32[16]{0:T(128)S(1)}, f32[16,16]{1,0:T(8,128)S(1)}, f32[1,32,64]{2,1,0:T(8,128)S(1)}, f32[]{:T(128)}, f32[1,64,512]{2,1,0:T(8,128)S(1)}, /*index=5*/bf16[1,64,512]{2,1,0:T(8,128)(2,1)S(1)}) conditional(s32[]{:T(128)} %convert_element_type.531, (bf16[8,64,512]{2,1,0:T(8,128)(2,1)S(1)}, f32[8,64,512]{2,1,0:T(8,128)S(1)}, ...), branch_computations={%region_41.42_spmd, %region_42.43_spmd} | conditional | flops 9570816 | bytes 6907750
  616.1 4.7 fusion.333
  627.0 4.8 collective-permute-start.37
  637.5 7.1 conditional.44
  645.9 36.9 %collective-permute-start.39 = (bf16[1,64,512]{2,1,0:T(8,128)(2,1)S(1)}, bf16[1,64,512]{2,1,0:T(8,128)(2,1)S(1)}, u32[]{:S(2)}, u32[]{:S(2)}) collective-permute-start(bf16[1,64,512]{2,1,0:T(8,128)(2,1)S(1)} %get-tuple-element.2070), channel_id=1, source_target_pairs={{0,16},{16,0},{1,17},{17,1},{2,18},{18,2},{3,19},{19,3},{4,20},{20... | collective-permute-start | bytes 196616 | tf_op jit(solution)/shard_map/ppermute | solution.py:38
  684.3 5.1 collective-permute-start.40
  696.6 27.6 %conditional.45 = (f32[16]{0:T(128)S(1)}, f32[16,16]{1,0:T(8,128)S(1)}, f32[1,32,64]{2,1,0:T(8,128)S(1)}, f32[]{:T(128)}, bf16[1,64,512]{2,1,0:T(8,128)(2,1)S(1)}, /*index=5*/bf16[1,64,512]{2,1,0:T(8,128)(2,1)S(1)}) conditional(s32[]{:T(128)} %convert_element_type.531, (bf16[8,64,512]{2,1,0:T(8,128)(2,1)S(1)}, f32[8,64,512]{2,1,0:T(8,128)S(1)}, ...), branch_computations={%region_47.48_spmd, %region_48.49_spmd} | conditional | flops 9603584 | bytes 6711142
  715.7 4.7 fusion.377
  724.3 4.8 collective-permute-start.42
  731.8 46.0 %all-reduce.1 = (f32[16]{0:T(128)S(1)}, f32[]{:T(128)}, f32[16,16]{1,0:T(8,128)S(1)}) all-reduce(f32[16]{0:T(128)S(1)} %multiply_add_fusion.3, f32[]{:T(128)S(6)} %add.738, f32[16,16]{1,0:T(8,128)S(1)} %multiply_add_fusion.1), channel_id=1, replica_groups=mesh['section'=2,'wide'=16] {'section','wide'}, use_global_device_ids=true, to_apply=%region_49.50 | all-reduce | flops 273 | bytes 2184 | tf_op jit(solution)/shard_map/psum | solution.py:230
  781.4 34.3 %collective-permute-start.44 = (bf16[1,64,512]{2,1,0:T(8,128)(2,1)S(1)}, bf16[1,64,512]{2,1,0:T(8,128)(2,1)S(1)}, u32[]{:S(2)}, u32[]{:S(2)}) collective-permute-start(bf16[1,64,512]{2,1,0:T(8,128)(2,1)S(1)} %broadcast_select_fusion), channel_id=1, source_target_pairs={{0,16},{16,0},{1,17},{17,1},{2,18},{18,2},{3,19},{19,3},{4,20},{20... | collective-permute-start | bytes 196616 | tf_op jit(solution)/shard_map/ppermute | solution.py:38
  817.3 10.5 conditional.47
  819.2 5.1 multiply_bitcast_fusion.1
  832.3 4.2 collective-permute-done.46
  836.7 191.1 %conditional.48 = (f32[16,4,5,5]{0,1,3,2:T(4,128)S(1)}, f32[16]{0:T(128)S(1)}, bf16[8,64,512]{2,1,0:T(8,128)(2,1)S(1)}) conditional(s32[]{:T(128)} %convert_element_type.531, bf16[8,64,512]{2,1,0:T(8,128)(2,1)S(1)} %copy-done.45, (bf16[8,68,512]{2,1,0:T(8,128)(2,1)}, bf16[8,64,512]{2,1,0:T(8,128)(2,1)S(1)}, bf16[68]{0:T(256)(128)(2,1)S(1)}, ...), branch_computations={%region_67.68_spmd, %region_68.71_spmd} | conditional | flops 104939504 | bytes 19308388 | solution.py:275
  842.3 8.4 copy.1198
  850.7 11.1 %fusion.437 = f32[16,4,5,5]{0,1,3,2:T(4,128)S(1)} fusion(bf16[8,67,4,128]{0,2,3,1:T(4,128)(2,1)} %copy.1198, bf16[8,32,16,64]{2,0,3,1:T(8,128)(2,1)} %copy.1199), kind=kOutput, calls=%fused_computation.699 | convolution fusion | flops 51937280 | bytes 1079552 | tf_op jit(solution)/shard_map/cond/branch_1_fun/conv_general_dilated | solution.py:121
  868.9 143.7 %fusion.438 = f32[8,64,4,128]{0,2,3,1:T(4,128)} fusion(bf16[8,34,16,64]{2,0,3,1:T(8,128)(2,1)} %copy.1200, bf16[16,4,5,5]{0,1,3,2:T(4,128)(2,1)S(1)} %copy.1273), kind=kOutput, calls=%fused_computation.700 | convolution fusion | flops 51937280 | bytes 1608832 | tf_op jit(solution)/shard_map/cond/branch_1_fun/conv_general_dilated | solution.py:106
  1012.5 12.3 %copy.1201 = f32[8,64,4,128]{3,2,1,0:T(4,128)S(1)} copy(f32[8,64,4,128]{0,2,3,1:T(4,128)} %fusion.438) | data formatting | bytes 2097152 | tf_op jit(solution)/shard_map/cond/branch_1_fun/conv_general_dilated | solution.py:106
  1029.7 42.2 %all-reduce = (f32[2,1600]{1,0:T(2,128)S(1)}, f32[16]{0:T(128)}, f32[4]{0:T(128)}) all-reduce(f32[2,1600]{1,0:T(2,128)S(1)} %broadcast_select_fusion.11, f32[16]{0:T(128)S(1)} %get-tuple-element.993, f32[4]{0:T(128)S(1)} %add_add_fusion.1), channel_id=1, replica_groups=mesh['section'=2,'wide'=16] {'section','wide'}, use_global_device_ids=true, to_apply=%region_71.72 | all-reduce | flops 3220 | bytes 25760 | tf_op jit(solution)/shard_map/psum | solution.py:283
  (606 shorter events, 225.7 us)
Async XLA Ops:
  4.6 9.7 collective-permute-start
  9.5 5.5 collective-permute-start.1
  10.8 769.5 %copy-start.33 = (bf16[68]{0:T(256)(128)(2,1)}, bf16[68]{0:T(256)(128)(2,1)S(1)}, u32[]{:S(2)}) copy-start(bf16[68]{0:T(256)(128)(2,1)S(1)} %and_convert_fusion) | copy-start | bytes 412
  31.6 5.6 collective-permute-start.2
  35.9 5.5 collective-permute-start.3
  42.1 33.5 %collective-permute-start.4 = (bf16[1,64,512]{2,1,0:T(8,128)(2,1)S(1)}, bf16[1,64,512]{2,1,0:T(8,128)(2,1)S(1)}, u32[]{:S(2)}, u32[]{:S(2)}) collective-permute-start(bf16[1,64,512]{2,1,0:T(8,128)(2,1)S(1)} %get-tuple-element.2084), channel_id=1, source_target_pairs={{0,16},{16,0},{1,17},{17,1},{2,18},{18,2},{3,19},{19,3},{4,20},{20... | collective-permute-start | bytes 196616 | tf_op jit(solution)/shard_map/ppermute | solution.py:38
  75.7 5.8 collective-permute-start.5
  80.3 5.5 collective-permute-start.6
  101.6 6.0 collective-permute-start.7
  106.3 5.5 collective-permute-start.8
  120.3 46.4 %copy-start.65 = (f32[4]{0:T(128)}, f32[4]{0:T(128)S(1)}, u32[]{:S(2)}) copy-start(f32[4]{0:T(128)S(1)} %get-tuple-element.994) | copy-start | bytes 52
  120.9 40.6 %collective-permute-start.9 = (bf16[1,64,512]{2,1,0:T(8,128)(2,1)S(1)}, bf16[1,64,512]{2,1,0:T(8,128)(2,1)S(1)}, u32[]{:S(2)}, u32[]{:S(2)}) collective-permute-start(bf16[1,64,512]{2,1,0:T(8,128)(2,1)S(1)} %get-tuple-element.2082), channel_id=1, source_target_pairs={{0,16},{16,0},{1,17},{17,1},{2,18},{18,2},{3,19},{19,3},{4,20},{20... | collective-permute-start | bytes 196616 | tf_op jit(solution)/shard_map/ppermute | solution.py:38
  162.2 5.8 collective-permute-start.10
  166.7 5.5 collective-permute-start.11
  193.4 5.3 collective-permute-start.12
  197.4 5.5 collective-permute-start.13
  211.3 41.2 %copy-start.67 = (f32[4]{0:T(128)}, f32[4]{0:T(128)S(1)}, u32[]{:S(2)}) copy-start(f32[4]{0:T(128)S(1)} %get-tuple-element.995) | copy-start | bytes 52
  212.0 35.9 %collective-permute-start.14 = (bf16[1,64,512]{2,1,0:T(8,128)(2,1)S(1)}, bf16[1,64,512]{2,1,0:T(8,128)(2,1)S(1)}, u32[]{:S(2)}, u32[]{:S(2)}) collective-permute-start(bf16[1,64,512]{2,1,0:T(8,128)(2,1)S(1)} %get-tuple-element.2080), channel_id=1, source_target_pairs={{0,16},{16,0},{1,17},{17,1},{2,18},{18,2},{3,19},{19,3},{4,20},{20... | collective-permute-start | bytes 196616 | tf_op jit(solution)/shard_map/ppermute | solution.py:38
  248.5 5.3 collective-permute-start.15
  252.5 5.5 collective-permute-start.16
  279.4 5.3 collective-permute-start.17
  283.4 5.5 collective-permute-start.18
  297.2 41.2 %copy-start.69 = (f32[4]{0:T(128)}, f32[4]{0:T(128)S(1)}, u32[]{:S(2)}) copy-start(f32[4]{0:T(128)S(1)} %get-tuple-element.996) | copy-start | bytes 52
  297.8 35.6 %collective-permute-start.19 = (bf16[1,64,512]{2,1,0:T(8,128)(2,1)S(1)}, bf16[1,64,512]{2,1,0:T(8,128)(2,1)S(1)}, u32[]{:S(2)}, u32[]{:S(2)}) collective-permute-start(bf16[1,64,512]{2,1,0:T(8,128)(2,1)S(1)} %get-tuple-element.2078), channel_id=1, source_target_pairs={{0,16},{16,0},{1,17},{17,1},{2,18},{18,2},{3,19},{19,3},{4,20},{20... | collective-permute-start | bytes 196616 | tf_op jit(solution)/shard_map/ppermute | solution.py:38
  334.1 5.6 collective-permute-start.20
  338.4 5.5 collective-permute-start.21
  365.2 5.3 collective-permute-start.22
  369.2 5.5 collective-permute-start.23
  383.2 40.8 %copy-start.71 = (f32[4]{0:T(128)}, f32[4]{0:T(128)S(1)}, u32[]{:S(2)}) copy-start(f32[4]{0:T(128)S(1)} %get-tuple-element.997) | copy-start | bytes 52
  383.9 35.5 %collective-permute-start.24 = (bf16[1,64,512]{2,1,0:T(8,128)(2,1)S(1)}, bf16[1,64,512]{2,1,0:T(8,128)(2,1)S(1)}, u32[]{:S(2)}, u32[]{:S(2)}) collective-permute-start(bf16[1,64,512]{2,1,0:T(8,128)(2,1)S(1)} %get-tuple-element.2076), channel_id=1, source_target_pairs={{0,16},{16,0},{1,17},{17,1},{2,18},{18,2},{3,19},{19,3},{4,20},{20... | collective-permute-start | bytes 196616 | tf_op jit(solution)/shard_map/ppermute | solution.py:38
  420.0 5.9 collective-permute-start.25
  424.0 5.5 collective-permute-start.26
  450.7 7.8 collective-permute-start.27
  454.7 5.5 collective-permute-start.28
  460.2 51.9 %copy-start.5 = (f32[1,64,512]{2,1,0:T(8,128)S(1)}, f32[1,64,512]{2,1,0:T(8,128)}, u32[]{:S(2)}) copy-start(f32[1,64,512]{2,1,0:T(8,128)} %copy-done.4) | copy-start | bytes 393220
  468.7 42.0 %copy-start.73 = (f32[4]{0:T(128)}, f32[4]{0:T(128)S(1)}, u32[]{:S(2)}) copy-start(f32[4]{0:T(128)S(1)} %get-tuple-element.998) | copy-start | bytes 52
  469.4 36.4 %collective-permute-start.29 = (bf16[1,64,512]{2,1,0:T(8,128)(2,1)S(1)}, bf16[1,64,512]{2,1,0:T(8,128)(2,1)S(1)}, u32[]{:S(2)}, u32[]{:S(2)}) collective-permute-start(bf16[1,64,512]{2,1,0:T(8,128)(2,1)S(1)} %get-tuple-element.2074), channel_id=1, source_target_pairs={{0,16},{16,0},{1,17},{17,1},{2,18},{18,2},{3,19},{19,3},{4,20},{20... | collective-permute-start | bytes 196616 | tf_op jit(solution)/shard_map/ppermute | solution.py:38
  506.5 8.3 collective-permute-start.30
  510.8 5.5 collective-permute-start.31
  538.3 10.1 collective-permute-start.32
  542.9 5.5 collective-permute-start.33
  548.4 44.4 %copy-start.8 = (f32[1,64,512]{2,1,0:T(8,128)S(1)}, f32[1,64,512]{2,1,0:T(8,128)}, u32[]{:S(2)}) copy-start(f32[1,64,512]{2,1,0:T(8,128)} %copy-done.7) | copy-start | bytes 393220
  548.5 53.4 %copy-start.23 = (f32[1,32,64]{2,1,0:T(8,128)S(1)}, f32[1,32,64]{2,1,0:T(8,128)}, u32[]{:S(2)}) copy-start(f32[1,32,64]{2,1,0:T(8,128)} %get-tuple-element.963) | copy-start | bytes 24580
  556.8 49.0 %copy-start.75 = (f32[4]{0:T(128)}, f32[4]{0:T(128)S(1)}, u32[]{:S(2)}) copy-start(f32[4]{0:T(128)S(1)} %get-tuple-element.999) | copy-start | bytes 52
  557.5 36.3 %collective-permute-start.34 = (bf16[1,64,512]{2,1,0:T(8,128)(2,1)S(1)}, bf16[1,64,512]{2,1,0:T(8,128)(2,1)S(1)}, u32[]{:S(2)}, u32[]{:S(2)}) collective-permute-start(bf16[1,64,512]{2,1,0:T(8,128)(2,1)S(1)} %get-tuple-element.2072), channel_id=1, source_target_pairs={{0,16},{16,0},{1,17},{17,1},{2,18},{18,2},{3,19},{19,3},{4,20},{20... | collective-permute-start | bytes 196616 | tf_op jit(solution)/shard_map/ppermute | solution.py:38
  594.4 8.8 collective-permute-start.35
  598.9 6.1 collective-permute-start.36
  627.0 10.2 collective-permute-start.37
  631.8 5.6 collective-permute-start.38
  637.5 45.3 %copy-start.12 = (f32[1,64,512]{2,1,0:T(8,128)S(1)}, f32[1,64,512]{2,1,0:T(8,128)}, u32[]{:S(2)}) copy-start(f32[1,64,512]{2,1,0:T(8,128)} %copy-done.11) | copy-start | bytes 393220
  645.9 37.8 %collective-permute-start.39 = (bf16[1,64,512]{2,1,0:T(8,128)(2,1)S(1)}, bf16[1,64,512]{2,1,0:T(8,128)(2,1)S(1)}, u32[]{:S(2)}, u32[]{:S(2)}) collective-permute-start(bf16[1,64,512]{2,1,0:T(8,128)(2,1)S(1)} %get-tuple-element.2070), channel_id=1, source_target_pairs={{0,16},{16,0},{1,17},{17,1},{2,18},{18,2},{3,19},{19,3},{4,20},{20... | collective-permute-start | bytes 196616 | tf_op jit(solution)/shard_map/ppermute | solution.py:38
  684.3 9.3 collective-permute-start.40
  689.4 6.9 collective-permute-start.41
  696.6 81.2 %copy-start.90 = (f32[16]{0:T(128)S(1)}, f32[16]{0:T(128)}, u32[]{:S(2)}) copy-start(f32[16]{0:T(128)} %param.56) | copy-start | bytes 196
  696.6 82.4 %copy-start.61 = (f32[16,16]{1,0:T(8,128)S(1)}, f32[16,16]{1,0:T(8,128)}, u32[]{:S(2)}) copy-start(f32[16,16]{1,0:T(8,128)} %param.57) | copy-start | bytes 3076
  724.3 56.0 %collective-permute-start.42 = (bf16[1,2,512]{2,1,0:T(2,128)(2,1)S(1)}, bf16[1,2,512]{2,1,0:T(2,128)(2,1)S(1)}, u32[]{:S(2)}, u32[]{:S(2)}) collective-permute-start(bf16[1,2,512]{2,1,0:T(2,128)(2,1)S(1)} %get-tuple-element.2085), channel_id=1, source_target_pairs={{0,1},{1,2},{2,3},{3,4},{4,5},{5,6},{6,7},{7,8},{8,9},{9,10},{10,1... | collective-permute-start | bytes 6152 | tf_op jit(solution)/shard_map/ppermute | solution.py:31
  730.5 49.8 %collective-permute-start.43 = (bf16[1,2,512]{2,1,0:T(2,128)(2,1)S(1)}, bf16[1,2,512]{2,1,0:T(2,128)(2,1)S(1)}, u32[]{:S(2)}, u32[]{:S(2)}) collective-permute-start(bf16[1,2,512]{2,1,0:T(2,128)(2,1)S(1)} %get-tuple-element.2086), channel_id=1, source_target_pairs={{1,0},{2,1},{3,2},{4,3},{5,4},{6,5},{7,6},{8,7},{9,8},{10,9},{11,1... | collective-permute-start | bytes 6152 | tf_op jit(solution)/shard_map/ppermute | solution.py:32
  780.3 36.9 %copy-start.2 = (bf16[8,64,512]{2,1,0:T(8,128)(2,1)S(1)}, bf16[8,64,512]{2,1,0:T(8,128)(2,1)}, u32[]{:S(2)}) copy-start(bf16[8,64,512]{2,1,0:T(8,128)(2,1)} %get-tuple-element.2069) | copy-start | bytes 1572868
  781.4 35.2 %collective-permute-start.44 = (bf16[1,64,512]{2,1,0:T(8,128)(2,1)S(1)}, bf16[1,64,512]{2,1,0:T(8,128)(2,1)S(1)}, u32[]{:S(2)}, u32[]{:S(2)}) collective-permute-start(bf16[1,64,512]{2,1,0:T(8,128)(2,1)S(1)} %broadcast_select_fusion), channel_id=1, source_target_pairs={{0,16},{16,0},{1,17},{17,1},{2,18},{18,2},{3,19},{19,3},{4,20},{20... | collective-permute-start | bytes 196616 | tf_op jit(solution)/shard_map/ppermute | solution.py:38
  827.8 4.4 collective-permute-start.45
  830.9 5.6 collective-permute-start.46
  836.7 191.2 %copy-start.36 = (f32[16,4,5,5]{0,1,3,2:T(4,128)S(1)}, f32[16,4,5,5]{0,1,3,2:T(4,128)}, u32[]{:S(2)}) copy-start(f32[16,4,5,5]{0,1,3,2:T(4,128)} %copy-done.35) | copy-start | bytes 19204
  836.7 192.9 %copy-start.91 = (pred[2]{0:T(512)(128)(4,1)S(1)}, pred[2]{0:T(512)(128)(4,1)}, u32[]{:S(2)}) copy-start(pred[2]{0:T(512)(128)(4,1)} %iota_compare_fusion.29) | copy-start | bytes 10
  1027.8 44.6 %copy-start.46 = (bf16[8,64,512]{2,1,0:T(8,128)(2,1)}, bf16[8,64,512]{2,1,0:T(8,128)(2,1)S(1)}, u32[]{:S(2)}) copy-start(bf16[8,64,512]{2,1,0:T(8,128)(2,1)S(1)} %get-tuple-element.983) | copy-start | bytes 1572868
  (87 other events, 1104.8 us)
where the time goes:
time: 1080 us; the launch traced here: 1070 us
  starting transfers between devices  425 us (39%)
  matrix products  212 us (20%)
  local copies, waits for them, and re-layouts  125 us (12%)
  loops' own time  117 us (11%)
  blocking collectives  88.2 us (8%)
  waiting for transfers between devices  59.3 us (5%)
  other arithmetic  38.2 us (4%)
    ppermute x9, starting transfers between devices, partner(): lax.ppermute(x, axis, [(i, i ^ 1 << stride) for i in range(lax.axis_size(...  318 us
    conv_general_dilated x1, matrix products, spread_conv(): lax.conv_general_dilated(shaped, kern[:, :, ::-1, ::-1], (1, 1), ((0, 1),...  144 us
    ppermute x19, starting transfers between devices, extended(): before = lax.ppermute(last, axis, up)  82.3 us
    unnamed x9, loops' own time  58.6 us
    conv_general_dilated x45, local copies, waits for them, and re-layouts, strided_conv(): lax.conv_general_dilated(shaped, kern, (2, 2), ((0, 0), (2, 2)), dimensio...  58 us
    another operation x9, loops' own time, shards(): lax.cond(section_index == 0, encode_wait, decode_back)  57.7 us
    ppermute x19, waiting for transfers between devices, extended(): after = lax.ppermute(first, axis, down)  54 us
    psum x1, blocking collectives, shards(): lax.psum((first_sum, second_sum, valid_total), ('section', 'wide'))  46 us
  transfers between devices with their start and end apart: 47, of which 25 were waited for; matrix products, arithmetic and copies ran while one was open for 2% of the time, Pallas kernels for 0%

commit v1 on v0

v1 whole, which is shorter than its diff:
```python
import jax
import jax.numpy as jnp
from jax import lax
from jax.experimental import pallas as pl
from jax.experimental.pallas import tpu as pltpu
from jax.sharding import PartitionSpec as P

CIN = 4
CCODE = 16
KS = 5
HW = 128

UW = 16
NB = 5
HALO = 8
NK = CCODE * CIN * KS * KS

decay_rate = 0.9
whiten_weight = 0.25

F32 = jnp.float32
BF16 = jnp.bfloat16


def iota(shape, dim):
    return lax.broadcasted_iota(jnp.int32, shape, dim)


def hot(mask):
    return jnp.where(mask, 1.0, 0.0).astype(BF16)


def dot(a, b, dims=((1,), (0,))):
    return lax.dot_general(a, b, (dims, ((), ())), preferred_element_type=F32)


def fold(x, steps):
    for step in steps:
        x = x + pltpu.roll(x, step, 1)
    return x


def split(x):
    high = x.astype(BF16)
    rest = x - high.astype(F32)
    mid = rest.astype(BF16)
    return high, mid, (rest - mid.astype(F32)).astype(BF16)


class Sizes:
    def __init__(self, fields, sections):
        self.micro, self.band, self.span = fields
        self.sections = sections
        self.mb = self.micro // sections
        self.jf = self.band // 2 + HALO // 2
        self.rows = self.jf * self.mb
        self.own = self.mb * self.band
        self.halo = self.mb * HALO
        self.shift = self.mb.bit_length() - 1
        self.frame = NB * self.rows


def tap_target(n):
    o = (n * 5243) >> 19
    t = n - 100 * o
    c = (t * 1311) >> 15
    t = t - 25 * c
    k = (t * 205) >> 10
    l = t - 5 * k
    return (3 * k + (l >> 1)) * 8 + 2 * c + (l & 1), o


def tap_onehot():
    target, _ = tap_target(iota((1, NK), 1))
    return hot(iota((128, NK), 0) == target)


def gather_rows(z, odd):
    row = iota((2 * z.rows, 1), 0)
    parity = (row >= z.rows).astype(jnp.int32)
    q = row - parity * z.rows
    j = (q >> z.shift) - odd * (HALO // 2)
    m = q & (z.mb - 1)
    r = 2 * j + parity
    halo = z.own + m * HALO
    target = jnp.where(
        r < 0, halo + r + HALO, jnp.where(r >= z.band, halo + r - z.band, m * z.band + r)
    )
    return hot(iota((2 * z.rows, z.own + z.halo), 1) == target)


def scatter_rows(z, odd):
    row = iota((z.own, 1), 0)
    band_shift = z.band.bit_length() - 1
    m = row >> band_shift
    r = row & (z.band - 1)
    target = (r & 1) * z.rows + ((r >> 1) + odd * (HALO // 2)) * z.mb + m
    return hot(iota((z.own, 2 * z.rows), 1) == target)


def pixel_target(lane, inner):
    u_local = (lane >> 3) & (UW - 1)
    u = (lane >> 7) * (UW - 2) + u_local - 1
    valid = (u >= 0) & (u < HW // 2)
    if inner:
        valid = valid & (u_local >= 1) & (u_local <= UW - 2)
    return 2 * u + (lane & 1), (lane >> 1) & 3, valid


def window_columns():
    col, c, valid = pixel_target(iota((1, NB * 128), 1), False)
    target = jnp.where(valid, c * HW + col, -1)
    return hot(iota((CIN * HW, NB * 128), 0) == target)


def unwindow_columns():
    col, c, valid = pixel_target(iota((NB * 128, 1), 0), True)
    target = jnp.where(valid, c * HW + col, -1)
    return hot(iota((NB * 128, CIN * HW), 1) == target)


def window_mask_columns():
    col, _, valid = pixel_target(iota((1, NB * 128), 1), False)
    return hot(iota((HW, NB * 128), 0) == jnp.where(valid, col, -1))


def code_mask_columns():
    lane = iota((1, NB * 256), 1)
    u_local = (lane >> 4) & (UW - 1)
    u = (lane >> 8) * (UW - 2) + u_local - 1
    valid = (u_local >= 1) & (u_local <= UW - 2) & (u < HW // 2)
    return hot(iota((HW, NB * 256), 0) == jnp.where(valid, 2 * u, -1))


def own_rows(z, odd):
    j = (iota((z.rows, 1), 0) >> z.shift) - odd * (HALO // 2)
    return (j >= 0) & (j < z.band // 2)


def mend_coarse(blocks):
    last = HW // 2 - (NB - 1) * (UW - 2)
    rows = blocks[0].shape[0]
    lane = iota((rows, 128), 1)
    halves = [(x[:, :128], x[:, 128:]) for x in blocks]
    done = []
    for b, (low, high) in enumerate(halves):
        before = pltpu.roll(halves[b - 1][1], 32, 1) if b else 0.0
        new_low = jnp.where(lane < 16, before, low)
        if b + 1 < NB:
            after = pltpu.roll(halves[b + 1][0], 96, 1)
            new_high = jnp.where(lane >= 112, after, high)
        else:
            new_high = jnp.where(lane < (last + 1) * 16 - 128, high, 0.0)
        done.append((new_low, new_high))
    return done


def mend_fine(halves):
    rows = halves[0][0].shape[0]
    lane = iota((rows, 128), 1)
    done = []
    for b in range(NB):
        pair = []
        for h in range(2):
            x = halves[b][h]
            before = pltpu.roll(halves[b - 1][h], 16, 1) if b else 0.0
            after = pltpu.roll(halves[b + 1][h], 112, 1) if b + 1 < NB else 0.0
            x = jnp.where(lane < 8, before, x)
            pair.append(jnp.where(lane >= 120, after, x))
        done.append(tuple(pair))
    return done


def put_frame(z, sh, halves):
    zeros = jnp.zeros((NB, 8, 256), F32)
    sh[:, 0:8, :] = zeros
    sh[:, 8 + z.rows : 16 + z.rows, :] = zeros
    for b, (low, high) in enumerate(halves):
        sh[b, 8 : 8 + z.rows, 0:128] = low
        sh[b, 8 : 8 + z.rows, 128:256] = high


def fine_taps(z, sh, b):
    up = sh[b, 8 - z.mb : 8 - z.mb + z.rows, :]
    here = sh[b, 8 : 8 + z.rows, :]
    down = sh[b, 8 + z.mb : 8 + z.mb + z.rows, 0:128]
    return jnp.concatenate([up, here, down], axis=1).astype(BF16)


def coarse_taps(z, sh, b):
    down = sh[b, 8 + z.mb : 8 + z.mb + z.rows, :]
    here = sh[b, 8 : 8 + z.rows, :]
    up = sh[b, 8 - z.mb : 8 - z.mb + z.rows, :]
    return [x.astype(BF16) for x in (down, here, up)]


def spread(z, sh, weights):
    taps = [coarse_taps(z, sh, b) for b in range(NB)]
    down, here, up = (jnp.concatenate([t[i] for t in taps], axis=0) for i in range(3))
    nt = ((1,), (1,))
    out = dot(down, weights[0:256], nt) + dot(here, weights[256:512], nt)
    extra = dot(up, weights[512:640], nt)
    return out[:, :128] + extra, out[:, 128:]


def pick_taps(grads):
    lane = iota((CCODE, 128), 1)
    place = lane >> 3
    kept = jnp.zeros((CCODE, 128), F32)
    for k in range(KS):
        for shift in (-1, 0, 1):
            total = jnp.zeros((CCODE, 128), F32)
            for u in range(1, UW - 1):
                part = grads[u * 16 : u * 16 + 16, k * 128 : k * 128 + 128]
                total = jnp.where(place == u + shift, part, total)
            total = fold(total, (64, 32, 16, 8))
            kept = jnp.where(place == 3 * k + shift + 1, total, kept)
    return kept


def to_pixels(z, odd, low, high):
    rows = z.rows
    flat = [
        jnp.concatenate([h[b * rows : b * rows + rows].astype(BF16) for b in range(NB)], axis=1)
        for h in (low, high)
    ]
    native = dot(jnp.concatenate(flat, axis=0), unwindow_columns()).astype(BF16)
    return dot(scatter_rows(z, odd), native).astype(BF16)


def build_weights(kernel_pair, out_ref):
    row = iota((2 * CCODE, NK), 0)
    _, o = tap_target(iota((1, NK), 1))
    values = jnp.where(row < CCODE, kernel_pair[0], kernel_pair[1])
    spreaded = jnp.where((row & (CCODE - 1)) == o, values, 0.0).astype(BF16)
    taps = dot(tap_onehot(), spreaded, ((1,), (1,))).astype(BF16)
    lane = iota((2 * CCODE, 512), 1)
    repeat = hot(iota((2 * CCODE, 512), 0) == ((lane >> 8) * CCODE + (lane & 15)))
    wide_taps = dot(taps, repeat)
    row_u = iota((128, 256), 0) >> 3
    lane_u = iota((128, 256), 1) >> 4
    for which in range(2):
        for k in range(KS):
            total = jnp.zeros((128, 256), F32)
            for shift in (-1, 0, 1):
                q = 3 * k + shift + 1
                piece = wide_taps[8 * q : 8 * q + 8, 256 * which : 256 * which + 256]
                piece = jnp.broadcast_to(piece[None], (16, 8, 256)).reshape(128, 256)
                total = jnp.where(row_u == lane_u + shift, piece, total)
            out_ref[which, k * 128 : k * 128 + 128, :] = total.astype(BF16)


def encode_kernel(
    z, fields, mask, halo, kernel_own, kernel_other, enc_bias, counts,
    taps_out, code_out, slope_out, inmask_out, codemask_out, weights_out, pay_out,
    field_buf, mask_buf, sh, sems,
):
    section = lax.axis_index("section")
    wide = lax.axis_index("wide")
    odd = lax.rem(wide, 2)
    first = section * z.mb
    field_copy = pltpu.make_async_copy(fields.at[pl.ds(first, z.mb)], field_buf, sems.at[0])
    mask_copy = pltpu.make_async_copy(mask.at[pl.ds(first, z.mb)], mask_buf, sems.at[1])
    field_copy.start()
    mask_copy.start()
    mine, other = kernel_own[...].astype(F32), kernel_other[...].astype(F32)
    leads = section == 0
    build_weights(
        (jnp.where(leads, mine, other), jnp.where(leads, other, mine)), weights_out
    )
    gather = gather_rows(z, odd)
    rows = z.rows
    mask_copy.wait()
    pixel_mask = jnp.concatenate(
        [
            mask_buf[...].astype(F32).astype(BF16).reshape(z.own, HW),
            halo[:, 2 * z.span : 2 * z.span + HW],
        ],
        axis=0,
    )
    framed_mask = dot(gather, pixel_mask).astype(BF16)
    in_mask = dot(framed_mask, window_mask_columns())
    code_mask = dot(framed_mask[0:rows], code_mask_columns())
    field_now = wide * z.band // HW
    micro = iota((rows, 128), 0) & (z.mb - 1)
    count = jnp.zeros((rows, 128), jnp.int32)
    for m in range(z.mb):
        count = jnp.where(micro == m, counts[first + m, field_now], count)
    channel_ok = ((iota((rows, 128), 1) >> 1) & 3) < count
    field_copy.wait()
    pixels = jnp.concatenate(
        [field_buf[...].reshape(z.own, z.span), halo[:, 0 : z.span]], axis=0
    )
    windowed = dot(dot(gather, pixels).astype(BF16), window_columns())
    halves = []
    for b in range(NB):
        pair = []
        for h in range(2):
            rs, cs = slice(h * rows, h * rows + rows), slice(b * 128, b * 128 + 128)
            allowed = jnp.where(channel_ok, in_mask[rs, cs], 0.0)
            inmask_out[b, :, h * 128 : h * 128 + 128] = allowed.astype(BF16)
            pair.append(windowed[rs, cs] * allowed)
        halves.append(pair)
    put_frame(z, sh, halves)
    for b in range(NB):
        taps_out[b] = fine_taps(z, sh, b)
    lane = iota((1, 256), 1) & 15
    bias = jnp.zeros((1, 256), F32)
    for o in range(CCODE):
        bias = jnp.where(lane == o, enc_bias[o], bias)
    pre = dot(taps_out[...].reshape(z.frame, KS * 128), weights_out[0]) + bias
    slope = jnp.exp(jnp.minimum(pre, 0.0))
    code = jnp.where(pre > 0, pre, slope - 1.0).astype(BF16).astype(F32)
    slope_out[...] = slope.reshape(NB, rows, 256)
    mine_rows = own_rows(z, odd)
    first_sum = jnp.zeros((1, 256), F32)
    count_sum = jnp.zeros((1, 256), F32)
    blocks, weighted = [], []
    for b in range(NB):
        here = code[b * rows : b * rows + rows]
        allowed = code_mask[:, b * 256 : b * 256 + 256]
        codemask_out[b] = allowed.astype(BF16)
        allowed = jnp.where(mine_rows, allowed, 0.0)
        first_sum = first_sum + jnp.sum(here * allowed, axis=0, keepdims=True)
        count_sum = count_sum + jnp.sum(allowed, axis=0, keepdims=True)
        blocks.append(here)
        weighted.append((here * allowed).astype(BF16))
    second = dot(jnp.concatenate(weighted, axis=0), code.astype(BF16), ((0,), (0,)))
    for b, (low, high) in enumerate(mend_coarse(blocks)):
        code_out[b, :, 0:128] = low.astype(BF16)
        code_out[b, :, 128:256] = high.astype(BF16)
    lane_u = iota((16, 256), 1) >> 4
    total = jnp.zeros((16, 256), F32)
    for u in range(1, UW - 1):
        total = jnp.where(lane_u == u, second[u * 16 : u * 16 + 16], total)
    total = fold(total[:, :128] + total[:, 128:], (64, 32, 16))
    diagonal = (iota((8, 128), 1) >> 4) == iota((8, 128), 0)
    pay = [
        jnp.sum(jnp.where(diagonal, total[h * 8 : h * 8 + 8], 0.0), axis=0, keepdims=True)
        for h in range(2)
    ]
    for s in (first_sum, count_sum):
        pay.append(fold(jnp.broadcast_to(s[:, :128] + s[:, 128:], (8, 128)), (64, 32, 16))[0:1])
    pay = jnp.concatenate(pay, axis=0)
    for i in range(pay_out.shape[0]):
        pay_out[i] = pay


def decode_kernel(
    z, cotangent, halo, code, in_mask, weights, dec_bias,
    recon_out, sent_out, pay_out,
    cot_buf, sh, sems,
):
    section = lax.axis_index("section")
    odd = lax.rem(lax.axis_index("wide"), 2)
    rows = z.rows
    copy = pltpu.make_async_copy(
        cotangent.at[pl.ds(section * z.mb, z.mb)], cot_buf, sems.at[0]
    )
    copy.start()
    put_frame(
        z, sh, [(code[b, :, 0:128].astype(F32), code[b, :, 128:256].astype(F32)) for b in range(NB)]
    )
    raws = spread(z, sh, weights[1])
    lane_c = (iota((1, 128), 1) >> 1) & 3
    bias = jnp.zeros((1, 128), F32)
    for c in range(CIN):
        bias = jnp.where(lane_c == c, dec_bias[c], bias)
    copy.wait()
    pixels = jnp.concatenate(
        [cot_buf[...].reshape(z.own, z.span), halo[:, z.span : 2 * z.span]], axis=0
    )
    windowed = dot(dot(gather_rows(z, odd), pixels).astype(BF16), window_columns())
    mine_rows = own_rows(z, odd)
    u_local = (iota((1, 128), 1) >> 3) & (UW - 1)
    inner = mine_rows & (u_local >= 1) & (u_local <= UW - 2)
    recons, grads = [], []
    bias_sum = jnp.zeros((1, 128), F32)
    for h in range(2):
        raw = raws[h] + bias
        slope = jnp.exp(jnp.minimum(raw, 0.0))
        recon = jnp.where(raw > 0, raw, slope - 1.0)
        pieces = []
        for b in range(NB):
            allowed = in_mask[b, :, h * 128 : h * 128 + 128].astype(F32)
            cot = windowed[h * rows : h * rows + rows, b * 128 : b * 128 + 128]
            rs = slice(b * rows, b * rows + rows)
            pieces.append((recon[rs] * allowed).astype(BF16))
            grad = (cot * allowed * slope[rs]).astype(BF16).astype(F32)
            bias_sum = bias_sum + jnp.sum(jnp.where(inner, grad, 0.0), axis=0, keepdims=True)
            grads.append(grad)
        recons.append(jnp.concatenate(pieces, axis=0))
    recon_out[...] = to_pixels(z, odd, *recons).reshape(z.mb, z.band, z.span)
    put_frame(z, sh, mend_fine([(grads[b], grads[NB + b]) for b in range(NB)]))
    taps = jnp.concatenate([fine_taps(z, sh, b) for b in range(NB)], axis=0)
    sent_out[...] = dot(taps, weights[1]).astype(BF16).reshape(NB, rows, 256)
    mine = jnp.concatenate(
        [jnp.where(mine_rows, code[b].astype(F32), 0.0).astype(BF16) for b in range(NB)], axis=0
    )
    pay = pick_taps(dot(mine, taps, ((0,), (0,))))
    bias_sum = fold(jnp.broadcast_to(bias_sum, (16, 128)), (64, 32, 16, 8))
    lane = iota((16, 128), 1)
    keep = (lane < 8) & ((lane >> 1) == iota((16, 128), 0))
    column = jnp.sum(jnp.where(keep, bias_sum, 0.0), axis=1, keepdims=True)
    pay_out[...] = jnp.where(lane == 121, column, pay)


def whiten_kernel(
    z, stats, code, slope, sent, code_mask, taps, decode_pay, run_mean, run_cov,
    grad_out, keep_out, send_out, mean_out, cov_out,
):
    section = lax.axis_index("section")
    odd = lax.rem(lax.axis_index("wide"), 2)
    rows = z.rows
    pay = jnp.sum(stats[...], axis=0)
    count = pay[3:4]
    mean = pay[2:3] / count
    diagonal = (iota((8, 128), 1) >> 4) == iota((8, 128), 0)
    second = jnp.concatenate(
        [
            fold(jnp.where(diagonal, jnp.broadcast_to(pay[h : h + 1], (8, 128)), 0.0), (64, 32, 16))
            for h in range(2)
        ],
        axis=0,
    )
    lane = iota((16, 128), 1)
    row = iota((16, 128), 0)
    wide_mean = jnp.broadcast_to(mean, (16, 128))
    mean_column = jnp.sum(jnp.where(lane == row, wide_mean, 0.0), axis=1, keepdims=True)
    cov = second / jnp.broadcast_to(count, (16, 128)) - mean_column * wide_mean
    mean_out[...] = decay_rate * run_mean[...] + (1.0 - decay_rate) * mean[:, 0:CCODE]
    cov_out[...] = decay_rate * run_cov[...] + (1.0 - decay_rate) * cov[:, 0:CCODE]
    offset = cov - jnp.where((lane & 15) == row, 1.0, 0.0)
    pulled = jnp.sum(offset * mean_column, axis=0, keepdims=True)
    linear = whiten_weight * mean - 2.0 * whiten_weight * pulled
    linear = jnp.concatenate([linear, linear], axis=1)
    offset = 2.0 * whiten_weight * jnp.concatenate([offset, offset], axis=1)
    same = (iota((256, 256), 0) >> 4) == (iota((256, 256), 1) >> 4)
    matrix = jnp.broadcast_to(offset[None], (16, 16, 256)).reshape(256, 256)
    high, mid, _ = split(jnp.where(same, matrix, 0.0))
    flat = code[...].reshape(z.frame, 256)
    turned = dot(flat, high) + dot(flat, mid) + linear
    mine_rows = own_rows(z, odd)
    lane_u = iota((1, 256), 1) >> 4
    inner = mine_rows & (lane_u >= 1) & (lane_u <= UW - 2)
    last = HW // 2 - (NB - 1) * (UW - 2)
    blocks, mine = [], []
    bias_sum = jnp.zeros((1, 256), F32)
    for b in range(NB):
        pull = code_mask[b].astype(F32) * turned[b * rows : b * rows + rows]
        grad = ((sent[b].astype(F32) + pull) * slope[b]).astype(BF16).astype(F32)
        kept = jnp.where(inner & (lane_u <= last) if b == NB - 1 else inner, grad, 0.0)
        bias_sum = bias_sum + jnp.sum(kept, axis=0, keepdims=True)
        blocks.append(grad)
        mine.append(kept.astype(BF16))
    for b, (low, high) in enumerate(mend_coarse(blocks)):
        grad_out[b, :, 0:128] = low.astype(BF16)
        grad_out[b, :, 128:256] = high.astype(BF16)
    products = dot(
        jnp.concatenate(mine, axis=0), taps[...].reshape(z.frame, KS * 128), ((0,), (0,))
    )
    encode_pay = pick_taps(products)
    bias_sum = fold(
        jnp.broadcast_to(bias_sum[:, :128] + bias_sum[:, 128:], (16, 128)), (64, 32, 16)
    )
    column = jnp.sum(jnp.where(lane == row, bias_sum, 0.0), axis=1, keepdims=True)
    encode_pay = jnp.where(lane == 120, column, encode_pay)
    decoded = decode_pay[...]
    encode_pay = jnp.where(lane == 121, decoded, encode_pay)
    decoded = jnp.where(lane == 120, column, decoded)
    leads = section == 0
    keep_out[...] = jnp.where(leads, encode_pay, decoded)
    send_out[...] = jnp.where(leads, decoded, encode_pay)


def spread_kernel(z, grad, in_mask, weights, pixels_out, sh):
    odd = lax.rem(lax.axis_index("wide"), 2)
    rows = z.rows
    put_frame(
        z, sh, [(grad[b, :, 0:128].astype(F32), grad[b, :, 128:256].astype(F32)) for b in range(NB)]
    )
    raws = spread(z, sh, weights[0])
    outs = []
    for h in range(2):
        pieces = [
            raws[h][b * rows : b * rows + rows] * in_mask[b, :, h * 128 : h * 128 + 128].astype(F32)
            for b in range(NB)
        ]
        outs.append(jnp.concatenate(pieces, axis=0).astype(BF16))
    pixels_out[...] = to_pixels(z, odd, *outs).reshape(z.mb, z.band, z.span)


def finish_kernel(z, parts, kernel_out, enc_out, dec_out):
    total = jnp.sum(parts[...], axis=0)
    lane = iota((16, 128), 1)
    row = iota((16, 128), 0)
    for slot, out in ((120, enc_out), (121, dec_out)):
        column = jnp.sum(jnp.where(lane == slot, total, 0.0), axis=1, keepdims=True)
        flat = jnp.sum(jnp.where(lane == row, column, 0.0), axis=0, keepdims=True)
        out[...] = flat[:, 0 : out.shape[1]]
    onehot = tap_onehot()
    chosen = sum(dot(x, onehot) for x in split(total))
    _, o = tap_target(iota((1, NK), 1))
    kernel_out[...] = jnp.sum(
        jnp.where(iota((16, NK), 0) == o, chosen, 0.0), axis=0, keepdims=True
    )


VMEM = pl.BlockSpec(memory_space=pltpu.VMEM)
SMEM = pl.BlockSpec(memory_space=pltpu.SMEM)
ANY = pl.BlockSpec(memory_space=pl.ANY)
PARAMS = pltpu.CompilerParams(vmem_limit_bytes=48 * 1024 * 1024)


def shards(sections, wides):
    def run(
        fields, pixel_mask, channel_counts, kernels, enc_bias, dec_bias, cotangent, run_mean, run_cov
    ):
        z = Sizes(fields.shape, sections)
        assert 2 * z.band == HW and z.span == CIN * HW and z.mb == 4
        section = lax.axis_index("section")
        wide = lax.axis_index("wide")
        odd = lax.rem(wide, 2)
        swap = [(i, i ^ 1) for i in range(sections)]
        pair = [(i, i ^ 1) for i in range(wides)]
        start = jnp.where(odd == 0, z.band - HALO, 0)

        def edge(x):
            piece = lax.dynamic_slice(
                x, (section * z.mb, start, 0), (z.mb, HALO, x.shape[2])
            )
            return piece.reshape(z.halo, x.shape[2]).astype(BF16)

        halo = jnp.concatenate([edge(fields), edge(cotangent), edge(pixel_mask)], axis=1)
        halo = lax.ppermute(halo, "wide", pair)
        kernel_other = lax.ppermute(kernels, "section", swap)

        def shape(*dims, dtype=BF16):
            return jax.ShapeDtypeStruct(dims, dtype)

        frame = (NB, z.rows, 256)
        peers = sections * wides
        taps, code, slope, in_mask, code_mask, weights, pay = pl.pallas_call(
            lambda *refs: encode_kernel(z, *refs),
            out_shape=(
                shape(NB, z.rows, KS * 128), shape(*frame), shape(*frame, dtype=F32),
                shape(*frame), shape(*frame), shape(2, KS * 128, 256),
                shape(peers, 4, 128, dtype=F32),
            ),
            in_specs=[ANY, ANY, VMEM, VMEM, VMEM, SMEM, SMEM],
            out_specs=[VMEM] * 7,
            scratch_shapes=[
                pltpu.VMEM((z.mb, z.band, z.span), BF16),
                pltpu.VMEM((z.mb, z.band, HW), jnp.int32),
                pltpu.VMEM((NB, z.rows + 16, 256), F32),
                pltpu.SemaphoreType.DMA((2,)),
            ],
            compiler_params=PARAMS,
            name="encode",
        )(fields, pixel_mask, halo, kernels, kernel_other, enc_bias, channel_counts)
        stats = lax.all_to_all(pay, ("section", "wide"), 0, 0)
        recon, sent, decode_pay = pl.pallas_call(
            lambda *refs: decode_kernel(z, *refs),
            out_shape=(
                shape(z.mb, z.band, z.span), shape(*frame), shape(CCODE, 128, dtype=F32),
            ),
            in_specs=[ANY, VMEM, VMEM, VMEM, VMEM, SMEM],
            out_specs=[VMEM] * 3,
            scratch_shapes=[
                pltpu.VMEM((z.mb, z.band, z.span), BF16),
                pltpu.VMEM((NB, z.rows + 16, 256), F32),
                pltpu.SemaphoreType.DMA((1,)),
            ],
            compiler_params=PARAMS,
            cost_estimate=pl.CostEstimate(
                flops=4_000_000_000, bytes_accessed=4_000_000, transcendentals=0
            ),
            name="decode",
        )(cotangent, halo, code, in_mask, weights, dec_bias)
        grad, keep, send, new_mean, new_cov = pl.pallas_call(
            lambda *refs: whiten_kernel(z, *refs),
            out_shape=(
                shape(*frame), shape(CCODE, 128, dtype=F32), shape(CCODE, 128, dtype=F32),
                shape(1, CCODE, dtype=F32), shape(CCODE, CCODE, dtype=F32),
            ),
            in_specs=[VMEM] * 9,
            out_specs=[VMEM] * 5,
            compiler_params=PARAMS,
            name="whiten",
        )(stats, code, slope, sent, code_mask, taps, decode_pay, run_mean.reshape(1, CCODE), run_cov)
        total = keep + lax.ppermute(send, "section", swap)
        parts = lax.all_to_all(
            jnp.broadcast_to(total[None], (wides, CCODE, 128)), "wide", 0, 0
        )
        pixels = pl.pallas_call(
            lambda *refs: spread_kernel(z, *refs),
            out_shape=shape(z.mb, z.band, z.span),
            in_specs=[VMEM] * 3,
            out_specs=VMEM,
            scratch_shapes=[pltpu.VMEM((NB, z.rows + 16, 256), F32)],
            compiler_params=PARAMS,
            cost_estimate=pl.CostEstimate(
                flops=4_000_000_000, bytes_accessed=4_000_000, transcendentals=0
            ),
            name="spread",
        )(grad, in_mask, weights)
        arrived = lax.ppermute(jnp.where(section == 0, recon, pixels), "section", swap)
        pixels_out = jnp.where(
            section == 0,
            jnp.concatenate([pixels, arrived], axis=0),
            jnp.concatenate([arrived, recon], axis=0),
        )[None]
        kernel_grads, enc_grad, dec_grad = pl.pallas_call(
            lambda *refs: finish_kernel(z, *refs),
            out_shape=(
                shape(1, NK, dtype=F32), shape(1, CCODE, dtype=F32), shape(1, CIN, dtype=F32),
            ),
            in_specs=[VMEM],
            out_specs=[VMEM] * 3,
            compiler_params=PARAMS,
            name="finish",
        )(parts)
        return (
            pixels_out,
            kernel_grads,
            enc_grad.reshape(CCODE),
            dec_grad.reshape(CIN),
            new_mean.reshape(CCODE),
            new_cov,
        )

    return run


def solution(mesh):
    in_specs = (
        P(None, "wide", None),
        P(None, "wide", None),
        P(),
        P("section", None),
        P(),
        P(),
        P(None, "wide", None),
        P(),
        P(),
    )
    out_specs = (P("section", None, "wide", None), P("section", None), P(), P(), P(), P())
    run = shards(mesh.shape["section"], mesh.shape["wide"])
    return jax.shard_map(run, mesh=mesh, in_specs=in_specs, out_specs=out_specs, check_vma=False)
```

time: 1080 us -> 49.9 us (0.05)
  starting transfers between devices: 425 us -> 9.95 us
  matrix products: 212 us -> 0 us
  local copies, waits for them, and re-layouts: 125 us -> 6.15 us
  loops' own time: 117 us -> 0 us
  blocking collectives: 88.2 us -> 13.8 us
  waiting for transfers between devices: 59.3 us -> 4.04 us
  other arithmetic: 38.2 us -> 1.69 us
  Pallas kernels: 0 us -> 13 us
    ppermute x47 -> x4, starting transfers between devices: 425 us -> 3.57 us  [the longest x1 3 us: run(): halo = lax.ppermute(halo, 'wide', pair)]
    conv_general_dilated x11 -> x0, matrix products: 197 us -> none  [the longest x1 144 us: spread_conv(): lax.conv_general_dilated(shaped, kern[:, :, ::-1, ::-1], (1, 1), ((0, 1),...]
    psum x2 -> x0, blocking collectives: 88.2 us -> none  [the longest x1 46 us: shards(): lax.psum((first_sum, second_sum, valid_total), ('section', 'wide'))]
    conv_general_dilated x46 -> x0, local copies, waits for them, and re-layouts: 70.2 us -> none  [the longest x45 58 us: strided_conv(): lax.conv_general_dilated(shaped, kern, (2, 2), ((0, 0), (2, 2)), dimensio...]
    unnamed x9 -> x0, loops' own time: 58.6 us -> none
    another operation x11 -> x0, loops' own time: 58.3 us -> none  [the longest x9 57.7 us: shards(): lax.cond(section_index == 0, encode_wait, decode_back)]
    ppermute x47 -> x4, waiting for transfers between devices: 59.3 us -> 3.37 us  [the longest x1 1.17 us: run(): kernel_other = lax.ppermute(kernels, 'section', swap)]
    reshape x35 -> x1, local copies, waits for them, and re-layouts: 23.4 us -> 0.78 us  [edge(): return piece.reshape(z.halo, x.shape[2]).astype(BF16)]
  transfers between devices with their start and end apart: 47 -> 5, of which waited for: 25 -> 4; matrix products, arithmetic and copies ran while one was open for 2% -> 0% of each run, Pallas kernels for 0% -> 10%
where the time goes in v1:
time: 49.9 us; the launch traced here: 49.5 us
  blocking collectives  13.8 us (28%)
  Pallas kernels  13 us (26%)
  starting transfers between devices  9.95 us (20%)
  local copies, waits for them, and re-layouts  6.15 us (12%)
  waiting for transfers between devices  4.04 us (8%)
  other arithmetic  1.69 us (3%)
  between operations  0.77 us (2%)
    all_to_all x1, blocking collectives, run(): lax.all_to_all(jnp.broadcast_to(total[None], (wides, CCODE, 128)), 'wide'...  13.8 us
    all_to_all x1, starting transfers between devices, run(): stats = lax.all_to_all(pay, ('section', 'wide'), 0, 0)  6.38 us
    unnamed x24, local copies, waits for them, and re-layouts  5.36 us
    pallas_call x1, Pallas kernels, run(): pl.pallas_call(lambda *refs: encode_kernel(z, *refs), out_shape=(shape(NB...  4.75 us
    pallas_call x1, Pallas kernels, run(): pl.pallas_call(lambda *refs: decode_kernel(z, *refs), out_shape=(shape(z....  3.84 us
    ppermute x1, starting transfers between devices, run(): halo = lax.ppermute(halo, 'wide', pair)  3 us
    pallas_call x1, Pallas kernels, run(): pl.pallas_call(lambda *refs: whiten_kernel(z, *refs), out_shape=(shape(*f...  2.23 us
    pallas_call x1, Pallas kernels, run(): pl.pallas_call(lambda *refs: spread_kernel(z, *refs), out_shape=shape(z.m...  1.25 us
  transfers between devices with their start and end apart: 5, of which 4 were waited for; matrix products, arithmetic and copies ran while one was open for 0% of the time, Pallas kernels for 10%

profile of v1, /device:TPU:0, one launch (start us, length us, event | category | flops | bytes accessed | tf_op | source)
XLA Modules:
  0.0 49.5 jit_solution(5254174581942061281)
XLA Ops:
  0.6 0.0 copy-start.1
  0.7 0.8 %fusion = bf16[32,128]{1,0:T(8,128)(2,1)S(1)} fusion(s32[8,64,128]{2,1,0:T(8,128)} %refs_1_.1, s32[]{:T(128)S(6)} %select_n.36, s32[]{:T(128)S(6)} %select_n.37), kind=kLoop, calls=%fused_computation.6 | loop fusion | flops 4096 | bytes 24584 | tf_op jit(solution)/shard_map/convert_element_type | solution.py:532
  1.4 0.8 %dynamic-slice_bitcast_fusion = (bf16[32,512]{1,0:T(8,128)(2,1)S(1)}, bf16[32,512]{1,0:T(8,128)(2,1)S(1)}) fusion(bf16[8,64,512]{2,1,0:T(8,128)(2,1)} %refs_0_.3, s32[]{:T(128)S(6)} %select_n.36, s32[]{:T(128)S(6)} %select_n.37, bf16[8,64,512]{2,1,0:T(8,128)(2,1)} %refs_0_.2), kind=kLoop, calls=%fused_computation.3 | loop fusion | bytes 131080 | tf_op jit(solution)/shard_map/reshape | solution.py:532
  2.2 0.0 copy-start.3
  2.2 0.0 copy-start.4
  2.2 0.0 copy-start.6
  2.2 3.0 %collective-permute-start = (bf16[32,1152]{1,0:T(8,128)(2,1)S(1)}, bf16[32,1152]{1,0:T(8,128)(2,1)S(1)}, u32[]{:S(2)}, u32[]{:S(2)}) collective-permute-start(bf16[32,1152]{1,0:T(8,128)(2,1)S(1)} %pad_maximum_fusion), channel_id=1, source_target_pairs={{0,1},{1,0},{2,3},{3,2},{4,5},{5,4},{6,7},{7,6},{8,9},{9,8},{10,11... | collective-permute-start | bytes 221192 | tf_op jit(solution)/shard_map/ppermute | solution.py:535
  5.2 0.0 copy-done.3
  5.2 0.0 collective-permute-start.1
  5.3 1.2 %collective-permute-done.1.refs_4_ = bf16[1,1600]{1,0:T(2,128)(2,1)S(1)} collective-permute-done((bf16[1,1600]{1,0:T(2,128)(2,1)S(1)}, bf16[1,1600]{1,0:T(2,128)(2,1)S(1)}, u32[]{:S(2)}, u32[]{:S(2)}) %collective-permute-start.1) | collective-permute-done | bytes 3232 | tf_op jit(solution)/shard_map/ppermute | solution.py:536
  6.4 1.2 %collective-permute-done.refs_2_.refs_1_ = bf16[32,1152]{1,0:T(8,128)(2,1)S(1)} collective-permute-done((bf16[32,1152]{1,0:T(8,128)(2,1)S(1)}, bf16[32,1152]{1,0:T(8,128)(2,1)S(1)}, u32[]{:S(2)}, u32[]{:S(2)}) %collective-permute-start) | collective-permute-done | bytes 73760 | tf_op jit(solution)/shard_map/ppermute | solution.py:535
  7.6 0.0 copy-done.1
  7.6 0.0 copy-done.4
  7.6 0.0 copy-done.6
  7.6 0.0 copy-start
  7.6 1.0 %copy-done = bf16[8,64,512]{2,1,0:T(8,128)(2,1)S(1)} copy-done((bf16[8,64,512]{2,1,0:T(8,128)(2,1)S(1)}, bf16[8,64,512]{2,1,0:T(8,128)(2,1)}, u32[]{:S(2)}) %copy-start) | copy-done | bytes 524312
  8.6 4.7 %encode.1 = (bf16[5,144,640]{2,1,0:T(8,128)(2,1)S(1)}, bf16[5,144,256]{2,1,0:T(8,128)(2,1)S(1)}, f32[5,144,256]{2,1,0:T(8,128)S(1)}, bf16[5,144,256]{2,1,0:T(8,1...) custom-call(bf16[8,64,512]{2,1,0:T(8,128)(2,1)S(1)} %copy-done, ...), custom_call_target="tpu_custom_call" | custom-call | tf_op jit(solution)/shard_map/encode/pallas_call | solution.py:543
  13.4 0.0 copy-start.8
  13.4 0.9 %copy-done.8 = bf16[2,640,256]{2,1,0:T(8,128)(2,1)} copy-done((bf16[2,640,256]{2,1,0:T(8,128)(2,1)}, bf16[2,640,256]{2,1,0:T(8,128)(2,1)S(1)}, u32[]{:S(2)}) %copy-start.8) | copy-done | bytes 655384
  14.3 6.4 %all-to-all-start = ((f32[32,4,128]{2,1,0:T(4,128)}), f32[32,4,128]{2,1,0:T(4,128)S(1)}, u32[]{:S(2)}, u32[]{:S(2)}) async-start(f32[32,4,128]{2,1,0:T(4,128)} %get-tuple-element.24), calls=%async_computation | async-start | bytes 131072 | tf_op jit(solution)/shard_map/all_to_all | solution.py:561
  20.7 0.0 copy-start.11
  20.7 0.6 %copy-done.11 = f32[4]{0:T(128)S(1)} copy-done((f32[4]{0:T(128)S(1)}, f32[4]{0:T(128)}, u32[]{:S(2)}) %copy-start.11) | copy-done | bytes 40
  21.3 0.0 copy-start.5
  21.3 1.0 %copy-done.5 = bf16[8,64,512]{2,1,0:T(8,128)(2,1)S(1)} copy-done((bf16[8,64,512]{2,1,0:T(8,128)(2,1)S(1)}, bf16[8,64,512]{2,1,0:T(8,128)(2,1)}, u32[]{:S(2)}) %copy-start.5) | copy-done | bytes 524312
  22.4 0.0 copy-start.9
  22.4 1.1 %copy-done.9 = bf16[2,640,256]{2,1,0:T(8,128)(2,1)S(1)} copy-done((bf16[2,640,256]{2,1,0:T(8,128)(2,1)S(1)}, bf16[2,640,256]{2,1,0:T(8,128)(2,1)}, u32[]{:S(2)}) %copy-start.9) | copy-done | bytes 655384
  23.4 3.8 %decode.1 = (bf16[4,64,512]{2,1,0:T(8,128)(2,1)S(1)}, bf16[5,144,256]{2,1,0:T(8,128)(2,1)S(1)}, f32[16,128]{1,0:T(8,128)S(1)}) custom-call(bf16[8,64,512]{2,1,0:T(8,128)(2,1)S(1)} %copy-done.5, bf16[32,1152]{1,0:T(8,128)(2,1)S(1)} %collective-permute-done.refs_2_.refs_1_, bf16[5,144,256]{2,1,0:T(8,128)(2,1)S(1)} %get-tuple-element.25.refs_2_.refs_1_, ...), custom_call_target="tpu_custom_call" | custom-call | flops 4000000000 | bytes 4000000 | tf_op jit(solution)/shard_map/decode/pallas_call | solution.py:562
  27.3 0.0 copy-start.2
  27.3 0.7 %all-to-all-done.refs_0_ = f32[32,4,128]{2,1,0:T(4,128)S(1)} async-done(((f32[32,4,128]{2,1,0:T(4,128)}), f32[32,4,128]{2,1,0:T(4,128)S(1)}, u32[]{:S(2)}, u32[]{:S(2)}) %all-to-all-start) | async-done | bytes 65568 | tf_op jit(solution)/shard_map/all_to_all | solution.py:561
  28.0 0.0 copy-start.7
  28.0 0.0 copy-done.2
  28.0 0.6 %copy-done.7 = f32[16]{0:T(128)S(1)} copy-done((f32[16]{0:T(128)S(1)}, f32[16]{0:T(128)}, u32[]{:S(2)}) %copy-start.7) | copy-done | bytes 88
  28.6 0.0 copy-start.10
  28.6 2.2 %whiten.1 = (bf16[5,144,256]{2,1,0:T(8,128)(2,1)S(1)}, f32[16,128]{1,0:T(8,128)S(1)}, f32[16,128]{1,0:T(8,128)S(1)}, f32[1,16]{1,0:T(1,128)}, f32[16,16]{1,0:T(8,128)}) custom-call(f32[32,4,128]{2,1,0:T(4,128)S(1)} %all-to-all-done.refs_0_, bf16[5,144,256]{2,1,0:T(8,128)(2,1)S(1)} %get-tuple-element.25.refs_2_.refs_1_, ...), custom_call_target="tpu_custom_call" | custom-call | tf_op jit(solution)/shard_map/whiten/pallas_call | solution.py:580
  30.9 0.0 copy-done.10
  30.9 1.2 %spread.1 = bf16[4,64,512]{2,1,0:T(8,128)(2,1)S(1)} custom-call(bf16[5,144,256]{2,1,0:T(8,128)(2,1)S(1)} %get-tuple-element.33.refs_0_, bf16[5,144,256]{2,1,0:T(8,128)(2,1)S(1)} %get-tuple-element.27.refs_3_.refs_1_, bf16[2,640,256]{2,1,0:T(8,128)(2,1)S(1)} %copy-done.10), custom_call_target="tpu_custom_call" | custom-call | flops 4000000000 | bytes 4000000 | tf_op jit(solution)/shard_map/spread/pallas_call | solution.py:595
  32.2 0.1 collective-permute-start.2
  32.2 0.5 %collective-permute-start.3 = (f32[16,128]{1,0:T(8,128)S(1)}, f32[16,128]{1,0:T(8,128)S(1)}, u32[]{:S(2)}, u32[]{:S(2)}) collective-permute-start(f32[16,128]{1,0:T(8,128)S(1)} %get-tuple-element.36), channel_id=1, source_target_pairs={{0,16},{16,0},{1,17},{17,1},{2,18},{18,2},{3,19},{19,3},{4,20},{20... | collective-permute-start | bytes 24584 | tf_op jit(solution)/shard_map/ppermute | solution.py:591
  32.7 1.0 %collective-permute-done.3 = f32[16,128]{1,0:T(8,128)S(1)} collective-permute-done((f32[16,128]{1,0:T(8,128)S(1)}, f32[16,128]{1,0:T(8,128)S(1)}, u32[]{:S(2)}, u32[]{:S(2)}) %collective-permute-start.3) | collective-permute-done | bytes 8224 | tf_op jit(solution)/shard_map/ppermute | solution.py:591
  33.8 13.8 %all_to_all.10.refs_0_ = f32[16,16,128]{2,1,0:T(8,128)S(1)} all-to-all(f32[16,16,128]{2,1,0:T(8,128)S(1)} %broadcast_in_dim.2), channel_id=1, replica_groups=mesh['section'=2,'wide'=16] {'wide'}, dimensions={0} | all-to-all | bytes 262144 | tf_op jit(solution)/shard_map/all_to_all | solution.py:592
  47.6 1.0 %finish.1 = (f32[1,1600]{1,0:T(1,128)}, f32[1,16]{1,0:T(1,128)}, f32[1,4]{1,0:T(1,128)}) custom-call(f32[16,16,128]{2,1,0:T(8,128)S(1)} %all_to_all.10.refs_0_), custom_call_target="tpu_custom_call" | custom-call | tf_op jit(solution)/shard_map/finish/pallas_call | solution.py:613
  48.6 0.0 collective-permute-done.2
  48.6 0.9 %maximum_select_fusion = bf16[1,8,64,512]{3,2,1,0:T(8,128)(2,1)} fusion(bf16[1,4,64,512]{3,2,1,0:T(8,128)(2,1)S(1)} %bitcast.16, bf16[1,4,64,512]{3,2,1,0:T(8,128)(2,1)S(1)} %bitcast.14, bf16[1,4,64,512]{3,2,1,0:T(8,128)(2,1)S(1)} %bitcast.13, pred[]{:T(512)S(6)} %eq.7), kind=kLoop, calls=%fused_computation | loop fusion | flops 786432 | bytes 1310721 | tf_op jit(solution)/shard_map/jit(_where)/select_n | solution.py:608
  (4 shorter events, 0.1 us)
Async XLA Ops:
  0.6 7.0 %copy-start.1 = (s32[8,64,128]{2,1,0:T(8,128)S(1)}, s32[8,64,128]{2,1,0:T(8,128)}, u32[]{:S(2)}) copy-start(s32[8,64,128]{2,1,0:T(8,128)} %refs_1_.1) | copy-start | bytes 786436
  2.2 3.0 %copy-start.3 = (bf16[1,1600]{1,0:T(2,128)(2,1)S(1)}, bf16[1,1600]{1,0:T(2,128)(2,1)}, u32[]{:S(2)}) copy-start(bf16[1,1600]{1,0:T(2,128)(2,1)} %refs_3_.1) | copy-start | bytes 9604
  2.2 5.4 %copy-start.4 = (s32[8,8]{1,0:T(8,128)S(1)}, s32[8,8]{1,0:T(8,128)}, u32[]{:S(2)}) copy-start(s32[8,8]{1,0:T(8,128)} %refs_6_.1) | copy-start | bytes 772
  2.2 5.4 %copy-start.6 = (f32[16]{0:T(128)S(1)}, f32[16]{0:T(128)}, u32[]{:S(2)}) copy-start(f32[16]{0:T(128)} %refs_5_.2) | copy-start | bytes 196
  2.2 5.3 %collective-permute-start = (bf16[32,1152]{1,0:T(8,128)(2,1)S(1)}, bf16[32,1152]{1,0:T(8,128)(2,1)S(1)}, u32[]{:S(2)}, u32[]{:S(2)}) collective-permute-start(bf16[32,1152]{1,0:T(8,128)(2,1)S(1)} %pad_maximum_fusion), channel_id=1, source_target_pairs={{0,1},{1,0},{2,3},{3,2},{4,5},{5,4},{6,7},{7,6},{8,9},{9,8},{10,11... | collective-permute-start | bytes 221192 | tf_op jit(solution)/shard_map/ppermute | solution.py:535
  5.2 1.2 %collective-permute-start.1 = (bf16[1,1600]{1,0:T(2,128)(2,1)S(1)}, bf16[1,1600]{1,0:T(2,128)(2,1)S(1)}, u32[]{:S(2)}, u32[]{:S(2)}) collective-permute-start(bf16[1,1600]{1,0:T(2,128)(2,1)S(1)} %copy-done.3), channel_id=1, source_target_pairs={{0,16},{16,0},{1,17},{17,1},{2,18},{18,2},{3,19},{19,3},{4,20},{20... | collective-permute-start | bytes 9608 | tf_op jit(solution)/shard_map/ppermute | solution.py:536
  7.6 1.0 %copy-start = (bf16[8,64,512]{2,1,0:T(8,128)(2,1)S(1)}, bf16[8,64,512]{2,1,0:T(8,128)(2,1)}, u32[]{:S(2)}) copy-start(bf16[8,64,512]{2,1,0:T(8,128)(2,1)} %refs_0_.2) | copy-start | bytes 1572868
  13.4 0.9 %copy-start.8 = (bf16[2,640,256]{2,1,0:T(8,128)(2,1)}, bf16[2,640,256]{2,1,0:T(8,128)(2,1)S(1)}, u32[]{:S(2)}) copy-start(bf16[2,640,256]{2,1,0:T(8,128)(2,1)S(1)} %get-tuple-element.28.refs_4_.refs_2_) | copy-start | bytes 1966084
  14.3 13.7 %all-to-all-start = ((f32[32,4,128]{2,1,0:T(4,128)}), f32[32,4,128]{2,1,0:T(4,128)S(1)}, u32[]{:S(2)}, u32[]{:S(2)}) async-start(f32[32,4,128]{2,1,0:T(4,128)} %get-tuple-element.24), calls=%async_computation | async-start | bytes 131072 | tf_op jit(solution)/shard_map/all_to_all | solution.py:561
  20.7 0.7 %copy-start.11 = (f32[4]{0:T(128)S(1)}, f32[4]{0:T(128)}, u32[]{:S(2)}) copy-start(f32[4]{0:T(128)} %refs_5_.3) | copy-start | bytes 52
  21.3 1.0 %copy-start.5 = (bf16[8,64,512]{2,1,0:T(8,128)(2,1)S(1)}, bf16[8,64,512]{2,1,0:T(8,128)(2,1)}, u32[]{:S(2)}) copy-start(bf16[8,64,512]{2,1,0:T(8,128)(2,1)} %refs_0_.3) | copy-start | bytes 1572868
  22.4 1.1 %copy-start.9 = (bf16[2,640,256]{2,1,0:T(8,128)(2,1)S(1)}, bf16[2,640,256]{2,1,0:T(8,128)(2,1)}, u32[]{:S(2)}) copy-start(bf16[2,640,256]{2,1,0:T(8,128)(2,1)} %copy-done.8) | copy-start | bytes 1966084
  27.3 0.7 %copy-start.2 = (f32[16,16]{1,0:T(8,128)S(1)}, f32[16,16]{1,0:T(8,128)}, u32[]{:S(2)}) copy-start(f32[16,16]{1,0:T(8,128)} %refs_8_.1) | copy-start | bytes 3076
  28.0 0.7 %copy-start.7 = (f32[16]{0:T(128)S(1)}, f32[16]{0:T(128)}, u32[]{:S(2)}) copy-start(f32[16]{0:T(128)} %param.16) | copy-start | bytes 196
  28.6 2.2 %copy-start.10 = (bf16[2,640,256]{2,1,0:T(8,128)(2,1)S(1)}, bf16[2,640,256]{2,1,0:T(8,128)(2,1)}, u32[]{:S(2)}) copy-start(bf16[2,640,256]{2,1,0:T(8,128)(2,1)} %copy-done.8) | copy-start | bytes 1966084
  32.2 16.4 %collective-permute-start.2 = (bf16[4,64,512]{2,1,0:T(8,128)(2,1)S(1)}, bf16[4,64,512]{2,1,0:T(8,128)(2,1)S(1)}, u32[]{:S(2)}, u32[]{:S(2)}) collective-permute-start(bf16[4,64,512]{2,1,0:T(8,128)(2,1)S(1)} %broadcast_select_fusion), channel_id=1, source_target_pairs={{0,16},{16,0},{1,17},{17,1},{2,18},{18,2},{3,19},{19,3},{4,20},{20... | collective-permute-start | bytes 786440 | tf_op jit(solution)/shard_map/ppermute | solution.py:607
  32.2 1.5 %collective-permute-start.3 = (f32[16,128]{1,0:T(8,128)S(1)}, f32[16,128]{1,0:T(8,128)S(1)}, u32[]{:S(2)}, u32[]{:S(2)}) collective-permute-start(f32[16,128]{1,0:T(8,128)S(1)} %get-tuple-element.36), channel_id=1, source_target_pairs={{0,16},{16,0},{1,17},{17,1},{2,18},{18,2},{3,19},{19,3},{4,20},{20... | collective-permute-start | bytes 24584 | tf_op jit(solution)/shard_map/ppermute | solution.py:591

commit v2 on v1

v2 whole, which is shorter than its diff:
```python
import jax
import jax.numpy as jnp
from jax import lax
from jax.experimental import pallas as pl
from jax.experimental.pallas import tpu as pltpu
from jax.sharding import PartitionSpec as P

CIN = 4
CCODE = 16
KS = 5
HW = 128

UW = 16
NB = 5
HALO = 8
NK = CCODE * CIN * KS * KS

decay_rate = 0.9
whiten_weight = 0.25

F32 = jnp.float32
BF16 = jnp.bfloat16


def iota(shape, dim):
    return lax.broadcasted_iota(jnp.int32, shape, dim)


def hot(mask):
    return jnp.where(mask, 1.0, 0.0).astype(BF16)


def dot(a, b, dims=((1,), (0,))):
    return lax.dot_general(a, b, (dims, ((), ())), preferred_element_type=F32)


def fold(x, steps):
    for step in steps:
        x = x + pltpu.roll(x, step, 1)
    return x


def split(x):
    high = x.astype(BF16)
    rest = x - high.astype(F32)
    mid = rest.astype(BF16)
    return high, mid, (rest - mid.astype(F32)).astype(BF16)


class Sizes:
    def __init__(self, fields, sections):
        self.micro, self.band, self.span = fields
        self.sections = sections
        self.mb = self.micro // sections
        self.jf = self.band // 2 + HALO // 2
        self.rows = self.jf * self.mb
        self.own = self.mb * self.band
        self.halo = self.mb * HALO
        self.shift = self.mb.bit_length() - 1
        self.frame = NB * self.rows


def tap_target(n):
    o = (n * 5243) >> 19
    t = n - 100 * o
    c = (t * 1311) >> 15
    t = t - 25 * c
    k = (t * 205) >> 10
    l = t - 5 * k
    return (3 * k + (l >> 1)) * 8 + 2 * c + (l & 1), o


def tap_onehot():
    target, _ = tap_target(iota((1, NK), 1))
    return hot(iota((128, NK), 0) == target)


def row_target(z, row):
    half = z.own // 2
    parity = (row >= half).astype(jnp.int32)
    q = row - parity * half
    return (q & (z.mb - 1)) * z.band + 2 * (q >> z.shift) + parity


def gather_rows(z):
    return hot(iota((z.own, z.own), 1) == row_target(z, iota((z.own, 1), 0)))


def scatter_rows(z):
    return hot(iota((z.own, z.own), 0) == row_target(z, iota((1, z.own), 1)))


def gather_halo(z):
    row = iota((z.halo, 1), 0)
    half = z.halo // 2
    parity = (row >= half).astype(jnp.int32)
    q = row - parity * half
    target = (q & (z.mb - 1)) * HALO + 2 * (q >> z.shift) + parity
    return hot(iota((z.halo, z.halo), 1) == target)


def pixel_target(lane, inner):
    u_local = (lane >> 3) & (UW - 1)
    u = (lane >> 7) * (UW - 2) + u_local - 1
    valid = (u >= 0) & (u < HW // 2)
    if inner:
        valid = valid & (u_local >= 1) & (u_local <= UW - 2)
    return 2 * u + (lane & 1), (lane >> 1) & 3, valid


def window_columns():
    col, c, valid = pixel_target(iota((1, NB * 128), 1), False)
    target = jnp.where(valid, c * HW + col, -1)
    return hot(iota((CIN * HW, NB * 128), 0) == target)


def unwindow_columns():
    col, c, valid = pixel_target(iota((NB * 128, 1), 0), True)
    target = jnp.where(valid, c * HW + col, -1)
    return hot(iota((NB * 128, CIN * HW), 1) == target)


def window_mask_columns():
    col, _, valid = pixel_target(iota((1, NB * 128), 1), False)
    return hot(iota((HW, NB * 128), 0) == jnp.where(valid, col, -1))


def code_mask_lanes():
    lane = iota((1, 256), 1)
    u_local = lane >> 4
    inner = (u_local >= 1) & (u_local <= UW - 2)
    return hot(iota((128, 256), 0) == jnp.where(inner, u_local * 8, -1))


def own_rows(z, odd):
    j = (iota((z.rows, 1), 0) >> z.shift) - odd * (HALO // 2)
    return (j >= 0) & (j < z.band // 2)


def places(z, odd):
    own = pl.multiple_of(odd * (z.halo // 2), 16)
    halo = pl.multiple_of((1 - odd) * (z.own // 2), 16)
    return own, halo


def mend_coarse(blocks):
    last = HW // 2 - (NB - 1) * (UW - 2)
    rows = blocks[0].shape[0]
    lane = iota((rows, 128), 1)
    halves = [(x[:, :128], x[:, 128:]) for x in blocks]
    done = []
    for b, (low, high) in enumerate(halves):
        before = pltpu.roll(halves[b - 1][1], 32, 1) if b else 0.0
        new_low = jnp.where(lane < 16, before, low)
        if b + 1 < NB:
            after = pltpu.roll(halves[b + 1][0], 96, 1)
            new_high = jnp.where(lane >= 112, after, high)
        else:
            new_high = jnp.where(lane < (last + 1) * 16 - 128, high, 0.0)
        done.append((new_low, new_high))
    return done


def mend_fine(halves):
    rows = halves[0][0].shape[0]
    lane = iota((rows, 128), 1)
    done = []
    for b in range(NB):
        pair = []
        for h in range(2):
            x = halves[b][h]
            before = pltpu.roll(halves[b - 1][h], 16, 1) if b else 0.0
            after = pltpu.roll(halves[b + 1][h], 112, 1) if b + 1 < NB else 0.0
            x = jnp.where(lane < 8, before, x)
            pair.append(jnp.where(lane >= 120, after, x))
        done.append(tuple(pair))
    return done


def pad_frame(z, sh):
    zeros = jnp.zeros((NB, 8, 256), F32)
    sh[:, 0:8, :] = zeros
    sh[:, 8 + z.rows : 16 + z.rows, :] = zeros


def put_frame(z, sh, halves):
    pad_frame(z, sh)
    for b, (low, high) in enumerate(halves):
        sh[b, 8 : 8 + z.rows, 0:128] = low
        sh[b, 8 : 8 + z.rows, 128:256] = high


def put_pixels(z, sh, odd, own, halo):
    pad_frame(z, sh)
    for start, part in zip(places(z, odd), (own, halo)):
        half = part.shape[0] // 2
        rows = pl.ds(pl.multiple_of(8 + start, 8), half)
        for b in range(NB):
            for h in range(2):
                sh[b, rows, h * 128 : h * 128 + 128] = part[
                    h * half : h * half + half, b * 128 : b * 128 + 128
                ]


def fine_taps(z, sh, b):
    up = sh[b, 8 - z.mb : 8 - z.mb + z.rows, :]
    here = sh[b, 8 : 8 + z.rows, :]
    down = sh[b, 8 + z.mb : 8 + z.mb + z.rows, 0:128]
    return jnp.concatenate([up, here, down], axis=1).astype(BF16)


def coarse_taps(z, sh, b):
    down = sh[b, 8 + z.mb : 8 + z.mb + z.rows, :]
    here = sh[b, 8 : 8 + z.rows, :]
    up = sh[b, 8 - z.mb : 8 - z.mb + z.rows, :]
    return [x.astype(BF16) for x in (down, here, up)]


def spread(z, sh, weights):
    taps = [coarse_taps(z, sh, b) for b in range(NB)]
    down, here, up = (jnp.concatenate([t[i] for t in taps], axis=0) for i in range(3))
    nt = ((1,), (1,))
    out = dot(down, weights[0:256], nt) + dot(here, weights[256:512], nt)
    extra = dot(up, weights[512:640], nt)
    return out[:, :128] + extra, out[:, 128:]


def pick_taps(grads):
    lane = iota((CCODE, 128), 1)
    place = lane >> 3
    pieces = []
    for k in range(KS):
        for shift in (-1, 0, 1):
            total = jnp.zeros((CCODE, 128), F32)
            for u in range(1, UW - 1):
                part = grads[u * 16 : u * 16 + 16, k * 128 : k * 128 + 128]
                total = jnp.where(place == u + shift, part, total)
            pieces.append(total)
    pieces.append(jnp.zeros((CCODE, 128), F32))
    step = 64
    while step >= 8:
        half = len(pieces) // 2
        low = (lane & step) == 0
        merged = []
        for x, y in zip(pieces[:half], pieces[half:]):
            other = jnp.where(low, y, x)
            moved = pltpu.roll(other, step, 1)
            if step < 64:
                moved = jnp.where(low, pltpu.roll(other, 128 - step, 1), moved)
            merged.append(jnp.where(low, x, y) + moved)
        pieces = merged
        step //= 2
    return pieces[0]


def to_pixels(z, odd, sh, in_mask):
    start, _ = places(z, odd)
    half = z.own // 2
    rows = pl.ds(pl.multiple_of(8 + start, 8), half)
    flat = jnp.concatenate(
        [
            jnp.concatenate(
                [sh[b, rows, h * 128 : h * 128 + 128] for b in range(NB)], axis=1
            )
            for h in range(2)
        ],
        axis=0,
    )
    flat = flat.astype(BF16) * in_mask
    native = dot(flat, unwindow_columns()).astype(BF16)
    return dot(scatter_rows(z), native).astype(BF16).reshape(z.mb, z.band, z.span)


def build_weights(kernel_pair, outs):
    row = iota((2 * CCODE, NK), 0)
    _, o = tap_target(iota((1, NK), 1))
    values = jnp.where(row < CCODE, kernel_pair[0], kernel_pair[1])
    spreaded = jnp.where((row & (CCODE - 1)) == o, values, 0.0).astype(BF16)
    taps = dot(tap_onehot(), spreaded, ((1,), (1,))).astype(BF16)
    lane = iota((2 * CCODE, 512), 1)
    repeat = hot(iota((2 * CCODE, 512), 0) == ((lane >> 8) * CCODE + (lane & 15)))
    wide_taps = dot(taps, repeat)
    row_u = iota((128, 256), 0) >> 3
    lane_u = iota((128, 256), 1) >> 4
    for which in range(2):
        for k in range(KS):
            total = jnp.zeros((128, 256), F32)
            for shift in (-1, 0, 1):
                q = 3 * k + shift + 1
                piece = wide_taps[8 * q : 8 * q + 8, 256 * which : 256 * which + 256]
                piece = jnp.broadcast_to(piece[None], (16, 8, 256)).reshape(128, 256)
                total = jnp.where(row_u == lane_u + shift, piece, total)
            outs[which][k * 128 : k * 128 + 128, :] = total.astype(BF16)


def edge_kernel(
    z, fields, cotangent, mask, kernel, out, kernel_out, field_buf, cot_buf, mask_buf, sems
):
    odd = lax.rem(lax.axis_index("wide"), 2)
    first = lax.axis_index("section") * z.mb
    start = pl.multiple_of((1 - odd) * (z.band - 16), 16)
    copies = [
        pltpu.make_async_copy(
            source.at[pl.ds(first, z.mb), pl.ds(start, 16), :], buf, sems.at[i]
        )
        for i, (source, buf) in enumerate(
            ((fields, field_buf), (cotangent, cot_buf), (mask, mask_buf))
        )
    ]
    copies.append(pltpu.make_async_copy(kernel, kernel_out, sems.at[3]))
    for copy in copies:
        copy.start()
    lane = 0
    copies[3].wait()
    for copy, buf in zip(copies[:3], (field_buf, cot_buf, mask_buf)):
        copy.wait()
        rows = buf[...].astype(F32)
        rows = jnp.where(odd == 1, rows[:, :HALO], rows[:, HALO:])
        width = rows.shape[2]
        out[:, lane : lane + width] = rows.reshape(z.halo, width).astype(BF16)
        lane += width


def prepare_kernel(
    z, fields, mask, enc_bias, dec_bias, counts, run_mean, run_cov, kernel_own, kernel_other,
    pixels_out, inmask_out, w0_out, w1_out, aux_out,
    field_buf, mask_buf, enc_buf, dec_buf, count_buf, mean_buf, cov_buf, sems,
):
    section = lax.axis_index("section")
    wide = lax.axis_index("wide")
    first = section * z.mb
    copies = [
        pltpu.make_async_copy(source, buf, sems.at[i])
        for i, (source, buf) in enumerate(
            (
                (mask.at[pl.ds(first, z.mb)], mask_buf),
                (fields.at[pl.ds(first, z.mb)], field_buf),
                (counts, count_buf),
                (enc_bias, enc_buf),
                (dec_bias, dec_buf),
                (run_mean, mean_buf),
                (run_cov, cov_buf),
            )
        )
    ]
    for copy in copies:
        copy.start()
    mine, other = kernel_own[...].astype(F32), kernel_other[...].astype(F32)
    leads = section == 0
    build_weights(
        (jnp.where(leads, mine, other), jnp.where(leads, other, mine)), (w0_out, w1_out)
    )
    gather = gather_rows(z)
    for copy in copies[2:]:
        copy.wait()
    lane = iota((8, 128), 1)
    dec_row = jnp.zeros((8, 128), F32)
    for c in range(CIN):
        dec_row = jnp.where(((lane >> 1) & 3) == c, dec_buf[c], dec_row)
    enc_row = jnp.zeros((8, 128), F32)
    mean_row = jnp.zeros((8, 128), F32)
    for o in range(CCODE):
        enc_row = jnp.where((lane & 15) == o, enc_buf[o], enc_row)
        mean_row = jnp.where((lane & 15) == o, mean_buf[o], mean_row)
    aux_out[0:8] = dec_row
    aux_out[8:16] = enc_row
    aux_out[16:24] = mean_row
    aux_out[24:40] = jnp.zeros((16, 128), F32)
    aux_out[24:40, 0:CCODE] = cov_buf[...]
    field_now = wide * z.band // HW
    micro = iota((16, 128), 0) & (z.mb - 1)
    count = jnp.zeros((16, 128), jnp.int32)
    for m in range(z.mb):
        count = jnp.where(micro == m, count_buf[first + m, field_now], count)
    channel_ok = jnp.where(((iota((16, 128), 1) >> 1) & 3) < count, 1.0, 0.0)
    aux_out[40:56] = channel_ok
    copies[0].wait()
    pixel_mask = mask_buf[...].astype(F32).astype(BF16).reshape(z.own, HW)
    framed_mask = dot(gather, pixel_mask).astype(BF16)
    in_mask = dot(framed_mask, window_mask_columns())
    repeats = (z.own // 16, NB)
    in_mask = in_mask * jnp.tile(channel_ok, repeats)
    inmask_out[...] = in_mask.astype(BF16)
    copies[1].wait()
    pixels = field_buf[...].reshape(z.own, z.span)
    windowed = dot(dot(gather, pixels).astype(BF16), window_columns())
    pixels_out[...] = (windowed * in_mask).astype(BF16)


def encode_kernel(
    z, pixels, own_mask, halo, weights, aux,
    taps_out, code_out, slope_out, halomask_out, pay_out,
    sh, masks,
):
    odd = lax.rem(lax.axis_index("wide"), 2)
    rows = z.rows
    gather = gather_halo(z)
    framed_mask = dot(gather, halo[:, 2 * z.span : 2 * z.span + HW]).astype(BF16)
    channel_ok = jnp.tile(aux[40:56], (z.halo // 16, NB))
    halo_mask = dot(framed_mask, window_mask_columns()) * channel_ok
    halomask_out[...] = halo_mask.astype(BF16)
    halo_pixels = dot(dot(gather, halo[:, 0 : z.span]).astype(BF16), window_columns())
    put_pixels(z, sh, odd, pixels[...].astype(F32), halo_pixels * halo_mask)
    for b in range(NB):
        taps_out[b] = fine_taps(z, sh, b)
    own_start, halo_start = places(z, odd)
    for start, part in ((own_start, own_mask), (halo_start, halomask_out)):
        half = part.shape[0] // 2
        for b in range(NB):
            masks[b, pl.ds(start, half), :] = part[0:half, b * 128 : b * 128 + 128]
    code_mask = dot(masks[...].reshape(z.frame, 128), code_mask_lanes())
    bias = jnp.concatenate([aux[8:9], aux[8:9]], axis=1)
    pre = dot(taps_out[...].reshape(z.frame, KS * 128), weights[...]) + bias
    slope = jnp.exp(jnp.minimum(pre, 0.0))
    code = jnp.where(pre > 0, pre, slope - 1.0).astype(BF16).astype(F32)
    slope_out[...] = jnp.where(code_mask > 0.5, slope, -slope).reshape(NB, rows, 256)
    mine_rows = own_rows(z, odd)
    first_sum = jnp.zeros((1, 256), F32)
    count_sum = jnp.zeros((1, 256), F32)
    blocks, weighted = [], []
    for b in range(NB):
        here = code[b * rows : b * rows + rows]
        allowed = jnp.where(mine_rows, code_mask[b * rows : b * rows + rows], 0.0)
        first_sum = first_sum + jnp.sum(here * allowed, axis=0, keepdims=True)
        count_sum = count_sum + jnp.sum(allowed, axis=0, keepdims=True)
        blocks.append(here)
        weighted.append((here * allowed).astype(BF16))
    second = dot(jnp.concatenate(weighted, axis=0), code.astype(BF16), ((0,), (0,)))
    for b, (low, high) in enumerate(mend_coarse(blocks)):
        code_out[b, :, 0:128] = low.astype(BF16)
        code_out[b, :, 128:256] = high.astype(BF16)
    lane_u = iota((16, 256), 1) >> 4
    total = jnp.zeros((16, 256), F32)
    for u in range(1, UW - 1):
        total = jnp.where(lane_u == u, second[u * 16 : u * 16 + 16], total)
    total = fold(total[:, :128] + total[:, 128:], (64, 32, 16))
    diagonal = (iota((8, 128), 1) >> 4) == iota((8, 128), 0)
    pay = [
        jnp.sum(jnp.where(diagonal, total[h * 8 : h * 8 + 8], 0.0), axis=0, keepdims=True)
        for h in range(2)
    ]
    for s in (first_sum, count_sum):
        pay.append(fold(jnp.broadcast_to(s[:, :128] + s[:, 128:], (8, 128)), (64, 32, 16))[0:1])
    pay = jnp.concatenate(pay, axis=0)
    for i in range(pay_out.shape[0]):
        pay_out[i] = pay


def decode_kernel(
    z, cotangent, halo, code, in_mask, halo_mask, weights, aux,
    recon_out, sent_out, pay_out,
    cot_buf, sh, cot_frame, sems,
):
    section = lax.axis_index("section")
    odd = lax.rem(lax.axis_index("wide"), 2)
    rows = z.rows
    copy = pltpu.make_async_copy(
        cotangent.at[pl.ds(section * z.mb, z.mb)], cot_buf, sems.at[0]
    )
    copy.start()
    put_frame(
        z, sh, [(code[b, :, 0:128].astype(F32), code[b, :, 128:256].astype(F32)) for b in range(NB)]
    )
    raws = spread(z, sh, weights)
    columns = window_columns()
    halo_cot = dot(dot(gather_halo(z), halo[:, z.span : 2 * z.span]).astype(BF16), columns)
    copy.wait()
    own_cot = dot(dot(gather_rows(z), cot_buf[...].reshape(z.own, z.span)).astype(BF16), columns)
    put_pixels(
        z, cot_frame, odd, own_cot * in_mask[...].astype(F32), halo_cot * halo_mask[...].astype(F32)
    )
    mine_rows = own_rows(z, odd)
    u_local = (iota((1, 128), 1) >> 3) & (UW - 1)
    inner = mine_rows & (u_local >= 1) & (u_local <= UW - 2)
    grads = []
    bias_sum = jnp.zeros((1, 128), F32)
    for h in range(2):
        raw = raws[h] + aux[0:1]
        slope = jnp.exp(jnp.minimum(raw, 0.0))
        recon = jnp.where(raw > 0, raw, slope - 1.0)
        cs = slice(h * 128, h * 128 + 128)
        for b in range(NB):
            rs = slice(b * rows, b * rows + rows)
            sh[b, 8 : 8 + rows, cs] = recon[rs]
            grad = (cot_frame[b, 8 : 8 + rows, cs] * slope[rs]).astype(BF16).astype(F32)
            bias_sum = bias_sum + jnp.sum(jnp.where(inner, grad, 0.0), axis=0, keepdims=True)
            grads.append(grad)
    recon_out[...] = to_pixels(z, odd, sh, in_mask[...])
    put_frame(z, sh, mend_fine([(grads[b], grads[NB + b]) for b in range(NB)]))
    taps = jnp.concatenate([fine_taps(z, sh, b) for b in range(NB)], axis=0)
    sent_out[...] = dot(taps, weights[...]).astype(BF16).reshape(NB, rows, 256)
    mine = jnp.concatenate(
        [jnp.where(mine_rows, code[b].astype(F32), 0.0).astype(BF16) for b in range(NB)], axis=0
    )
    pay = pick_taps(dot(mine, taps, ((0,), (0,))))
    bias_sum = fold(jnp.broadcast_to(bias_sum, (16, 128)), (64, 32, 16, 8))
    lane = iota((16, 128), 1)
    keep = (lane < 8) & ((lane >> 1) == iota((16, 128), 0))
    column = jnp.sum(jnp.where(keep, bias_sum, 0.0), axis=1, keepdims=True)
    pay_out[...] = jnp.where(lane >= 120, column, pay)


def whiten_kernel(
    z, stats, code, slope, sent, taps, decode_pay, aux,
    grad_out, pay_out, mean_out, cov_out,
):
    odd = lax.rem(lax.axis_index("wide"), 2)
    rows = z.rows
    pay = jnp.sum(stats[...], axis=0)
    count = pay[3:4]
    mean = pay[2:3] / count
    diagonal = (iota((8, 128), 1) >> 4) == iota((8, 128), 0)
    second = jnp.concatenate(
        [
            fold(jnp.where(diagonal, jnp.broadcast_to(pay[h : h + 1], (8, 128)), 0.0), (64, 32, 16))
            for h in range(2)
        ],
        axis=0,
    )
    lane = iota((16, 128), 1)
    row = iota((16, 128), 0)
    wide_mean = jnp.broadcast_to(mean, (16, 128))
    mean_column = jnp.sum(jnp.where(lane == row, wide_mean, 0.0), axis=1, keepdims=True)
    cov = second / jnp.broadcast_to(count, (16, 128)) - mean_column * wide_mean
    mean_out[...] = decay_rate * aux[16:17, 0:CCODE] + (1.0 - decay_rate) * mean[:, 0:CCODE]
    cov_out[...] = decay_rate * aux[24:40, 0:CCODE] + (1.0 - decay_rate) * cov[:, 0:CCODE]
    offset = cov - jnp.where((lane & 15) == row, 1.0, 0.0)
    pulled = jnp.sum(offset * mean_column, axis=0, keepdims=True)
    linear = whiten_weight * mean - 2.0 * whiten_weight * pulled
    linear = jnp.concatenate([linear, linear], axis=1)
    offset = 2.0 * whiten_weight * jnp.concatenate([offset, offset], axis=1)
    same = (iota((256, 256), 0) >> 4) == (iota((256, 256), 1) >> 4)
    matrix = jnp.broadcast_to(offset[None], (16, 16, 256)).reshape(256, 256)
    high, mid, _ = split(jnp.where(same, matrix, 0.0))
    flat = code[...].reshape(z.frame, 256)
    turned = dot(
        jnp.concatenate([flat, flat], axis=1), jnp.concatenate([high, mid], axis=0)
    ) + linear
    mine_rows = own_rows(z, odd)
    lane_u = iota((1, 256), 1) >> 4
    inner = mine_rows & (lane_u >= 1) & (lane_u <= UW - 2)
    last = HW // 2 - (NB - 1) * (UW - 2)
    blocks, mine = [], []
    bias_sum = jnp.zeros((1, 256), F32)
    for b in range(NB):
        signed = slope[b]
        pull = jnp.where(signed > 0, turned[b * rows : b * rows + rows], 0.0)
        grad = ((sent[b].astype(F32) + pull) * jnp.abs(signed)).astype(BF16).astype(F32)
        kept = jnp.where(inner & (lane_u <= last) if b == NB - 1 else inner, grad, 0.0)
        bias_sum = bias_sum + jnp.sum(kept, axis=0, keepdims=True)
        blocks.append(grad)
        mine.append(kept.astype(BF16))
    for b, (low, high) in enumerate(mend_coarse(blocks)):
        grad_out[b, :, 0:128] = low.astype(BF16)
        grad_out[b, :, 128:256] = high.astype(BF16)
    products = dot(
        jnp.concatenate(mine, axis=0), taps[...].reshape(z.frame, KS * 128), ((0,), (0,))
    )
    encode_pay = pick_taps(products)
    bias_sum = fold(
        jnp.broadcast_to(bias_sum[:, :128] + bias_sum[:, 128:], (16, 128)), (64, 32, 16)
    )
    column = jnp.sum(jnp.where(lane == row, bias_sum, 0.0), axis=1, keepdims=True)
    decoded = decode_pay[...]
    biases = jnp.where((lane & 1) == 0, column, decoded)
    coarse = biases.astype(BF16).astype(F32)
    biases = jnp.where((lane & 2) == 0, coarse, biases - coarse)
    encode_pay = jnp.where(lane >= 120, biases, encode_pay)
    decoded = jnp.where(lane >= 120, biases, decoded)
    half = pay_out.shape[0] // 2
    for i in range(half):
        pay_out[i] = encode_pay.astype(BF16)
        pay_out[half + i] = decoded.astype(BF16)


def spread_kernel(z, grad, in_mask, weights, pixels_out, sh):
    odd = lax.rem(lax.axis_index("wide"), 2)
    rows = z.rows
    put_frame(
        z, sh, [(grad[b, :, 0:128].astype(F32), grad[b, :, 128:256].astype(F32)) for b in range(NB)]
    )
    raws = spread(z, sh, weights)
    for h in range(2):
        for b in range(NB):
            sh[b, 8 : 8 + rows, h * 128 : h * 128 + 128] = raws[h][b * rows : b * rows + rows]
    pixels_out[...] = to_pixels(z, odd, sh, in_mask[...])


def place_kernel(z, mine, arrived, pixels_out, order_out, sems):
    first = lax.axis_index("section") * z.mb
    copies = [
        pltpu.make_async_copy(mine, pixels_out.at[0, pl.ds(first, z.mb)], sems.at[0]),
        pltpu.make_async_copy(
            arrived, pixels_out.at[0, pl.ds(z.micro - z.mb - first, z.mb)], sems.at[1]
        ),
    ]
    for copy in copies:
        copy.start()
    order_out[...] = jnp.zeros((8, 128), F32)
    for copy in copies:
        copy.wait()


def finish_kernel(z, parts, order, kernel_out, enc_out, dec_out):
    total = jnp.sum(parts[...].astype(F32), axis=0)
    lane = iota((16, 128), 1)
    row = iota((16, 128), 0)
    for slot, out in ((120, enc_out), (121, dec_out)):
        chosen = (lane == slot) | (lane == slot + 2)
        column = jnp.sum(jnp.where(chosen, total, 0.0), axis=1, keepdims=True)
        flat = jnp.sum(jnp.where(lane == row, column, 0.0), axis=0, keepdims=True)
        out[...] = flat[:, 0 : out.shape[1]]
    onehot = tap_onehot()
    chosen = sum(dot(x, onehot) for x in split(total))
    _, o = tap_target(iota((1, NK), 1))
    kernel_out[...] = jnp.sum(
        jnp.where(iota((16, NK), 0) == o, chosen, 0.0), axis=0, keepdims=True
    )


VMEM = pl.BlockSpec(memory_space=pltpu.VMEM)
HBM = pl.BlockSpec(memory_space=pltpu.HBM)
PARAMS = pltpu.CompilerParams(vmem_limit_bytes=24 * 1024 * 1024)
DMA = pltpu.SemaphoreType.DMA


def shape(*dims, dtype=BF16):
    return jax.ShapeDtypeStruct(dims, dtype)


def shards(sections, wides):
    def run(
        fields, pixel_mask, channel_counts, kernels, enc_bias, dec_bias, cotangent, run_mean, run_cov
    ):
        z = Sizes(fields.shape, sections)
        assert 2 * z.band == HW and z.span == CIN * HW and z.mb == 4
        (
            fields, cotangent, pixel_mask, kernels, channel_counts, enc_bias, dec_bias,
            run_mean, run_cov,
        ) = (
            pltpu.with_memory_space_constraint(x, pltpu.HBM)
            for x in (
                fields, cotangent, pixel_mask, kernels, channel_counts, enc_bias, dec_bias,
                run_mean, run_cov,
            )
        )
        section = lax.axis_index("section")
        leads = section == 0
        swap = [(i, i ^ 1) for i in range(sections)]
        pair = [(i, i ^ 1) for i in range(wides)]
        frame = (NB, z.rows, 256)
        framed = pltpu.VMEM((NB, z.rows + 16, 256), F32)
        band_buf = pltpu.VMEM((z.mb, z.band, z.span), BF16)
        mask_buf = pltpu.VMEM((z.mb, z.band, HW), jnp.int32)
        edge_buf = pltpu.VMEM((z.mb, 16, z.span), BF16)
        heavy = pl.CostEstimate(flops=4_000_000_000, bytes_accessed=4_000_000, transcendentals=0)

        def call(kernel, name, outs, ins, scratch, out_specs=None, cost=None):
            return pl.pallas_call(
                lambda *refs: kernel(z, *refs),
                out_shape=outs,
                in_specs=ins,
                out_specs=out_specs or [VMEM] * len(outs),
                scratch_shapes=scratch,
                compiler_params=PARAMS,
                cost_estimate=cost,
                name=name,
            )

        halo, kernel_own = call(
            edge_kernel,
            "edge",
            [shape(z.halo, 2 * z.span + HW), shape(1, NK)],
            [HBM] * 4,
            [edge_buf, edge_buf, pltpu.VMEM((z.mb, 16, HW), jnp.int32), DMA((4,))],
        )(fields, cotangent, pixel_mask, kernels)
        halo = lax.ppermute(halo, "wide", pair)
        kernel_other = lax.ppermute(kernel_own, "section", swap)
        pixels, in_mask, w0, w1, aux = call(
            prepare_kernel,
            "prepare",
            [
                shape(z.own, NB * 128),
                shape(z.own, NB * 128),
                shape(KS * 128, 256),
                shape(KS * 128, 256),
                shape(56, 128, dtype=F32),
            ],
            [HBM] * 7 + [VMEM] * 2,
            [
                band_buf,
                mask_buf,
                pltpu.SMEM(enc_bias.shape, F32),
                pltpu.SMEM(dec_bias.shape, F32),
                pltpu.SMEM(channel_counts.shape, jnp.int32),
                pltpu.SMEM(run_mean.shape, F32),
                pltpu.VMEM(run_cov.shape, F32),
                DMA((7,)),
            ],
            cost=heavy,
        )(
            fields, pixel_mask, enc_bias, dec_bias, channel_counts, run_mean, run_cov,
            kernel_own, kernel_other,
        )
        taps, code, slope, halo_mask, pay = call(
            encode_kernel,
            "encode",
            [
                shape(NB, z.rows, KS * 128),
                shape(*frame),
                shape(*frame, dtype=F32),
                shape(z.halo, NB * 128),
                shape(sections * wides, 4, 128, dtype=F32),
            ],
            [VMEM] * 5,
            [framed, pltpu.VMEM((NB, z.rows, 128), BF16)],
        )(pixels, in_mask, halo, w0, aux)
        stats = lax.all_to_all(pay, ("section", "wide"), 0, 0)
        recon, sent, decode_pay = call(
            decode_kernel,
            "decode",
            [shape(z.mb, z.band, z.span), shape(*frame), shape(CCODE, 128, dtype=F32)],
            [HBM] + [VMEM] * 6,
            [band_buf, framed, framed, DMA((1,))],
            cost=heavy,
        )(cotangent, halo, code, in_mask, halo_mask, w1, aux)
        grad, pay, new_mean, new_cov = call(
            whiten_kernel,
            "whiten",
            [
                shape(*frame),
                shape(sections * wides, CCODE, 128),
                shape(1, CCODE, dtype=F32),
                shape(CCODE, CCODE, dtype=F32),
            ],
            [VMEM] * 7,
            [],
        )(stats, code, slope, sent, taps, decode_pay, aux)
        parts = lax.all_to_all(pay, ("section", "wide"), 0, 0)
        (pixels,) = call(
            spread_kernel,
            "spread",
            [shape(z.mb, z.band, z.span)],
            [VMEM] * 3,
            [framed],
            cost=heavy,
        )(grad, in_mask, w0)
        mine = jnp.where(leads, pixels, recon)
        arrived = lax.ppermute(jnp.where(leads, recon, pixels), "section", swap)
        pixels_out, order = call(
            place_kernel,
            "place",
            [shape(1, z.micro, z.band, z.span), shape(8, 128, dtype=F32)],
            [VMEM] * 2,
            [DMA((2,))],
            out_specs=[HBM, VMEM],
        )(mine, arrived)
        kernel_grads, enc_grad, dec_grad = call(
            finish_kernel,
            "finish",
            [
                shape(1, NK, dtype=F32),
                shape(1, CCODE, dtype=F32),
                shape(1, CIN, dtype=F32),
            ],
            [VMEM] * 2,
            [],
        )(parts, order)
        return (
            pixels_out,
            kernel_grads,
            enc_grad.reshape(CCODE),
            dec_grad.reshape(CIN),
            new_mean.reshape(CCODE),
            new_cov,
        )

    return run


def solution(mesh):
    in_specs = (
        P(None, "wide", None),
        P(None, "wide", None),
        P(),
        P("section", None),
        P(),
        P(),
        P(None, "wide", None),
        P(),
        P(),
    )
    out_specs = (P("section", None, "wide", None), P("section", None), P(), P(), P(), P())
    run = shards(mesh.shape["section"], mesh.shape["wide"])
    return jax.shard_map(run, mesh=mesh, in_specs=in_specs, out_specs=out_specs, check_vma=False)
```

time: 49.9 us -> 39.9 us (0.80)
  blocking collectives: 13.8 us -> 0 us
  waiting for transfers between devices: 4.04 us -> 10.7 us
  local copies, waits for them, and re-layouts: 6.15 us -> 0.97 us
  starting transfers between devices: 9.95 us -> 12.6 us
  other arithmetic: 1.69 us -> 0.05 us
  Pallas kernels: 13 us -> 14.5 us
    all_to_all x1 -> x0, blocking collectives: 13.8 us -> none  [run(): lax.all_to_all(jnp.broadcast_to(total[None], (wides, CCODE, 128)), 'wide'...]
    all_to_all x0 -> x1, waiting for transfers between devices: none -> 7.08 us  [run(): parts = lax.all_to_all(pay, ('section', 'wide'), 0, 0)]
    unnamed x24 -> x4, local copies, waits for them, and re-layouts: 5.36 us -> 0.97 us
    all_to_all x0 -> x1, starting transfers between devices: none -> 3.32 us  [run(): parts = lax.all_to_all(pay, ('section', 'wide'), 0, 0)]
    ppermute x3 -> x2, waiting for transfers between devices: 2.21 us -> 0.01 us  [the longest x1 0.01 us: run(): kernel_other = lax.ppermute(kernel_own, 'section', swap)]
    all_to_all x1, waiting for transfers between devices: 0.67 us -> 2.7 us  [run(): stats = lax.all_to_all(pay, ('section', 'wide'), 0, 0)]
    pallas_call x5 -> x8, Pallas kernels: 13 us -> 14.5 us  [the longest x1 3.64 us: run(): call(decode_kernel, 'decode', [shape(z.mb, z.band, z.span), shape(*frame)...]
    select_n x2 -> x1, other arithmetic: 0.91 us -> 0.05 us  [run(): arrived = lax.ppermute(jnp.where(leads, recon, pixels), 'section', swap)]
  transfers between devices with their start and end apart: 5 -> 5, of which waited for: 4 -> 3; matrix products, arithmetic and copies ran while one was open for 0% -> 0% of each run, Pallas kernels for 10% -> 16%
where the time goes in v2:
time: 39.9 us; the launch traced here: 39.5 us
  Pallas kernels  14.5 us (36%)
  starting transfers between devices  12.6 us (32%)
  waiting for transfers between devices  10.7 us (27%)
  local copies, waits for them, and re-layouts  0.97 us (2%)
  between operations  0.73 us (2%)
    all_to_all x1, waiting for transfers between devices, run(): parts = lax.all_to_all(pay, ('section', 'wide'), 0, 0)  7.08 us
    all_to_all x1, starting transfers between devices, run(): stats = lax.all_to_all(pay, ('section', 'wide'), 0, 0)  6.11 us
    pallas_call x1, Pallas kernels, run(): call(decode_kernel, 'decode', [shape(z.mb, z.band, z.span), shape(*frame)...  3.64 us
    all_to_all x1, starting transfers between devices, run(): parts = lax.all_to_all(pay, ('section', 'wide'), 0, 0)  3.32 us
    all_to_all x1, waiting for transfers between devices, run(): stats = lax.all_to_all(pay, ('section', 'wide'), 0, 0)  2.7 us
    ppermute x1, starting transfers between devices, run(): halo = lax.ppermute(halo, 'wide', pair)  2.56 us
    pallas_call x1, Pallas kernels, run(): call(whiten_kernel, 'whiten', [shape(*frame), shape(sections * wides, CCO...  2.47 us
    pallas_call x1, Pallas kernels, run(): call(encode_kernel, 'encode', [shape(NB, z.rows, KS * 128), shape(*frame)...  2.41 us
  transfers between devices with their start and end apart: 5, of which 3 were waited for; matrix products, arithmetic and copies ran while one was open for 0% of the time, Pallas kernels for 16%

profile of v2, /device:TPU:0, one launch (start us, length us, event | category | flops | bytes accessed | tf_op | source)
XLA Modules:
  0.0 39.5 jit_solution(6114098876480230892)
XLA Ops:
  0.6 0.9 %edge.1 = (bf16[32,1152]{1,0:T(8,128)(2,1)S(1)}, bf16[1,1600]{1,0:T(2,128)(2,1)S(1)}) custom-call(bf16[8,64,512]{2,1,0:T(8,128)(2,1)} %refs_0_.4, bf16[8,64,512]{2,1,0:T(8,128)(2,1)} %refs_0_.5, s32[8,64,128]{2,1,0:T(8,128)} %refs_1_.3, bf16[1,1600]{1,0:T(2,128)(2,1)} %refs_3_.2), custom_call_target="tpu_custom_call" | custom-call | tf_op jit(solution)/shard_map/edge/pallas_call | solution.py:670
  1.6 0.5 %collective-permute-start = (bf16[1,1600]{1,0:T(2,128)(2,1)S(1)}, bf16[1,1600]{1,0:T(2,128)(2,1)S(1)}, u32[]{:S(2)}, u32[]{:S(2)}) collective-permute-start(bf16[1,1600]{1,0:T(2,128)(2,1)S(1)} %get-tuple-element.30.refs_7_), channel_id=1, source_target_pairs={{0,16},{16,0},{1,17},{17,1},{2,18},{18,2},{3,19},{19,3},{4,20},{20... | collective-permute-start | bytes 9608 | tf_op jit(solution)/shard_map/ppermute | solution.py:678
  2.1 2.6 %collective-permute-start.1 = (bf16[32,1152]{1,0:T(8,128)(2,1)S(1)}, bf16[32,1152]{1,0:T(8,128)(2,1)S(1)}, u32[]{:S(2)}, u32[]{:S(2)}) collective-permute-start(bf16[32,1152]{1,0:T(8,128)(2,1)S(1)} %get-tuple-element.33), channel_id=1, source_target_pairs={{0,1},{1,0},{2,3},{3,2},{4,5},{5,4},{6,7},{7,6},{8,9},{9,8},{10,11... | collective-permute-start | bytes 221192 | tf_op jit(solution)/shard_map/ppermute | solution.py:677
  4.7 0.0 collective-permute-done.refs_8_
  4.7 2.0 %prepare.1 = (bf16[256,640]{1,0:T(8,128)(2,1)S(1)}, bf16[256,640]{1,0:T(8,128)(2,1)S(1)}, bf16[640,256]{1,0:T(8,128)(2,1)S(1)}, bf16[640,256]{1,0:T(8,128)(2,1)S(1)}, f32[56,128]{1,0:T(8,128)S(1)}) custom-call(bf16[8,64,512]{2,1,0:T(8,128)(2,1)} %refs_0_.4, s32[8,64,128]{2,1,0:T(8,128)} %refs_1_.3, f32[16]{0:T(128)} %refs_2_.3, f32[4]{0:T(128)} %refs_3_.3, ...), custom_call_target="tpu_custom_call" | custom-call | flops 4000000000 | bytes 4000000 | tf_op jit(solution)/shard_map/prepare/pallas_call | solution.py:679
  6.6 0.0 copy-start
  6.6 0.9 %collective-permute-done.1.refs_2_.refs_1_ = bf16[32,1152]{1,0:T(8,128)(2,1)S(1)} collective-permute-done((bf16[32,1152]{1,0:T(8,128)(2,1)S(1)}, bf16[32,1152]{1,0:T(8,128)(2,1)S(1)}, u32[]{:S(2)}, u32[]{:S(2)}) %collective-permute-start.1) | collective-permute-done | bytes 73760 | tf_op jit(solution)/shard_map/ppermute | solution.py:677
  7.5 2.4 %encode.1 = (bf16[5,144,640]{2,1,0:T(8,128)(2,1)S(1)}, bf16[5,144,256]{2,1,0:T(8,128)(2,1)S(1)}, f32[5,144,256]{2,1,0:T(8,128)S(1)}, bf16[32,640]{1,0:T(8,128)(2,1)S(1)}, f32[32,4,128]{2,1,0:T(4,128)}) custom-call(bf16[256,640]{1,0:T(8,128)(2,1)S(1)} %get-tuple-element.31.refs_0_, bf16[256,640]{1,0:T(8,128)(2,1)S(1)} %get-tuple-element.32.refs_1_.refs_3_, ...), custom_call_target="tpu_custom_call" | custom-call | tf_op jit(solution)/shard_map/encode/pallas_call | solution.py:705
  9.9 0.0 copy-done
  9.9 6.1 %all-to-all-start = ((f32[32,4,128]{2,1,0:T(4,128)}), f32[32,4,128]{2,1,0:T(4,128)S(1)}, u32[]{:S(2)}, u32[]{:S(2)}) async-start(f32[32,4,128]{2,1,0:T(4,128)} %get-tuple-element.36), calls=%async_computation | async-start | bytes 131072 | tf_op jit(solution)/shard_map/all_to_all | solution.py:718
  16.1 0.0 copy-start.1
  16.1 1.0 %copy-done.1 = bf16[640,256]{1,0:T(8,128)(2,1)S(1)} copy-done((bf16[640,256]{1,0:T(8,128)(2,1)S(1)}, bf16[640,256]{1,0:T(8,128)(2,1)}, u32[]{:S(2)}) %copy-start.1) | copy-done | bytes 327704
  17.0 3.6 %decode.1 = (bf16[4,64,512]{2,1,0:T(8,128)(2,1)S(1)}, bf16[5,144,256]{2,1,0:T(8,128)(2,1)S(1)}, f32[16,128]{1,0:T(8,128)S(1)}) custom-call(bf16[8,64,512]{2,1,0:T(8,128)(2,1)} %refs_0_.5, bf16[32,1152]{1,0:T(8,128)(2,1)S(1)} %collective-permute-done.1.refs_2_.refs_1_, bf16[5,144,256]{2,1,0:T(8,128)(2,1)S(1)} %get-tuple-element.37.refs_2_.refs_1_, ...), custom_call_target="tpu_custom_call" | custom-call | flops 4000000000 | bytes 4000000 | tf_op jit(solution)/shard_map/decode/pallas_call | solution.py:719
  20.7 2.7 %all-to-all-done.refs_0_ = f32[32,4,128]{2,1,0:T(4,128)S(1)} async-done(((f32[32,4,128]{2,1,0:T(4,128)}), f32[32,4,128]{2,1,0:T(4,128)S(1)}, u32[]{:S(2)}, u32[]{:S(2)}) %all-to-all-start) | async-done | bytes 65568 | tf_op jit(solution)/shard_map/all_to_all | solution.py:718
  23.4 2.5 %whiten.1 = (bf16[5,144,256]{2,1,0:T(8,128)(2,1)S(1)}, bf16[32,16,128]{2,1,0:T(8,128)(2,1)}, f32[1,16]{1,0:T(1,128)}, f32[16,16]{1,0:T(8,128)}) custom-call(f32[32,4,128]{2,1,0:T(4,128)S(1)} %all-to-all-done.refs_0_, bf16[5,144,256]{2,1,0:T(8,128)(2,1)S(1)} %get-tuple-element.37.refs_2_.refs_1_, f32[5,144,256]{2,1,0:T(8,128)S(1)} %get-tuple-element.38.refs_2_, ...), custom_call_target="tpu_custom_call" | custom-call | tf_op jit(solution)/shard_map/whiten/pallas_call | solution.py:727
  25.8 1.3 %spread.1 = bf16[4,64,512]{2,1,0:T(8,128)(2,1)S(1)} custom-call(bf16[5,144,256]{2,1,0:T(8,128)(2,1)S(1)} %get-tuple-element.44.refs_0_, bf16[256,640]{1,0:T(8,128)(2,1)S(1)} %get-tuple-element.32.refs_1_.refs_3_, bf16[640,256]{1,0:T(8,128)(2,1)S(1)} %get-tuple-element.34.refs_3_.refs_2_), custom_call_target="tpu_custom_call" | custom-call | flops 4000000000 | bytes 4000000 | tf_op jit(solution)/shard_map/spread/pallas_call | solution.py:740
  27.2 0.1 collective-permute-start.2
  27.3 3.3 %all-to-all-start.1 = ((bf16[32,16,128]{2,1,0:T(8,128)(2,1)}), bf16[32,16,128]{2,1,0:T(8,128)(2,1)S(1)}, u32[]{:S(2)}, u32[]{:S(2)}) async-start(bf16[32,16,128]{2,1,0:T(8,128)(2,1)} %get-tuple-element.47), calls=%async_computation.1 | async-start | bytes 262144 | tf_op jit(solution)/shard_map/all_to_all | solution.py:739
  30.6 0.0 collective-permute-done.2.refs_1_
  30.6 0.8 %place.1 = (bf16[1,8,64,512]{3,2,1,0:T(8,128)(2,1)}, f32[8,128]{1,0:T(8,128)S(1)}) custom-call(bf16[4,64,512]{2,1,0:T(8,128)(2,1)S(1)} %get-tuple-element.55.refs_0_, bf16[4,64,512]{2,1,0:T(8,128)(2,1)S(1)} %collective-permute-done.2.refs_1_), custom_call_target="tpu_custom_call" | custom-call | tf_op jit(solution)/shard_map/place/pallas_call | solution.py:750
  31.5 7.1 %all-to-all-done.1.refs_0_ = bf16[32,16,128]{2,1,0:T(8,128)(2,1)S(1)} async-done(((bf16[32,16,128]{2,1,0:T(8,128)(2,1)}), bf16[32,16,128]{2,1,0:T(8,128)(2,1)S(1)}, u32[]{:S(2)}, u32[]{:S(2)}) %all-to-all-start.1) | async-done | bytes 131104 | tf_op jit(solution)/shard_map/all_to_all | solution.py:739
  38.5 1.0 %finish.1 = (f32[1,1600]{1,0:T(1,128)}, f32[1,16]{1,0:T(1,128)}, f32[1,4]{1,0:T(1,128)}) custom-call(bf16[32,16,128]{2,1,0:T(8,128)(2,1)S(1)} %all-to-all-done.1.refs_0_, f32[8,128]{1,0:T(8,128)S(1)} %get-tuple-element.48.refs_1_), custom_call_target="tpu_custom_call" | custom-call | tf_op jit(solution)/shard_map/finish/pallas_call | solution.py:758
  (1 shorter events, 0.0 us)
Async XLA Ops:
  1.6 3.1 %collective-permute-start = (bf16[1,1600]{1,0:T(2,128)(2,1)S(1)}, bf16[1,1600]{1,0:T(2,128)(2,1)S(1)}, u32[]{:S(2)}, u32[]{:S(2)}) collective-permute-start(bf16[1,1600]{1,0:T(2,128)(2,1)S(1)} %get-tuple-element.30.refs_7_), channel_id=1, source_target_pairs={{0,16},{16,0},{1,17},{17,1},{2,18},{18,2},{3,19},{19,3},{4,20},{20... | collective-permute-start | bytes 9608 | tf_op jit(solution)/shard_map/ppermute | solution.py:678
  2.1 5.4 %collective-permute-start.1 = (bf16[32,1152]{1,0:T(8,128)(2,1)S(1)}, bf16[32,1152]{1,0:T(8,128)(2,1)S(1)}, u32[]{:S(2)}, u32[]{:S(2)}) collective-permute-start(bf16[32,1152]{1,0:T(8,128)(2,1)S(1)} %get-tuple-element.33), channel_id=1, source_target_pairs={{0,1},{1,0},{2,3},{3,2},{4,5},{5,4},{6,7},{7,6},{8,9},{9,8},{10,11... | collective-permute-start | bytes 221192 | tf_op jit(solution)/shard_map/ppermute | solution.py:677
  6.6 3.3 %copy-start = (bf16[640,256]{1,0:T(8,128)(2,1)}, bf16[640,256]{1,0:T(8,128)(2,1)S(1)}, u32[]{:S(2)}) copy-start(bf16[640,256]{1,0:T(8,128)(2,1)S(1)} %get-tuple-element.40.refs_5_) | copy-start | bytes 983044
  9.9 13.4 %all-to-all-start = ((f32[32,4,128]{2,1,0:T(4,128)}), f32[32,4,128]{2,1,0:T(4,128)S(1)}, u32[]{:S(2)}, u32[]{:S(2)}) async-start(f32[32,4,128]{2,1,0:T(4,128)} %get-tuple-element.36), calls=%async_computation | async-start | bytes 131072 | tf_op jit(solution)/shard_map/all_to_all | solution.py:718
  16.1 1.0 %copy-start.1 = (bf16[640,256]{1,0:T(8,128)(2,1)S(1)}, bf16[640,256]{1,0:T(8,128)(2,1)}, u32[]{:S(2)}) copy-start(bf16[640,256]{1,0:T(8,128)(2,1)} %copy-done) | copy-start | bytes 983044
  27.2 3.4 %collective-permute-start.2 = (bf16[4,64,512]{2,1,0:T(8,128)(2,1)S(1)}, bf16[4,64,512]{2,1,0:T(8,128)(2,1)S(1)}, u32[]{:S(2)}, u32[]{:S(2)}) collective-permute-start(bf16[4,64,512]{2,1,0:T(8,128)(2,1)S(1)} %get-tuple-element.54), channel_id=1, source_target_pairs={{0,16},{16,0},{1,17},{17,1},{2,18},{18,2},{3,19},{19,3},{4,20},{20... | collective-permute-start | bytes 786440 | tf_op jit(solution)/shard_map/ppermute | solution.py:749
  27.3 11.2 %all-to-all-start.1 = ((bf16[32,16,128]{2,1,0:T(8,128)(2,1)}), bf16[32,16,128]{2,1,0:T(8,128)(2,1)S(1)}, u32[]{:S(2)}, u32[]{:S(2)}) async-start(bf16[32,16,128]{2,1,0:T(8,128)(2,1)} %get-tuple-element.47), calls=%async_computation.1 | async-start | bytes 262144 | tf_op jit(solution)/shard_map/all_to_all | solution.py:739

commit v3 on v2

v3 whole, which is shorter than its diff:
```python
import jax
import jax.numpy as jnp
from jax import lax
from jax.experimental import pallas as pl
from jax.experimental.pallas import tpu as pltpu
from jax.sharding import PartitionSpec as P

CIN = 4
CCODE = 16
KS = 5
HW = 128

UW = 16
NB = 5
HALO = 8
NK = CCODE * CIN * KS * KS
COPIES = 32

decay_rate = 0.9
whiten_weight = 0.25

F32 = jnp.float32
BF16 = jnp.bfloat16


def iota(shape, dim):
    return lax.broadcasted_iota(jnp.int32, shape, dim)


def hot(mask):
    return jnp.where(mask, 1.0, 0.0).astype(BF16)


def dot(a, b, dims=((1,), (0,))):
    return lax.dot_general(a, b, (dims, ((), ())), preferred_element_type=F32)


def fold(x, unit):
    rolled = [x] + [pltpu.roll(x, step, 1) for step in range(unit, 128, unit)]
    while len(rolled) > 1:
        rolled = [sum(rolled[i : i + 2]) for i in range(0, len(rolled), 2)]
    return rolled[0]


def split(x):
    high = x.astype(BF16)
    rest = x - high.astype(F32)
    mid = rest.astype(BF16)
    return high, mid, (rest - mid.astype(F32)).astype(BF16)


class Sizes:
    def __init__(self, fields, sections):
        self.micro, self.band, self.span = fields
        self.sections = sections
        self.mb = self.micro // sections
        self.jf = self.band // 2 + HALO // 2
        self.rows = self.jf * self.mb
        self.own = self.mb * self.band
        self.halo = self.mb * HALO
        self.shift = self.mb.bit_length() - 1
        self.frame = NB * self.rows
        self.sent = self.halo + self.halo // 2


def tap_target(n):
    o = (n * 5243) >> 19
    t = n - 100 * o
    c = (t * 1311) >> 15
    t = t - 25 * c
    k = (t * 205) >> 10
    l = t - 5 * k
    return (3 * k + (l >> 1)) * 8 + 2 * c + (l & 1), o


def tap_onehot():
    target, _ = tap_target(iota((1, NK), 1))
    return hot(iota((128, NK), 0) == target)


def row_target(z, row):
    half = z.own // 2
    parity = (row >= half).astype(jnp.int32)
    q = row - parity * half
    return (q & (z.mb - 1)) * z.band + 2 * (q >> z.shift) + parity


def gather_rows(z):
    return hot(iota((z.own, z.own), 1) == row_target(z, iota((z.own, 1), 0)))


def scatter_rows(z):
    return hot(iota((z.own, z.own), 0) == row_target(z, iota((1, z.own), 1)))


def gather_halo(z, odd):
    row = iota((2 * z.halo, 1), 0)
    second = (row >= z.halo).astype(jnp.int32)
    row = row - second * z.halo
    half = z.halo // 2
    parity = (row >= half).astype(jnp.int32)
    q = row - parity * half
    m = q & (z.mb - 1)
    r = 2 * (q >> z.shift) + parity
    near = r - odd * (HALO // 2)
    there = (near >= 0) & (near < HALO // 2)
    near = jnp.where(there, z.halo + m * (HALO // 2) + near, -1)
    target = jnp.where(second == 1, near, m * HALO + r)
    return hot(iota((2 * z.halo, z.sent), 1) == target)


def pixel_target(lane, inner):
    u_local = (lane >> 3) & (UW - 1)
    u = (lane >> 7) * (UW - 2) + u_local - 1
    valid = (u >= 0) & (u < HW // 2)
    if inner:
        valid = valid & (u_local >= 1) & (u_local <= UW - 2)
    return 2 * u + (lane & 1), (lane >> 1) & 3, valid


def window_columns():
    col, c, valid = pixel_target(iota((1, NB * 128), 1), False)
    target = jnp.where(valid, c * HW + col, -1)
    return hot(iota((CIN * HW, NB * 128), 0) == target)


def unwindow_columns():
    col, c, valid = pixel_target(iota((NB * 128, 1), 0), True)
    target = jnp.where(valid, c * HW + col, -1)
    return hot(iota((NB * 128, CIN * HW), 1) == target)


def window_mask_columns():
    col, _, valid = pixel_target(iota((1, NB * 128), 1), False)
    return hot(iota((HW, NB * 128), 0) == jnp.where(valid, col, -1))


def code_mask_lanes():
    lane = iota((1, 256), 1)
    u_local = lane >> 4
    inner = (u_local >= 1) & (u_local <= UW - 2)
    return hot(iota((128, 256), 0) == jnp.where(inner, u_local * 8, -1))


def own_rows(z, odd):
    j = (iota((z.rows, 1), 0) >> z.shift) - odd * (HALO // 2)
    return (j >= 0) & (j < z.band // 2)


def places(z, odd):
    own = pl.multiple_of(odd * (z.halo // 2), 16)
    halo = pl.multiple_of((1 - odd) * (z.own // 2), 16)
    return own, halo


def mend_coarse(blocks):
    last = HW // 2 - (NB - 1) * (UW - 2)
    rows = blocks[0].shape[0]
    lane = iota((rows, 128), 1)
    halves = [(x[:, :128], x[:, 128:]) for x in blocks]
    done = []
    for b, (low, high) in enumerate(halves):
        before = pltpu.roll(halves[b - 1][1], 32, 1) if b else 0.0
        new_low = jnp.where(lane < 16, before, low)
        if b + 1 < NB:
            after = pltpu.roll(halves[b + 1][0], 96, 1)
            new_high = jnp.where(lane >= 112, after, high)
        else:
            new_high = jnp.where(lane < (last + 1) * 16 - 128, high, 0.0)
        done.append((new_low, new_high))
    return done


def mend_fine(halves):
    rows = halves[0][0].shape[0]
    lane = iota((rows, 128), 1)
    done = []
    for b in range(NB):
        pair = []
        for h in range(2):
            x = halves[b][h]
            before = pltpu.roll(halves[b - 1][h], 16, 1) if b else 0.0
            after = pltpu.roll(halves[b + 1][h], 112, 1) if b + 1 < NB else 0.0
            x = jnp.where(lane < 8, before, x)
            pair.append(jnp.where(lane >= 120, after, x))
        done.append(tuple(pair))
    return done


def pad_frame(z, sh):
    zeros = jnp.zeros((NB, 8, 256), F32)
    sh[:, 0:8, :] = zeros
    sh[:, 8 + z.rows : 16 + z.rows, :] = zeros


def put_frame(z, sh, halves):
    pad_frame(z, sh)
    for b, (low, high) in enumerate(halves):
        sh[b, 8 : 8 + z.rows, 0:128] = low
        sh[b, 8 : 8 + z.rows, 128:256] = high


def put_pixels(z, sh, odd, own, halo):
    pad_frame(z, sh)
    for start, part in zip(places(z, odd), (own, halo)):
        half = part.shape[0] // 2
        rows = pl.ds(pl.multiple_of(8 + start, 8), half)
        for b in range(NB):
            for h in range(2):
                sh[b, rows, h * 128 : h * 128 + 128] = part[
                    h * half : h * half + half, b * 128 : b * 128 + 128
                ]


def fine_taps(z, sh, b):
    up = sh[b, 8 - z.mb : 8 - z.mb + z.rows, :]
    here = sh[b, 8 : 8 + z.rows, :]
    down = sh[b, 8 + z.mb : 8 + z.mb + z.rows, 0:128]
    return jnp.concatenate([up, here, down], axis=1).astype(BF16)


def coarse_taps(z, sh, b):
    down = sh[b, 8 + z.mb : 8 + z.mb + z.rows, :]
    here = sh[b, 8 : 8 + z.rows, :]
    up = sh[b, 8 - z.mb : 8 - z.mb + z.rows, :]
    return [x.astype(BF16) for x in (down, here, up)]


def spread(z, sh, weights):
    taps = [coarse_taps(z, sh, b) for b in range(NB)]
    down, here, up = (jnp.concatenate([t[i] for t in taps], axis=0) for i in range(3))
    nt = ((1,), (1,))
    out = dot(down, weights[0:256], nt) + dot(here, weights[256:512], nt)
    extra = dot(up, weights[512:640], nt)
    return out[:, :128] + extra, out[:, 128:]


def pick_taps(grads):
    lane = iota((CCODE, 128), 1)
    place = lane >> 3
    pieces = []
    for k in range(KS):
        for shift in (-1, 0, 1):
            total = jnp.zeros((CCODE, 128), F32)
            for u in range(1, UW - 1):
                part = grads[u * 16 : u * 16 + 16, k * 128 : k * 128 + 128]
                total = jnp.where(place == u + shift, part, total)
            pieces.append(total)
    pieces.append(jnp.zeros((CCODE, 128), F32))
    block = lane >> 5
    fours = []
    for first in range(4):
        group = pieces[first::4]
        parts = []
        for j in range(4):
            x = group[j]
            for t in range(1, 4):
                x = jnp.where(block == t, group[(t + j) & 3], x)
            parts.append(x)
        fours.append(
            (parts[0] + pltpu.roll(parts[1], 32, 1))
            + (pltpu.roll(parts[2], 64, 1) + pltpu.roll(parts[3], 96, 1))
        )
    inner = place & 3
    total = None
    for j in range(4):
        x = fours[j]
        for t in range(1, 4):
            x = jnp.where(inner == t, fours[(t + j) & 3], x)
        if j:
            x = jnp.where(inner >= j, pltpu.roll(x, 8 * j, 1), pltpu.roll(x, 96 + 8 * j, 1))
        total = x if total is None else total + x
    return total


def own_frame(z, odd, sh):
    start, _ = places(z, odd)
    half = z.own // 2
    rows = pl.ds(pl.multiple_of(8 + start, 8), half)
    flat = jnp.concatenate(
        [
            jnp.concatenate(
                [sh[b, rows, h * 128 : h * 128 + 128] for b in range(NB)], axis=1
            )
            for h in range(2)
        ],
        axis=0,
    )
    return flat.astype(BF16)


def spread_taps(kernel_pair):
    row = iota((2 * CCODE, NK), 0)
    _, o = tap_target(iota((1, NK), 1))
    values = jnp.where(row < CCODE, kernel_pair[0], kernel_pair[1])
    spreaded = jnp.where((row & (CCODE - 1)) == o, values, 0.0).astype(BF16)
    taps = dot(spreaded, tap_onehot(), ((1,), (1,))).astype(BF16)
    lane = iota((2 * CCODE, 512), 1)
    repeat = hot(iota((2 * CCODE, 512), 0) == ((lane >> 8) * CCODE + (lane & 15)))
    return dot(taps, repeat, ((0,), (0,))).astype(BF16)


def band_weights(wide_taps):
    wide_taps = wide_taps.astype(F32)
    row_u = iota((128, 256), 0) >> 3
    lane_u = iota((128, 256), 1) >> 4
    masks = [row_u == lane_u + shift for shift in (-1, 0, 1)]
    parts = []
    for k in range(KS):
        total = jnp.zeros((128, 256), F32)
        for i, mask in enumerate(masks):
            q = 3 * k + i
            piece = wide_taps[8 * q : 8 * q + 8]
            piece = jnp.broadcast_to(piece[None], (16, 8, 256)).reshape(128, 256)
            total = jnp.where(mask, piece, total)
        parts.append(total.astype(BF16))
    return jnp.concatenate(parts, axis=0)


def edge_kernel(
    z, fields, mask, cotangent, kernel, out, kernel_out,
    field_buf, mask_buf, cot_buf, kernel_buf, sems,
):
    odd = lax.rem(lax.axis_index("wide"), 2)
    first = lax.axis_index("section") * z.mb
    start = pl.multiple_of((1 - odd) * (z.band - 16), 16)
    copies = [
        pltpu.make_async_copy(
            source.at[pl.ds(first, z.mb), pl.ds(start, 16), :], buf, sems.at[i]
        )
        for i, (source, buf) in enumerate(
            ((fields, field_buf), (mask, mask_buf), (cotangent, cot_buf))
        )
    ]
    copies.append(pltpu.make_async_copy(kernel, kernel_buf, sems.at[3]))
    for copy in copies:
        copy.start()
    out[z.halo : z.sent, z.span : z.span + HW] = jnp.zeros((z.sent - z.halo, HW), BF16)
    for copy in copies:
        copy.wait()
    kernel_out[...] = jnp.broadcast_to(kernel_buf[...].astype(F32), (COPIES, NK)).astype(BF16)

    def edge_rows(buf, count):
        rows = buf[...].astype(F32)
        rows = jnp.where(odd == 1, rows[:, :count], rows[:, 16 - count :])
        return rows.reshape(z.mb * count, rows.shape[2]).astype(BF16)

    out[0 : z.halo, 0 : z.span] = edge_rows(field_buf, HALO)
    out[0 : z.halo, z.span : z.span + HW] = edge_rows(mask_buf, HALO)
    rows = cot_buf[...].astype(F32)
    rows = jnp.where(odd == 1, rows[:, :HALO], rows[:, 16 - HALO :])
    rows = [
        jnp.where(odd == 1, x[: HALO // 2], x[HALO // 2 :]) for x in (rows[m] for m in range(z.mb))
    ]
    out[z.halo : z.sent, 0 : z.span] = jnp.concatenate(rows, axis=0).astype(BF16)


def prepare_kernel(
    z, fields, mask, cotangent, counts, enc_bias, dec_bias, run_mean, run_cov,
    pixels_out, cot_out, inmask_out, mask_out, aux_out,
    count_buf, enc_buf, dec_buf, mean_buf, cov_buf, sems,
):
    section = lax.axis_index("section")
    wide = lax.axis_index("wide")
    first = section * z.mb
    mine_rows = pl.ds(first, z.mb)
    copies = [
        pltpu.make_async_copy(source, buf, sems.at[i])
        for i, (source, buf) in enumerate(
            (
                (counts, count_buf),
                (enc_bias, enc_buf),
                (dec_bias, dec_buf),
                (run_mean, mean_buf),
                (run_cov, cov_buf),
            )
        )
    ]
    for copy in copies:
        copy.start()
    gather = gather_rows(z)
    columns = window_columns()
    mask_columns = window_mask_columns()
    pixel_mask = mask[mine_rows].astype(F32).astype(BF16).reshape(z.own, HW)
    framed_mask = dot(gather, pixel_mask).astype(BF16)
    mask_out[...] = framed_mask
    in_mask = dot(framed_mask, mask_columns)
    pixels = jnp.concatenate(
        [x[mine_rows].reshape(z.own, z.span) for x in (fields, cotangent)], axis=1
    )
    pixels = dot(gather, pixels).astype(BF16)
    pixels = jnp.concatenate([pixels[:, 0 : z.span], pixels[:, z.span :]], axis=0)
    windowed = dot(pixels, columns)
    for copy in copies:
        copy.wait()
    lane = iota((8, 128), 1)
    dec_row = jnp.zeros((8, 128), F32)
    for c in range(CIN):
        dec_row = jnp.where(((lane >> 1) & 3) == c, dec_buf[c], dec_row)
    enc_row = jnp.zeros((8, 128), F32)
    mean_row = jnp.zeros((8, 128), F32)
    for o in range(CCODE):
        enc_row = jnp.where((lane & 15) == o, enc_buf[o], enc_row)
        mean_row = jnp.where((lane & 15) == o, mean_buf[o], mean_row)
    aux_out[0:8] = dec_row
    aux_out[8:16] = enc_row
    aux_out[16:24] = mean_row
    aux_out[24:40] = jnp.zeros((16, 128), F32)
    aux_out[24:40, 0:CCODE] = cov_buf[...]
    field_now = wide * z.band // HW
    micro = iota((16, 128), 0) & (z.mb - 1)
    count = jnp.zeros((16, 128), jnp.int32)
    for m in range(z.mb):
        count = jnp.where(micro == m, count_buf[first + m, field_now], count)
    channel_ok = jnp.where(((iota((16, 128), 1) >> 1) & 3) < count, 1.0, 0.0)
    aux_out[40:56] = channel_ok
    in_mask = in_mask * jnp.tile(channel_ok, (z.own // 16, NB))
    inmask_out[...] = in_mask.astype(BF16)
    pixels_out[...] = (windowed[0 : z.own] * in_mask).astype(BF16)
    cot_out[...] = (windowed[z.own : 2 * z.own] * in_mask).astype(BF16)


def taps_kernel(z, kernel_own, kernel_other, weights_out):
    mine, other = (x[0:16].astype(F32)[0:1] for x in (kernel_own, kernel_other))
    leads = lax.axis_index("section") == 0
    weights_out[...] = spread_taps((jnp.where(leads, mine, other), jnp.where(leads, other, mine)))


def local_taps(sh, b, rows, step):
    up = sh[b, 16 - step : 16 - step + rows, :]
    here = sh[b, 16 : 16 + rows, :]
    down = sh[b, 16 + step : 16 + step + rows, 0:128]
    return jnp.concatenate([up, here, down], axis=1).astype(BF16)


def encode_rows(taps, weights, bias, masks, mine):
    code_mask = dot(masks, code_mask_lanes())
    pre = dot(taps, band_weights(weights)) + bias
    slope = jnp.exp(jnp.minimum(pre, 0.0))
    code = jnp.where(pre > 0, pre, slope - 1.0).astype(BF16).astype(F32)
    slope = jnp.where(code_mask > 0.5, slope, -slope)
    allowed = code_mask if mine is None else jnp.where(mine, code_mask, 0.0)
    weighted = code * allowed
    second = dot(weighted.astype(BF16), code.astype(BF16), ((0,), (0,)))
    sums = [jnp.sum(x, axis=0, keepdims=True) for x in (weighted, allowed)]
    lane_u = iota((16, 256), 1) >> 4
    total = jnp.zeros((16, 256), F32)
    for u in range(1, UW - 1):
        total = jnp.where(lane_u == u, second[u * 16 : u * 16 + 16], total)
    total = fold(total[:, :128] + total[:, 128:], 16)
    diagonal = (iota((8, 128), 1) >> 4) == iota((8, 128), 0)
    pay = [
        jnp.sum(jnp.where(diagonal, total[h * 8 : h * 8 + 8], 0.0), axis=0, keepdims=True)
        for h in range(2)
    ]
    for s in sums:
        pay.append(fold(jnp.broadcast_to(s[:, :128] + s[:, 128:], (8, 128)), 16)[0:1])
    return code, slope, jnp.concatenate(pay, axis=0)


def put_codes(code, slope, count, start, code_out, slope_out):
    blocks = [code[b * count : b * count + count] for b in range(NB)]
    rows = pl.ds(start, count)
    for b, (low, high) in enumerate(mend_coarse(blocks)):
        code_out[b, rows, 0:128] = low.astype(BF16)
        code_out[b, rows, 128:256] = high.astype(BF16)
        slope_out[b, rows, :] = slope[b * count : b * count + count]


def inner_kernel(z, pixels, own_mask, weights, aux, taps_out, code_out, slope_out, pay_out, sh):
    odd = lax.rem(lax.axis_index("wide"), 2)
    half = z.own // 2
    count = half - 16
    zeros = jnp.zeros((NB, 16, 256), F32)
    sh[:, 0:16, :] = zeros
    sh[:, half : half + 16, :] = zeros
    here = pl.ds(pl.multiple_of((1 - odd) * 16, 16), half)
    for b in range(NB):
        for h in range(2):
            sh[b, here, h * 128 : h * 128 + 128] = pixels[
                h * half : h * half + half, b * 128 : b * 128 + 128
            ].astype(F32)
    start = pl.multiple_of(odd * 32, 16)
    taps = [local_taps(sh, b, count, z.mb) for b in range(NB)]
    for b in range(NB):
        taps_out[b, pl.ds(start, count), :] = taps[b]
    kept = pl.ds(pl.multiple_of(odd * 16, 16), count)
    masks = jnp.concatenate([own_mask[kept, b * 128 : b * 128 + 128] for b in range(NB)], axis=0)
    bias = jnp.concatenate([aux[8:9], aux[8:9]], axis=1)
    code, slope, pay = encode_rows(
        jnp.concatenate(taps, axis=0), weights[:, 0:256], bias, masks, None
    )
    pay_out[...] = pay
    put_codes(code, slope, count, start, code_out, slope_out)


def encode_kernel(
    z, pixels, own_mask, halo, weights, aux, inner_pay, taps_in, code_in, slope_in,
    taps_out, code_out, slope_out, cot_out, pay_out,
    sh, pays, sem,
):
    odd = lax.rem(lax.axis_index("wide"), 2)
    half = z.own // 2
    count = 32
    gather = gather_halo(z, odd)
    framed_mask = dot(gather[0 : z.halo], halo[:, z.span : z.span + HW]).astype(BF16)
    channel_ok = jnp.tile(aux[40:56], (z.halo // 16, NB))
    halo_mask = dot(framed_mask, window_mask_columns()) * channel_ok
    halo_pixels = dot(dot(gather, halo[:, 0 : z.span]).astype(BF16), window_columns())
    halo_x = halo_pixels[0 : z.halo] * halo_mask
    zeros = jnp.zeros((NB, 16, 256), F32)
    sh[:, 0:16, :] = zeros
    sh[:, 48:64, :] = zeros
    own_start = pl.multiple_of((1 - odd) * (half - 32), 16)
    own_there = pl.ds(pl.multiple_of(odd * 32, 16), 32)
    halo_there = pl.ds(pl.multiple_of((2 - odd) * 16, 16), 16)
    for b in range(NB):
        for h in range(2):
            cs = slice(b * 128, b * 128 + 128)
            own = pixels[pl.ds(pl.multiple_of(own_start + h * half, 16), 32), cs]
            sh[b, own_there, h * 128 : h * 128 + 128] = own.astype(F32)
            sh[b, halo_there, h * 128 : h * 128 + 128] = halo_x[h * 16 : h * 16 + 16, cs]
    start = pl.multiple_of((1 - odd) * (z.rows - count), 16)
    taps = [local_taps(sh, b, count, z.mb) for b in range(NB)]
    for b in range(NB):
        taps_out[b, pl.ds(start, count), :] = taps[b]
    edge_mask = own_mask[pl.ds(pl.multiple_of((1 - odd) * (half - 16), 16), 16), :].astype(F32)
    first = jnp.where(odd == 1, halo_mask[0:16], edge_mask)
    later = jnp.where(odd == 1, edge_mask, halo_mask[0:16])
    masks = jnp.concatenate(
        [x[:, b * 128 : b * 128 + 128] for b in range(NB) for x in (first, later)], axis=0
    ).astype(BF16)
    bias = jnp.concatenate([aux[8:9], aux[8:9]], axis=1)
    mine = ((iota((NB * count, 1), 0) >> 4) & 1) == odd
    code, slope, pay = encode_rows(
        jnp.concatenate(taps, axis=0), weights[:, 0:256], bias, masks, mine
    )
    pay = pay + inner_pay[...]
    for i in range(pays.shape[0]):
        pays[i] = pay
    copy = pltpu.make_async_copy(pays, pay_out, sem.at[0])
    copy.start()
    put_codes(code, slope, count, start, code_out, slope_out)
    cot_out[...] = (halo_pixels[z.halo : 2 * z.halo] * halo_mask).astype(BF16)
    copy.wait()


def decode_kernel(
    z, code, own_cot, halo_cot, weights, aux,
    recon_out, sent_out, pay_out,
    sh, cot_frame,
):
    odd = lax.rem(lax.axis_index("wide"), 2)
    rows = z.rows
    put_frame(
        z, sh, [(code[b, :, 0:128].astype(F32), code[b, :, 128:256].astype(F32)) for b in range(NB)]
    )
    banded = band_weights(weights[:, 256:512])
    raws = spread(z, sh, banded)
    put_pixels(z, cot_frame, odd, own_cot[...].astype(F32), halo_cot[...].astype(F32))
    mine_rows = own_rows(z, odd)
    u_local = (iota((1, 128), 1) >> 3) & (UW - 1)
    inner = mine_rows & (u_local >= 1) & (u_local <= UW - 2)
    grads = []
    bias_sum = jnp.zeros((1, 128), F32)
    for h in range(2):
        raw = raws[h] + aux[0:1]
        slope = jnp.exp(jnp.minimum(raw, 0.0))
        recon = jnp.where(raw > 0, raw, slope - 1.0)
        cs = slice(h * 128, h * 128 + 128)
        for b in range(NB):
            rs = slice(b * rows, b * rows + rows)
            sh[b, 8 : 8 + rows, cs] = recon[rs]
            grad = (cot_frame[b, 8 : 8 + rows, cs] * slope[rs]).astype(BF16).astype(F32)
            bias_sum = bias_sum + jnp.sum(jnp.where(inner, grad, 0.0), axis=0, keepdims=True)
            grads.append(grad)
    recon_out[...] = own_frame(z, odd, sh)
    put_frame(z, sh, mend_fine([(grads[b], grads[NB + b]) for b in range(NB)]))
    taps = jnp.concatenate([fine_taps(z, sh, b) for b in range(NB)], axis=0)
    sent_out[...] = dot(taps, banded).astype(BF16).reshape(NB, rows, 256)
    mine = jnp.concatenate(
        [jnp.where(mine_rows, code[b].astype(F32), 0.0).astype(BF16) for b in range(NB)], axis=0
    )
    pay = pick_taps(dot(mine, taps, ((0,), (0,))))
    bias_sum = fold(jnp.broadcast_to(bias_sum, (16, 128)), 8)
    lane = iota((16, 128), 1)
    keep = (lane < 8) & ((lane >> 1) == iota((16, 128), 0))
    column = jnp.sum(jnp.where(keep, bias_sum, 0.0), axis=1, keepdims=True)
    pay_out[...] = jnp.where(lane >= 120, column, pay)


def whiten_kernel(
    z, stats, code, slope, sent, taps, decode_pay, aux,
    grad_out, pay_out, moments_out,
    pays, sem,
):
    odd = lax.rem(lax.axis_index("wide"), 2)
    rows = z.rows
    pay = jnp.sum(stats[...], axis=0)
    count = pay[3:4]
    mean = pay[2:3] / count
    diagonal = (iota((8, 128), 1) >> 4) == iota((8, 128), 0)
    second = jnp.concatenate(
        [
            fold(jnp.where(diagonal, jnp.broadcast_to(pay[h : h + 1], (8, 128)), 0.0), 16)
            for h in range(2)
        ],
        axis=0,
    )
    lane = iota((16, 128), 1)
    row = iota((16, 128), 0)
    wide_mean = jnp.broadcast_to(mean, (16, 128))
    mean_column = jnp.sum(jnp.where(lane == row, wide_mean, 0.0), axis=1, keepdims=True)
    cov = second / jnp.broadcast_to(count, (16, 128)) - mean_column * wide_mean
    moments_out[0:CCODE] = cov
    moments_out[CCODE:] = jnp.broadcast_to(mean, (8, 128))
    offset = cov - jnp.where((lane & 15) == row, 1.0, 0.0)
    pulled = jnp.sum(offset * mean_column, axis=0, keepdims=True)
    linear = whiten_weight * mean - 2.0 * whiten_weight * pulled
    linear = jnp.concatenate([linear, linear], axis=1)
    offset = 2.0 * whiten_weight * jnp.concatenate([offset, offset], axis=1)
    same = (iota((256, 256), 0) >> 4) == (iota((256, 256), 1) >> 4)
    matrix = jnp.broadcast_to(offset[None], (16, 16, 256)).reshape(256, 256)
    high, mid, _ = split(jnp.where(same, matrix, 0.0))
    flat = code[...].reshape(z.frame, 256)
    turned = dot(
        jnp.concatenate([flat, flat], axis=1), jnp.concatenate([high, mid], axis=0)
    ) + linear
    mine_rows = own_rows(z, odd)
    lane_u = iota((1, 256), 1) >> 4
    inner = mine_rows & (lane_u >= 1) & (lane_u <= UW - 2)
    last = HW // 2 - (NB - 1) * (UW - 2)
    blocks, mine = [], []
    bias_sum = jnp.zeros((1, 256), F32)
    for b in range(NB):
        signed = slope[b]
        pull = jnp.where(signed > 0, turned[b * rows : b * rows + rows], 0.0)
        grad = ((sent[b].astype(F32) + pull) * jnp.abs(signed)).astype(BF16).astype(F32)
        kept = jnp.where(inner & (lane_u <= last) if b == NB - 1 else inner, grad, 0.0)
        bias_sum = bias_sum + jnp.sum(kept, axis=0, keepdims=True)
        blocks.append(grad)
        mine.append(kept.astype(BF16))
    products = dot(
        jnp.concatenate(mine, axis=0), taps[...].reshape(z.frame, KS * 128), ((0,), (0,))
    )
    encode_pay = pick_taps(products)
    bias_sum = fold(jnp.broadcast_to(bias_sum[:, :128] + bias_sum[:, 128:], (16, 128)), 16)
    column = jnp.sum(jnp.where(lane == row, bias_sum, 0.0), axis=1, keepdims=True)
    decoded = decode_pay[...]
    biases = jnp.where((lane & 1) == 0, column, decoded)
    coarse = biases.astype(BF16).astype(F32)
    biases = jnp.where((lane & 2) == 0, coarse, biases - coarse)
    encode_pay = jnp.where(lane >= 120, biases, encode_pay)
    decoded = jnp.where(lane >= 120, biases, decoded)
    half = pays.shape[0] // 2
    for i in range(half):
        pays[i] = encode_pay.astype(BF16)
        pays[half + i] = decoded.astype(BF16)
    copy = pltpu.make_async_copy(pays, pay_out, sem.at[0])
    copy.start()
    for b, (low, high) in enumerate(mend_coarse(blocks)):
        grad_out[b, :, 0:128] = low.astype(BF16)
        grad_out[b, :, 128:256] = high.astype(BF16)
    copy.wait()


def spread_kernel(
    z, grad, mask, weights, recon, aux, moments,
    pixels_out, send_out, onehot_out, mean_out, cov_out,
    sh, mine, means, covs, sems,
):
    section = lax.axis_index("section")
    odd = lax.rem(lax.axis_index("wide"), 2)
    rows = z.rows
    put_frame(
        z, sh, [(grad[b, :, 0:128].astype(F32), grad[b, :, 128:256].astype(F32)) for b in range(NB)]
    )
    raws = spread(z, sh, band_weights(weights[:, 0:256]))
    for h in range(2):
        for b in range(NB):
            sh[b, 8 : 8 + rows, h * 128 : h * 128 + 128] = raws[h][b * rows : b * rows + rows]
    in_mask = dot(mask[...], window_mask_columns()) * jnp.tile(aux[40:56], (z.own // 16, NB))
    in_mask = in_mask.astype(BF16)
    flat = own_frame(z, odd, sh) * in_mask
    other = recon[...] * in_mask
    leads = section == 0
    flat, other = jnp.where(leads, flat, other), jnp.where(leads, other, flat)
    native = dot(jnp.concatenate([flat, other], axis=0), unwindow_columns()).astype(BF16)
    scatter = scatter_rows(z)
    whole = (z.mb, z.band, z.span)
    mine[...] = dot(scatter, native[0 : z.own]).astype(BF16).reshape(whole)
    means[...] = decay_rate * aux[16:17, 0:CCODE] + (1.0 - decay_rate) * moments[16:17, 0:CCODE]
    covs[...] = decay_rate * aux[24:40, 0:CCODE] + (1.0 - decay_rate) * moments[0:16, 0:CCODE]
    copies = [
        pltpu.make_async_copy(source, target, sems.at[i])
        for i, (source, target) in enumerate(
            (
                (mine, pixels_out.at[0, pl.ds(section * z.mb, z.mb)]),
                (means, mean_out),
                (covs, cov_out),
            )
        )
    ]
    for copy in copies:
        copy.start()
    send_out[...] = dot(scatter, native[z.own : 2 * z.own]).astype(BF16).reshape(whole)
    onehot_out[...] = tap_onehot()
    for copy in copies:
        copy.wait()


def total_kernel(z, parts, out):
    out[...] = jnp.sum(parts[...].astype(F32), axis=0)


def finish_kernel(
    z, sums, arrived, onehot, half_done, pixels_out, kernel_out, enc_out, dec_out,
    kernels, encs, decs, sems,
):
    there = z.micro - z.mb - lax.axis_index("section") * z.mb
    copies = [
        pltpu.make_async_copy(source, target, sems.at[i])
        for i, (source, target) in enumerate(
            (
                (arrived, pixels_out.at[0, pl.ds(there, z.mb)]),
                (encs, enc_out),
                (decs, dec_out),
                (kernels, kernel_out),
            )
        )
    ]
    copies[0].start()
    total = sums[...]
    chosen = dot(jnp.concatenate(split(total), axis=0), onehot[...])
    chosen = chosen[0:16] + chosen[16:32] + chosen[32:48]
    _, o = tap_target(iota((1, NK), 1))
    kernels[...] = jnp.sum(jnp.where(iota((16, NK), 0) == o, chosen, 0.0), axis=0, keepdims=True)
    copies[3].start()
    lane = iota((16, 128), 1)
    row = iota((16, 128), 0)
    for slot, out in ((120, encs), (121, decs)):
        chosen = (lane == slot) | (lane == slot + 2)
        column = jnp.sum(jnp.where(chosen, total, 0.0), axis=1, keepdims=True)
        flat = jnp.sum(jnp.where(lane == row, column, 0.0), axis=0, keepdims=True)
        out[...] = flat[:, 0 : out.shape[1]]
    copies[1].start()
    copies[2].start()
    for copy in copies:
        copy.wait()


VMEM = pl.BlockSpec(memory_space=pltpu.VMEM)
HBM = pl.BlockSpec(memory_space=pltpu.HBM)
PARAMS = pltpu.CompilerParams(vmem_limit_bytes=24 * 1024 * 1024)
DMA = pltpu.SemaphoreType.DMA


def shape(*dims, dtype=BF16):
    return jax.ShapeDtypeStruct(dims, dtype)


def shards(sections, wides):
    def run(
        fields, pixel_mask, channel_counts, kernels, enc_bias, dec_bias, cotangent, run_mean, run_cov
    ):
        z = Sizes(fields.shape, sections)
        assert 2 * z.band == HW and z.span == CIN * HW and z.mb == 4
        whole = (fields, pixel_mask, cotangent)
        (
            fields, cotangent, pixel_mask, kernels, channel_counts, enc_bias, dec_bias,
            run_mean, run_cov,
        ) = (
            pltpu.with_memory_space_constraint(x, pltpu.HBM)
            for x in (
                fields, cotangent, pixel_mask, kernels, channel_counts, enc_bias, dec_bias,
                run_mean, run_cov,
            )
        )
        swap = [(i, i ^ 1) for i in range(sections)]
        pair = [(i, i ^ 1) for i in range(wides)]
        frame = (NB, z.rows, 256)
        framed = pltpu.VMEM((NB, z.rows + 16, 256), F32)
        band_buf = pltpu.VMEM((z.mb, z.band, z.span), BF16)
        edge_buf = pltpu.VMEM((z.mb, 16, z.span), BF16)
        heavy = pl.CostEstimate(flops=4_000_000_000, bytes_accessed=4_000_000, transcendentals=0)

        def call(kernel, name, outs, ins, scratch, out_specs=None, cost=None, alias=None):
            return pl.pallas_call(
                lambda *refs: kernel(z, *refs),
                out_shape=outs,
                in_specs=ins,
                out_specs=out_specs or [VMEM] * len(outs),
                scratch_shapes=scratch,
                compiler_params=PARAMS,
                cost_estimate=cost,
                input_output_aliases=alias or {},
                name=name,
            )

        halo, kernel_own = call(
            edge_kernel,
            "edge",
            [shape(z.sent, z.span + HW), shape(COPIES, NK)],
            [HBM] * 4,
            [
                edge_buf,
                pltpu.VMEM((z.mb, 16, HW), jnp.int32),
                edge_buf,
                pltpu.VMEM((1, NK), BF16),
                DMA((4,)),
            ],
        )(fields, pixel_mask, cotangent, kernels)
        halo = lax.ppermute(halo, "wide", pair)
        kernel_other = lax.ppermute(kernel_own, "section", swap)
        pixels, own_cot, in_mask, mask, aux = call(
            prepare_kernel,
            "prepare",
            [
                shape(z.own, NB * 128),
                shape(z.own, NB * 128),
                shape(z.own, NB * 128),
                shape(z.own, HW),
                shape(56, 128, dtype=F32),
            ],
            [VMEM] * 3 + [HBM] * 5,
            [
                pltpu.SMEM(channel_counts.shape, jnp.int32),
                pltpu.SMEM(enc_bias.shape, F32),
                pltpu.SMEM(dec_bias.shape, F32),
                pltpu.SMEM(run_mean.shape, F32),
                pltpu.VMEM(run_cov.shape, F32),
                DMA((5,)),
            ],
            cost=heavy,
        )(*whole, channel_counts, enc_bias, dec_bias, run_mean, run_cov)
        (weights,) = call(taps_kernel, "taps", [shape(128, 512)], [VMEM] * 2, [])(
            kernel_own, kernel_other
        )
        coded = [shape(NB, z.rows, KS * 128), shape(*frame), shape(*frame, dtype=F32)]
        taps, code, slope, pay = call(
            inner_kernel,
            "inner",
            coded + [shape(4, 128, dtype=F32)],
            [VMEM] * 4,
            [pltpu.VMEM((NB, z.own // 2 + 16, 256), F32)],
            cost=heavy,
        )(pixels, in_mask, weights, aux)
        taps, code, slope, halo_cot, pay = call(
            encode_kernel,
            "encode",
            coded + [shape(z.halo, NB * 128), shape(sections * wides, 4, 128, dtype=F32)],
            [VMEM] * 9,
            [
                pltpu.VMEM((NB, 64, 256), F32),
                pltpu.VMEM((sections * wides, 4, 128), F32),
                DMA((1,)),
            ],
            out_specs=[VMEM] * 4 + [HBM],
            alias={6: 0, 7: 1, 8: 2},
        )(pixels, in_mask, halo, weights, aux, pay, taps, code, slope)
        stats = lax.all_to_all(pay, ("section", "wide"), 0, 0)
        recon, sent, decode_pay = call(
            decode_kernel,
            "decode",
            [shape(z.own, NB * 128), shape(*frame), shape(CCODE, 128, dtype=F32)],
            [VMEM] * 5,
            [framed, framed],
            cost=heavy,
        )(code, own_cot, halo_cot, weights, aux)
        grad, pay, moments = call(
            whiten_kernel,
            "whiten",
            [
                shape(*frame),
                shape(sections * wides, CCODE, 128),
                shape(CCODE + 8, 128, dtype=F32),
            ],
            [VMEM] * 7,
            [pltpu.VMEM((sections * wides, CCODE, 128), BF16), DMA((1,))],
            out_specs=[VMEM, HBM, VMEM],
            alias={3: 0},
        )(stats, code, slope, sent, taps, decode_pay, aux)
        parts = lax.all_to_all(pay, ("section", "wide"), 0, 0)
        half_done, sending, onehot, new_mean, new_cov = call(
            spread_kernel,
            "spread",
            [
                shape(1, z.micro, z.band, z.span),
                shape(z.mb, z.band, z.span),
                shape(128, NK),
                shape(1, CCODE, dtype=F32),
                shape(CCODE, CCODE, dtype=F32),
            ],
            [VMEM] * 6,
            [
                framed,
                band_buf,
                pltpu.VMEM((1, CCODE), F32),
                pltpu.VMEM((CCODE, CCODE), F32),
                DMA((3,)),
            ],
            out_specs=[HBM, VMEM, VMEM, HBM, HBM],
            cost=heavy,
        )(grad, mask, weights, recon, aux, moments)
        arrived = lax.ppermute(sending, "section", swap)
        (sums,) = call(
            total_kernel,
            "total",
            [shape(CCODE, 128, dtype=F32)],
            [VMEM],
            [],
            cost=pl.CostEstimate(flops=100_000_000_000, bytes_accessed=0, transcendentals=0),
        )(parts)
        pixels_out, kernel_grads, enc_grad, dec_grad = call(
            finish_kernel,
            "finish",
            [
                shape(1, z.micro, z.band, z.span),
                shape(1, NK, dtype=F32),
                shape(1, CCODE, dtype=F32),
                shape(1, CIN, dtype=F32),
            ],
            [VMEM] * 3 + [HBM],
            [
                pltpu.VMEM((1, NK), F32),
                pltpu.VMEM((1, CCODE), F32),
                pltpu.VMEM((1, CIN), F32),
                DMA((4,)),
            ],
            out_specs=[HBM] * 4,
            alias={3: 0},
        )(sums, arrived, onehot, half_done)
        return (
            pixels_out,
            kernel_grads,
            enc_grad.reshape(CCODE),
            dec_grad.reshape(CIN),
            new_mean.reshape(CCODE),
            new_cov,
        )

    return run


def solution(mesh):
    in_specs = (
        P(None, "wide", None),
        P(None, "wide", None),
        P(),
        P("section", None),
        P(),
        P(),
        P(None, "wide", None),
        P(),
        P(),
    )
    out_specs = (P("section", None, "wide", None), P("section", None), P(), P(), P(), P())
    run = shards(mesh.shape["section"], mesh.shape["wide"])
    return jax.shard_map(run, mesh=mesh, in_specs=in_specs, out_specs=out_specs, check_vma=False)
```

time: 39.9 us -> 36.5 us (0.915)
  starting transfers between devices: 12.6 us -> 11.2 us
  Pallas kernels: 14.5 us -> 13.3 us
  local copies, waits for them, and re-layouts: 0.97 us -> 0.01 us
    all_to_all x1, waiting for transfers between devices: 2.7 us -> 5.38 us  [run(): stats = lax.all_to_all(pay, ('section', 'wide'), 0, 0)]
    all_to_all x1, waiting for transfers between devices: 7.08 us -> 5.41 us  [run(): parts = lax.all_to_all(pay, ('section', 'wide'), 0, 0)]
    unnamed x4 -> x6, local copies, waits for them, and re-layouts: 0.97 us -> 0.01 us
    ppermute x1, waiting for transfers between devices: 0.88 us -> 0.01 us  [run(): halo = lax.ppermute(halo, 'wide', pair)]
    all_to_all x1, starting transfers between devices: 3.32 us -> 2.59 us  [run(): parts = lax.all_to_all(pay, ('section', 'wide'), 0, 0)]
    pallas_call x1, Pallas kernels: 1.96 us -> 1.23 us  [run(): call(prepare_kernel, 'prepare', [shape(z.own, NB * 128), shape(z.own, NB...]
    all_to_all x1, starting transfers between devices: 6.11 us -> 5.44 us  [run(): stats = lax.all_to_all(pay, ('section', 'wide'), 0, 0)]
    ppermute x1, starting transfers between devices: 0.52 us -> 0.01 us  [run(): kernel_other = lax.ppermute(kernel_own, 'section', swap)]
  transfers between devices with their start and end apart: 5 -> 5, of which waited for: 3 -> 3; matrix products, arithmetic and copies ran while one was open for 0% -> 0% of each run, Pallas kernels for 16% -> 20%
where the time goes in v3:
time: 36.5 us; the launch traced here: 36.1 us
  Pallas kernels  13.3 us (36%)
  starting transfers between devices  11.2 us (31%)
  waiting for transfers between devices  10.8 us (30%)
  between operations  0.76 us (2%)
    all_to_all x1, starting transfers between devices, run(): stats = lax.all_to_all(pay, ('section', 'wide'), 0, 0)  5.44 us
    all_to_all x1, waiting for transfers between devices, run(): parts = lax.all_to_all(pay, ('section', 'wide'), 0, 0)  5.41 us
    all_to_all x1, waiting for transfers between devices, run(): stats = lax.all_to_all(pay, ('section', 'wide'), 0, 0)  5.38 us
    ppermute x1, starting transfers between devices, run(): halo = lax.ppermute(halo, 'wide', pair)  3 us
    all_to_all x1, starting transfers between devices, run(): parts = lax.all_to_all(pay, ('section', 'wide'), 0, 0)  2.59 us
    pallas_call x1, Pallas kernels, run(): call(spread_kernel, 'spread', [shape(1, z.micro, z.band, z.span), shape(z...  2.32 us
    pallas_call x1, Pallas kernels, run(): call(whiten_kernel, 'whiten', [shape(*frame), shape(sections * wides, CCO...  2.23 us
    pallas_call x1, Pallas kernels, run(): call(decode_kernel, 'decode', [shape(z.own, NB * 128), shape(*frame), sha...  1.94 us
  transfers between devices with their start and end apart: 5, of which 3 were waited for; matrix products, arithmetic and copies ran while one was open for 0% of the time, Pallas kernels for 20%

profile of v3, /device:TPU:0, one launch (start us, length us, event | category | flops | bytes accessed | tf_op | source)
XLA Modules:
  0.0 36.1 jit_solution(6482523243385291264)
XLA Ops:
  0.6 0.0 copy-start.1
  0.6 0.0 copy-start.2
  0.7 0.0 copy-start
  0.7 1.1 %edge.1 = (bf16[48,640]{1,0:T(8,128)(2,1)S(1)}, bf16[32,1600]{1,0:T(8,128)(2,1)S(1)}) custom-call(bf16[8,64,512]{2,1,0:T(8,128)(2,1)} %refs_0_.3, s32[8,64,128]{2,1,0:T(8,128)} %refs_1_.3, bf16[8,64,512]{2,1,0:T(8,128)(2,1)} %refs_2_.3, bf16[1,1600]{1,0:T(2,128)(2,1)} %refs_3_.3), custom_call_target="tpu_custom_call" | custom-call | tf_op jit(solution)/shard_map/edge/pallas_call | solution.py:800
  1.7 3.0 %collective-permute-start = (bf16[48,640]{1,0:T(8,128)(2,1)S(1)}, bf16[48,640]{1,0:T(8,128)(2,1)S(1)}, u32[]{:S(2)}, u32[]{:S(2)}) collective-permute-start(bf16[48,640]{1,0:T(8,128)(2,1)S(1)} %get-tuple-element.39), channel_id=1, source_target_pairs={{0,1},{1,0},{2,3},{3,2},{4,5},{5,4},{6,7},{7,6},{8,9},{9,8},{10,11... | collective-permute-start | bytes 184328 | tf_op jit(solution)/shard_map/ppermute | solution.py:813
  4.7 0.0 collective-permute-start.1
  4.7 0.0 copy-done.1
  4.7 0.0 copy-done.2
  4.8 0.0 copy-done
  4.8 1.2 %prepare.1 = (bf16[256,640]{1,0:T(8,128)(2,1)S(1)}, bf16[256,640]{1,0:T(8,128)(2,1)S(1)}, bf16[256,640]{1,0:T(8,128)(2,1)S(1)}, bf16[256,128]{1,0:T(8,128)(2,1)S(1)}, f32[56,128]{1,0:T(8,128)S(1)}) custom-call(bf16[8,64,512]{2,1,0:T(8,128)(2,1)S(1)} %copy-done, s32[8,64,128]{2,1,0:T(8,128)S(1)} %copy-done.2, bf16[8,64,512]{2,1,0:T(8,128)(2,1)S(1)} %copy-done.1, ...), custom_call_target="tpu_custom_call" | custom-call | flops 4000000000 | bytes 4000000 | tf_op jit(solution)/shard_map/prepare/pallas_call | solution.py:815
  6.0 0.1 collective-permute-done.1.refs_1_
  6.1 0.5 %taps.1.refs_2_.refs_3_ = bf16[128,512]{1,0:T(8,128)(2,1)S(1)} custom-call(bf16[32,1600]{1,0:T(8,128)(2,1)S(1)} %get-tuple-element.40.refs_0_, bf16[32,1600]{1,0:T(8,128)(2,1)S(1)} %collective-permute-done.1.refs_1_), custom_call_target="tpu_custom_call" | custom-call | tf_op jit(solution)/shard_map/taps/pallas_call | solution.py:836
  6.6 1.3 %inner.1 = (bf16[5,144,640]{2,1,0:T(8,128)(2,1)S(1)}, bf16[5,144,256]{2,1,0:T(8,128)(2,1)S(1)}, f32[5,144,256]{2,1,0:T(8,128)S(1)}, f32[4,128]{1,0:T(4,128)S(1)}) custom-call(bf16[256,640]{1,0:T(8,128)(2,1)S(1)} %get-tuple-element.37.refs_0_, bf16[256,640]{1,0:T(8,128)(2,1)S(1)} %get-tuple-element.38.refs_1_, bf16[128,512]{1,0:T(8,128)(2,1)S(1)} %taps.1.refs_2_.refs_3_, ...), custom_call_target="tpu_custom_call" | custom-call | flops 4000000000 | bytes 4000000 | tf_op jit(solution)/shard_map/inner/pallas_call | solution.py:840
  7.9 0.0 collective-permute-done.refs_2_
  7.9 1.8 %encode.1 = (bf16[5,144,640]{2,1,0:T(8,128)(2,1)S(1)}, bf16[5,144,256]{2,1,0:T(8,128)(2,1)S(1)}, f32[5,144,256]{2,1,0:T(8,128)S(1)}, bf16[32,640]{1,0:T(8,128)(2,1)S(1)}, f32[32,4,128]{2,1,0:T(4,128)}) custom-call(bf16[256,640]{1,0:T(8,128)(2,1)S(1)} %get-tuple-element.37.refs_0_, ...), custom_call_target="tpu_custom_call", output_to_operand_aliasing={{0}: (6, {}), {1}: (7, {}), {2}: (8, {})} | custom-call | tf_op jit(solution)/shard_map/encode/pallas_call | solution.py:848
  9.7 5.4 %all-to-all-start = ((f32[32,4,128]{2,1,0:T(4,128)}), f32[32,4,128]{2,1,0:T(4,128)S(1)}, u32[]{:S(2)}, u32[]{:S(2)}) async-start(f32[32,4,128]{2,1,0:T(4,128)} %get-tuple-element.46), calls=%async_computation | async-start | bytes 131072 | tf_op jit(solution)/shard_map/all_to_all | solution.py:861
  15.2 1.9 %decode.1 = (bf16[256,640]{1,0:T(8,128)(2,1)S(1)}, bf16[5,144,256]{2,1,0:T(8,128)(2,1)S(1)}, f32[16,128]{1,0:T(8,128)S(1)}) custom-call(bf16[5,144,256]{2,1,0:T(8,128)(2,1)S(1)} %get-tuple-element.47.refs_0_.refs_1_, bf16[256,640]{1,0:T(8,128)(2,1)S(1)} %get-tuple-element.49.refs_1_, bf16[32,640]{1,0:T(8,128)(2,1)S(1)} %get-tuple-element.50.refs_2_, ...), custom_call_target="tpu_custom_call" | custom-call | flops 4000000000 | bytes 4000000 | tf_op jit(solution)/shard_map/decode/pallas_call | solution.py:862
  17.1 5.4 %all-to-all-done.refs_0_ = f32[32,4,128]{2,1,0:T(4,128)S(1)} async-done(((f32[32,4,128]{2,1,0:T(4,128)}), f32[32,4,128]{2,1,0:T(4,128)S(1)}, u32[]{:S(2)}, u32[]{:S(2)}) %all-to-all-start) | async-done | bytes 65568 | tf_op jit(solution)/shard_map/all_to_all | solution.py:861
  22.5 2.2 %whiten.1 = (bf16[5,144,256]{2,1,0:T(8,128)(2,1)S(1)}, bf16[32,16,128]{2,1,0:T(8,128)(2,1)}, f32[24,128]{1,0:T(8,128)S(1)}) custom-call(f32[32,4,128]{2,1,0:T(4,128)S(1)} %all-to-all-done.refs_0_, bf16[5,144,256]{2,1,0:T(8,128)(2,1)S(1)} %get-tuple-element.47.refs_0_.refs_1_, ...), custom_call_target="tpu_custom_call", output_to_operand_aliasing={{0}: (3, {})} | custom-call | tf_op jit(solution)/shard_map/whiten/pallas_call | solution.py:870
  24.7 2.6 %all-to-all-start.1 = ((bf16[32,16,128]{2,1,0:T(8,128)(2,1)}), bf16[32,16,128]{2,1,0:T(8,128)(2,1)S(1)}, u32[]{:S(2)}, u32[]{:S(2)}) async-start(bf16[32,16,128]{2,1,0:T(8,128)(2,1)} %get-tuple-element.54), calls=%async_computation.1 | async-start | bytes 262144 | tf_op jit(solution)/shard_map/all_to_all | solution.py:883
  27.3 2.3 %spread.1 = (bf16[1,8,64,512]{3,2,1,0:T(8,128)(2,1)}, bf16[4,64,512]{2,1,0:T(8,128)(2,1)S(1)}, bf16[128,1600]{1,0:T(8,128)(2,1)S(1)}, f32[1,16]{1,0:T(1,128)}, f32[16,16]{1,0:T(8,128)}) custom-call(bf16[5,144,256]{2,1,0:T(8,128)(2,1)S(1)} %get-tuple-element.55.refs_0_, bf16[256,128]{1,0:T(8,128)(2,1)S(1)} %get-tuple-element.56.refs_1_, ...), custom_call_target="tpu_custom_call" | custom-call | flops 4000000000 | bytes 4000000 | tf_op jit(solution)/shard_map/spread/pallas_call | solution.py:884
  29.7 0.2 collective-permute-start.2
  29.8 5.4 %all-to-all-done.1.refs_0_ = bf16[32,16,128]{2,1,0:T(8,128)(2,1)S(1)} async-done(((bf16[32,16,128]{2,1,0:T(8,128)(2,1)}), bf16[32,16,128]{2,1,0:T(8,128)(2,1)S(1)}, u32[]{:S(2)}, u32[]{:S(2)}) %all-to-all-start.1) | async-done | bytes 131104 | tf_op jit(solution)/shard_map/all_to_all | solution.py:883
  35.3 0.0 collective-permute-done.2.refs_1_
  35.3 0.9 %finish.1 = (bf16[1,8,64,512]{3,2,1,0:T(8,128)(2,1)}, f32[1,1600]{1,0:T(1,128)}, f32[1,16]{1,0:T(1,128)}, f32[1,4]{1,0:T(1,128)}) custom-call(f32[16,128]{1,0:T(8,128)S(1)} %total.1.refs_0_, bf16[4,64,512]{2,1,0:T(8,128)(2,1)S(1)} %collective-permute-done.2.refs_1_, ...), custom_call_target="tpu_custom_call", output_to_operand_aliasing={{0}: (3, {})} | custom-call | tf_op jit(solution)/shard_map/finish/pallas_call | solution.py:914
  (1 shorter events, 0.0 us)
Async XLA Ops:
  0.6 4.1 %copy-start.1 = (bf16[8,64,512]{2,1,0:T(8,128)(2,1)S(1)}, bf16[8,64,512]{2,1,0:T(8,128)(2,1)}, u32[]{:S(2)}) copy-start(bf16[8,64,512]{2,1,0:T(8,128)(2,1)} %refs_2_.3) | copy-start | bytes 1572868
  0.6 4.1 %copy-start.2 = (s32[8,64,128]{2,1,0:T(8,128)S(1)}, s32[8,64,128]{2,1,0:T(8,128)}, u32[]{:S(2)}) copy-start(s32[8,64,128]{2,1,0:T(8,128)} %refs_1_.3) | copy-start | bytes 786436
  0.7 4.1 %copy-start = (bf16[8,64,512]{2,1,0:T(8,128)(2,1)S(1)}, bf16[8,64,512]{2,1,0:T(8,128)(2,1)}, u32[]{:S(2)}) copy-start(bf16[8,64,512]{2,1,0:T(8,128)(2,1)} %refs_0_.3) | copy-start | bytes 1572868
  1.7 6.1 %collective-permute-start = (bf16[48,640]{1,0:T(8,128)(2,1)S(1)}, bf16[48,640]{1,0:T(8,128)(2,1)S(1)}, u32[]{:S(2)}, u32[]{:S(2)}) collective-permute-start(bf16[48,640]{1,0:T(8,128)(2,1)S(1)} %get-tuple-element.39), channel_id=1, source_target_pairs={{0,1},{1,0},{2,3},{3,2},{4,5},{5,4},{6,7},{7,6},{8,9},{9,8},{10,11... | collective-permute-start | bytes 184328 | tf_op jit(solution)/shard_map/ppermute | solution.py:813
  4.7 1.3 %collective-permute-start.1 = (bf16[32,1600]{1,0:T(8,128)(2,1)S(1)}, bf16[32,1600]{1,0:T(8,128)(2,1)S(1)}, u32[]{:S(2)}, u32[]{:S(2)}) collective-permute-start(bf16[32,1600]{1,0:T(8,128)(2,1)S(1)} %get-tuple-element.40.refs_0_), channel_id=1, source_target_pairs={{0,16},{16,0},{1,17},{17,1},{2,18},{18,2},{3,19},{19,3},{4,20},{20... | collective-permute-start | bytes 307208 | tf_op jit(solution)/shard_map/ppermute | solution.py:814
  9.7 12.8 %all-to-all-start = ((f32[32,4,128]{2,1,0:T(4,128)}), f32[32,4,128]{2,1,0:T(4,128)S(1)}, u32[]{:S(2)}, u32[]{:S(2)}) async-start(f32[32,4,128]{2,1,0:T(4,128)} %get-tuple-element.46), calls=%async_computation | async-start | bytes 131072 | tf_op jit(solution)/shard_map/all_to_all | solution.py:861
  24.7 10.5 %all-to-all-start.1 = ((bf16[32,16,128]{2,1,0:T(8,128)(2,1)}), bf16[32,16,128]{2,1,0:T(8,128)(2,1)S(1)}, u32[]{:S(2)}, u32[]{:S(2)}) async-start(bf16[32,16,128]{2,1,0:T(8,128)(2,1)} %get-tuple-element.54), calls=%async_computation.1 | async-start | bytes 262144 | tf_op jit(solution)/shard_map/all_to_all | solution.py:883
  29.7 5.6 %collective-permute-start.2 = (bf16[4,64,512]{2,1,0:T(8,128)(2,1)S(1)}, bf16[4,64,512]{2,1,0:T(8,128)(2,1)S(1)}, u32[]{:S(2)}, u32[]{:S(2)}) collective-permute-start(bf16[4,64,512]{2,1,0:T(8,128)(2,1)S(1)} %get-tuple-element.59), channel_id=1, source_target_pairs={{0,16},{16,0},{1,17},{17,1},{2,18},{18,2},{3,19},{19,3},{4,20},{20... | collective-permute-start | bytes 786440 | tf_op jit(solution)/shard_map/ppermute | solution.py:905

commit v4 on v3

--- a/solution.py
+++ b/solution.py
@@ -91,22 +91,6 @@
 
 def scatter_rows(z):
     return hot(iota((z.own, z.own), 0) == row_target(z, iota((1, z.own), 1)))
-
-
-def gather_halo(z, odd):
-    row = iota((2 * z.halo, 1), 0)
-    second = (row >= z.halo).astype(jnp.int32)
-    row = row - second * z.halo
-    half = z.halo // 2
-    parity = (row >= half).astype(jnp.int32)
-    q = row - parity * half
-    m = q & (z.mb - 1)
-    r = 2 * (q >> z.shift) + parity
-    near = r - odd * (HALO // 2)
-    there = (near >= 0) & (near < HALO // 2)
-    near = jnp.where(there, z.halo + m * (HALO // 2) + near, -1)
-    target = jnp.where(second == 1, near, m * HALO + r)
-    return hot(iota((2 * z.halo, z.sent), 1) == target)
 
 
 def pixel_target(lane, inner):
@@ -340,24 +324,28 @@
         copy.wait()
     kernel_out[...] = jnp.broadcast_to(kernel_buf[...].astype(F32), (COPIES, NK)).astype(BF16)
 
-    def edge_rows(buf, count):
+    def beside(buf):
         rows = buf[...].astype(F32)
-        rows = jnp.where(odd == 1, rows[:, :count], rows[:, 16 - count :])
-        return rows.reshape(z.mb * count, rows.shape[2]).astype(BF16)
-
-    out[0 : z.halo, 0 : z.span] = edge_rows(field_buf, HALO)
-    out[0 : z.halo, z.span : z.span + HW] = edge_rows(mask_buf, HALO)
-    rows = cot_buf[...].astype(F32)
-    rows = jnp.where(odd == 1, rows[:, :HALO], rows[:, 16 - HALO :])
-    rows = [
-        jnp.where(odd == 1, x[: HALO // 2], x[HALO // 2 :]) for x in (rows[m] for m in range(z.mb))
-    ]
-    out[z.halo : z.sent, 0 : z.span] = jnp.concatenate(rows, axis=0).astype(BF16)
+        return jnp.where(odd == 1, rows[:, :HALO], rows[:, HALO:])
+
+    def ordered(rows, firsts):
+        return jnp.concatenate(
+            [rows[:, j + h] for h in range(2) for j in firsts], axis=0
+        ).astype(BF16)
+
+    mask_rows = beside(mask_buf)
+    allowed = jnp.concatenate([mask_rows] * CIN, axis=2)
+    every, half = range(0, HALO, 2), range(0, HALO // 2, 2)
+    out[0 : z.halo, 0 : z.span] = ordered(beside(field_buf) * allowed, every)
+    out[0 : z.halo, z.span : z.span + HW] = ordered(mask_rows, every)
+    near = beside(cot_buf) * allowed
+    near = jnp.where(odd == 1, near[:, : HALO // 2], near[:, HALO // 2 :])
+    out[z.halo : z.sent, 0 : z.span] = ordered(near, half)
 
 
 def prepare_kernel(
-    z, fields, mask, cotangent, counts, enc_bias, dec_bias, run_mean, run_cov,
-    pixels_out, cot_out, inmask_out, mask_out, aux_out,
+    z, fields, mask, counts, enc_bias, dec_bias, run_mean, run_cov,
+    pixels_out, inmask_out, aux_out,
     count_buf, enc_buf, dec_buf, mean_buf, cov_buf, sems,
 ):
     section = lax.axis_index("section")
@@ -383,14 +371,10 @@
     mask_columns = window_mask_columns()
     pixel_mask = mask[mine_rows].astype(F32).astype(BF16).reshape(z.own, HW)
     framed_mask = dot(gather, pixel_mask).astype(BF16)
-    mask_out[...] = framed_mask
     in_mask = dot(framed_mask, mask_columns)
-    pixels = jnp.concatenate(
-        [x[mine_rows].reshape(z.own, z.span) for x in (fields, cotangent)], axis=1
+    windowed = dot(
+        dot(gather, fields[mine_rows].reshape(z.own, z.span)).astype(BF16), columns
     )
-    pixels = dot(gather, pixels).astype(BF16)
-    pixels = jnp.concatenate([pixels[:, 0 : z.span], pixels[:, z.span :]], axis=0)
-    windowed = dot(pixels, columns)
     for copy in copies:
         copy.wait()
     lane = iota((8, 128), 1)
@@ -416,8 +400,7 @@
     aux_out[40:56] = channel_ok
     in_mask = in_mask * jnp.tile(channel_ok, (z.own // 16, NB))
     inmask_out[...] = in_mask.astype(BF16)
-    pixels_out[...] = (windowed[0 : z.own] * in_mask).astype(BF16)
-    cot_out[...] = (windowed[z.own : 2 * z.own] * in_mask).astype(BF16)
+    pixels_out[...] = (windowed * in_mask).astype(BF16)
 
 
 def taps_kernel(z, kernel_own, kernel_other, weights_out):
@@ -433,21 +416,24 @@
     return jnp.concatenate([up, here, down], axis=1).astype(BF16)
 
 
-def encode_rows(taps, weights, bias, masks, mine):
+def encode_rows(taps, banded, bias, masks, mine):
     code_mask = dot(masks, code_mask_lanes())
-    pre = dot(taps, band_weights(weights)) + bias
+    pre = dot(taps, banded) + bias
     slope = jnp.exp(jnp.minimum(pre, 0.0))
     code = jnp.where(pre > 0, pre, slope - 1.0).astype(BF16).astype(F32)
     slope = jnp.where(code_mask > 0.5, slope, -slope)
     allowed = code_mask if mine is None else jnp.where(mine, code_mask, 0.0)
     weighted = code * allowed
-    second = dot(weighted.astype(BF16), code.astype(BF16), ((0,), (0,)))
+    halves = [
+        jnp.concatenate([x[:, 0:128], x[:, 128:256]], axis=0).astype(BF16) for x in (weighted, code)
+    ]
+    second = dot(*halves, ((0,), (0,)))
     sums = [jnp.sum(x, axis=0, keepdims=True) for x in (weighted, allowed)]
-    lane_u = iota((16, 256), 1) >> 4
-    total = jnp.zeros((16, 256), F32)
-    for u in range(1, UW - 1):
+    lane_u = iota((16, 128), 1) >> 4
+    total = second[0:16]
+    for u in range(1, UW // 2):
         total = jnp.where(lane_u == u, second[u * 16 : u * 16 + 16], total)
-    total = fold(total[:, :128] + total[:, 128:], 16)
+    total = fold(total, 16)
     diagonal = (iota((8, 128), 1) >> 4) == iota((8, 128), 0)
     pay = [
         jnp.sum(jnp.where(diagonal, total[h * 8 : h * 8 + 8], 0.0), axis=0, keepdims=True)
@@ -458,16 +444,16 @@
     return code, slope, jnp.concatenate(pay, axis=0)
 
 
-def put_codes(code, slope, count, start, code_out, slope_out):
-    blocks = [code[b * count : b * count + count] for b in range(NB)]
+def put_codes(blocks, count, start, code_out):
     rows = pl.ds(start, count)
     for b, (low, high) in enumerate(mend_coarse(blocks)):
         code_out[b, rows, 0:128] = low.astype(BF16)
         code_out[b, rows, 128:256] = high.astype(BF16)
-        slope_out[b, rows, :] = slope[b * count : b * count + count]
-
-
-def inner_kernel(z, pixels, own_mask, weights, aux, taps_out, code_out, slope_out, pay_out, sh):
+
+
+def inner_kernel(
+    z, pixels, own_mask, weights, aux, taps_out, code_out, slope_out, pay_out, band_out, sh
+):
     odd = lax.rem(lax.axis_index("wide"), 2)
     half = z.own // 2
     count = half - 16
@@ -487,27 +473,28 @@
     kept = pl.ds(pl.multiple_of(odd * 16, 16), count)
     masks = jnp.concatenate([own_mask[kept, b * 128 : b * 128 + 128] for b in range(NB)], axis=0)
     bias = jnp.concatenate([aux[8:9], aux[8:9]], axis=1)
-    code, slope, pay = encode_rows(
-        jnp.concatenate(taps, axis=0), weights[:, 0:256], bias, masks, None
-    )
+    banded = band_weights(weights[:, 0:256])
+    band_out[...] = banded
+    code, slope, pay = encode_rows(jnp.concatenate(taps, axis=0), banded, bias, masks, None)
     pay_out[...] = pay
-    put_codes(code, slope, count, start, code_out, slope_out)
+    for b in range(NB):
+        rs = slice(b * count, b * count + count)
+        code_out[b, pl.ds(start, count), :] = code[rs].astype(BF16)
+        slope_out[b, pl.ds(start, count), :] = slope[rs]
 
 
 def encode_kernel(
-    z, pixels, own_mask, halo, weights, aux, inner_pay, taps_in, code_in, slope_in,
+    z, pixels, own_mask, halo, banded, aux, inner_pay, taps_in, code_in, slope_in,
     taps_out, code_out, slope_out, cot_out, pay_out,
     sh, pays, sem,
 ):
     odd = lax.rem(lax.axis_index("wide"), 2)
     half = z.own // 2
     count = 32
-    gather = gather_halo(z, odd)
-    framed_mask = dot(gather[0 : z.halo], halo[:, z.span : z.span + HW]).astype(BF16)
-    channel_ok = jnp.tile(aux[40:56], (z.halo // 16, NB))
-    halo_mask = dot(framed_mask, window_mask_columns()) * channel_ok
-    halo_pixels = dot(dot(gather, halo[:, 0 : z.span]).astype(BF16), window_columns())
-    halo_x = halo_pixels[0 : z.halo] * halo_mask
+    channel_ok = jnp.tile(aux[40:56], (1, NB))
+    halo_mask = dot(halo[0:16, z.span : z.span + HW], window_mask_columns())
+    halo_pixels = dot(halo[:, 0 : z.span], window_columns())
+    halo_x = halo_pixels[0 : z.halo] * jnp.tile(channel_ok, (2, 1))
     zeros = jnp.zeros((NB, 16, 256), F32)
     sh[:, 0:16, :] = zeros
     sh[:, 48:64, :] = zeros
@@ -525,39 +512,54 @@
     for b in range(NB):
         taps_out[b, pl.ds(start, count), :] = taps[b]
     edge_mask = own_mask[pl.ds(pl.multiple_of((1 - odd) * (half - 16), 16), 16), :].astype(F32)
-    first = jnp.where(odd == 1, halo_mask[0:16], edge_mask)
-    later = jnp.where(odd == 1, edge_mask, halo_mask[0:16])
+    first = jnp.where(odd == 1, halo_mask, edge_mask)
+    later = jnp.where(odd == 1, edge_mask, halo_mask)
     masks = jnp.concatenate(
         [x[:, b * 128 : b * 128 + 128] for b in range(NB) for x in (first, later)], axis=0
     ).astype(BF16)
     bias = jnp.concatenate([aux[8:9], aux[8:9]], axis=1)
     mine = ((iota((NB * count, 1), 0) >> 4) & 1) == odd
-    code, slope, pay = encode_rows(
-        jnp.concatenate(taps, axis=0), weights[:, 0:256], bias, masks, mine
-    )
+    code, slope, pay = encode_rows(jnp.concatenate(taps, axis=0), banded[...], bias, masks, mine)
     pay = pay + inner_pay[...]
     for i in range(pays.shape[0]):
         pays[i] = pay
     copy = pltpu.make_async_copy(pays, pay_out, sem.at[0])
     copy.start()
-    put_codes(code, slope, count, start, code_out, slope_out)
-    cot_out[...] = (halo_pixels[z.halo : 2 * z.halo] * halo_mask).astype(BF16)
+    for b in range(NB):
+        slope_out[b, pl.ds(start, count), :] = slope[b * count : b * count + count]
+    put_codes([code[b * count : b * count + count] for b in range(NB)], count, start, code_out)
+    inner = z.rows - count
+    inner_start = pl.multiple_of(odd * count, 16)
+    put_codes(
+        [code_in[b, pl.ds(inner_start, inner), :].astype(F32) for b in range(NB)],
+        inner, inner_start, code_out,
+    )
+    near = halo_pixels[z.halo : z.sent] * channel_ok
+    nothing = jnp.zeros((8, NB * 128), F32)
+    for h in range(2):
+        rows = near[h * 8 : h * 8 + 8]
+        rows = [jnp.where(odd == 1, nothing, rows), jnp.where(odd == 1, rows, nothing)]
+        cot_out[h * 16 : h * 16 + 16, :] = jnp.concatenate(rows, axis=0).astype(BF16)
     copy.wait()
 
 
 def decode_kernel(
-    z, code, own_cot, halo_cot, weights, aux,
-    recon_out, sent_out, pay_out,
+    z, cotangent, code, in_mask, halo_cot, weights, aux,
+    sent_out, pay_out,
     sh, cot_frame,
 ):
     odd = lax.rem(lax.axis_index("wide"), 2)
+    mine = pl.ds(lax.axis_index("section") * z.mb, z.mb)
     rows = z.rows
     put_frame(
         z, sh, [(code[b, :, 0:128].astype(F32), code[b, :, 128:256].astype(F32)) for b in range(NB)]
     )
     banded = band_weights(weights[:, 256:512])
     raws = spread(z, sh, banded)
-    put_pixels(z, cot_frame, odd, own_cot[...].astype(F32), halo_cot[...].astype(F32))
+    gather = gather_rows(z)
+    columns = window_columns()
+    own_cot = dot(dot(gather, cotangent[mine].reshape(z.own, z.span)).astype(BF16), columns)
+    put_pixels(z, cot_frame, odd, own_cot * in_mask[...].astype(F32), halo_cot[...].astype(F32))
     mine_rows = own_rows(z, odd)
     u_local = (iota((1, 128), 1) >> 3) & (UW - 1)
     inner = mine_rows & (u_local >= 1) & (u_local <= UW - 2)
@@ -566,15 +568,12 @@
     for h in range(2):
         raw = raws[h] + aux[0:1]
         slope = jnp.exp(jnp.minimum(raw, 0.0))
-        recon = jnp.where(raw > 0, raw, slope - 1.0)
         cs = slice(h * 128, h * 128 + 128)
         for b in range(NB):
             rs = slice(b * rows, b * rows + rows)
-            sh[b, 8 : 8 + rows, cs] = recon[rs]
             grad = (cot_frame[b, 8 : 8 + rows, cs] * slope[rs]).astype(BF16).astype(F32)
             bias_sum = bias_sum + jnp.sum(jnp.where(inner, grad, 0.0), axis=0, keepdims=True)
             grads.append(grad)
-    recon_out[...] = own_frame(z, odd, sh)
     put_frame(z, sh, mend_fine([(grads[b], grads[NB + b]) for b in range(NB)]))
     taps = jnp.concatenate([fine_taps(z, sh, b) for b in range(NB)], axis=0)
     sent_out[...] = dot(taps, banded).astype(BF16).reshape(NB, rows, 256)
@@ -618,14 +617,16 @@
     pulled = jnp.sum(offset * mean_column, axis=0, keepdims=True)
     linear = whiten_weight * mean - 2.0 * whiten_weight * pulled
     linear = jnp.concatenate([linear, linear], axis=1)
-    offset = 2.0 * whiten_weight * jnp.concatenate([offset, offset], axis=1)
-    same = (iota((256, 256), 0) >> 4) == (iota((256, 256), 1) >> 4)
-    matrix = jnp.broadcast_to(offset[None], (16, 16, 256)).reshape(256, 256)
-    high, mid, _ = split(jnp.where(same, matrix, 0.0))
+    matrix = jnp.tile(2.0 * whiten_weight * offset, (8, 1))
+    matrix = jnp.where((iota((128, 128), 0) >> 4) == (iota((128, 128), 1) >> 4), matrix, 0.0)
+    high = matrix.astype(BF16)
+    matrix = jnp.concatenate([high, (matrix - high.astype(F32)).astype(BF16)], axis=0)
     flat = code[...].reshape(z.frame, 256)
-    turned = dot(
-        jnp.concatenate([flat, flat], axis=1), jnp.concatenate([high, mid], axis=0)
-    ) + linear
+    flat = jnp.concatenate(
+        [jnp.concatenate([x, x], axis=1) for x in (flat[:, 0:128], flat[:, 128:256])], axis=0
+    )
+    turned = dot(flat, matrix)
+    turned = jnp.concatenate([turned[0 : z.frame], turned[z.frame :]], axis=1) + linear
     mine_rows = own_rows(z, odd)
     lane_u = iota((1, 256), 1) >> 4
     inner = mine_rows & (lane_u >= 1) & (lane_u <= UW - 2)
@@ -664,33 +665,40 @@
     copy.wait()
 
 
-def spread_kernel(
-    z, grad, mask, weights, recon, aux, moments,
-    pixels_out, send_out, onehot_out, mean_out, cov_out,
+def picture(z, decodes, grad, code, in_mask, weights, aux, sh):
+    odd = lax.rem(lax.axis_index("wide"), 2)
+    rows = z.rows
+    frames = [
+        jnp.where(decodes, code[b].astype(F32), grad[b].astype(F32)) for b in range(NB)
+    ]
+    put_frame(z, sh, [(x[:, 0:128], x[:, 128:256]) for x in frames])
+    chosen = jnp.where(decodes, weights[:, 256:512].astype(F32), weights[:, 0:256].astype(F32))
+    raws = spread(z, sh, band_weights(chosen))
+    for h in range(2):
+        raw = raws[h] + aux[0:1]
+        raw = jnp.where(raw > 0, raw, jnp.exp(jnp.minimum(raw, 0.0)) - 1.0)
+        raw = jnp.where(decodes, raw, raws[h])
+        for b in range(NB):
+            sh[b, 8 : 8 + rows, h * 128 : h * 128 + 128] = raw[b * rows : b * rows + rows]
+    flat = own_frame(z, odd, sh) * in_mask[...]
+    native = dot(flat, unwindow_columns()).astype(BF16)
+    return dot(scatter_rows(z), native).astype(BF16).reshape(z.mb, z.band, z.span)
+
+
+def send_kernel(z, grad, code, in_mask, weights, aux, send_out, sh):
+    decodes = lax.axis_index("section") == 0
+    send_out[...] = picture(z, decodes, grad, code, in_mask, weights, aux, sh)
+
+
+def keep_kernel(
+    z, grad, code, in_mask, weights, aux, moments,
+    pixels_out, onehot_out, mean_out, cov_out,
     sh, mine, means, covs, sems,
 ):
     section = lax.axis_index("section")
-    odd = lax.rem(lax.axis_index("wide"), 2)
-    rows = z.rows
-    put_frame(
-        z, sh, [(grad[b, :, 0:128].astype(F32), grad[b, :, 128:256].astype(F32)) for b in range(NB)]
-    )
-    raws = spread(z, sh, band_weights(weights[:, 0:256]))
-    for h in range(2):
-        for b in range(NB):
-            sh[b, 8 : 8 + rows, h * 128 : h * 128 + 128] = raws[h][b * rows : b * rows + rows]
-    in_mask = dot(mask[...], window_mask_columns()) * jnp.tile(aux[40:56], (z.own // 16, NB))
-    in_mask = in_mask.astype(BF16)
-    flat = own_frame(z, odd, sh) * in_mask
-    other = recon[...] * in_mask
-    leads = section == 0
-    flat, other = jnp.where(leads, flat, other), jnp.where(leads, other, flat)
-    native = dot(jnp.concatenate([flat, other], axis=0), unwindow_columns()).astype(BF16)
-    scatter = scatter_rows(z)
-    whole = (z.mb, z.band, z.span)
-    mine[...] = dot(scatter, native[0 : z.own]).astype(BF16).reshape(whole)
     means[...] = decay_rate * aux[16:17, 0:CCODE] + (1.0 - decay_rate) * moments[16:17, 0:CCODE]
     covs[...] = decay_rate * aux[24:40, 0:CCODE] + (1.0 - decay_rate) * moments[0:16, 0:CCODE]
+    mine[...] = picture(z, section == 1, grad, code, in_mask, weights, aux, sh)
     copies = [
         pltpu.make_async_copy(source, target, sems.at[i])
         for i, (source, target) in enumerate(
@@ -703,7 +711,6 @@
     ]
     for copy in copies:
         copy.start()
-    send_out[...] = dot(scatter, native[z.own : 2 * z.own]).astype(BF16).reshape(whole)
     onehot_out[...] = tap_onehot()
     for copy in copies:
         copy.wait()
@@ -812,17 +819,15 @@
         )(fields, pixel_mask, cotangent, kernels)
         halo = lax.ppermute(halo, "wide", pair)
         kernel_other = lax.ppermute(kernel_own, "section", swap)
-        pixels, own_cot, in_mask, mask, aux = call(
+        pixels, in_mask, aux = call(
             prepare_kernel,
             "prepare",
             [
                 shape(z.own, NB * 128),
                 shape(z.own, NB * 128),
-                shape(z.own, NB * 128),
-                shape(z.own, HW),
                 shape(56, 128, dtype=F32),
             ],
-            [VMEM] * 3 + [HBM] * 5,
+            [VMEM] * 2 + [HBM] * 5,
             [
                 pltpu.SMEM(channel_counts.shape, jnp.int32),
                 pltpu.SMEM(enc_bias.shape, F32),
@@ -832,15 +837,15 @@
                 DMA((5,)),
             ],
             cost=heavy,
-        )(*whole, channel_counts, enc_bias, dec_bias, run_mean, run_cov)
+        )(*whole[:2], channel_counts, enc_bias, dec_bias, run_mean, run_cov)
         (weights,) = call(taps_kernel, "taps", [shape(128, 512)], [VMEM] * 2, [])(
             kernel_own, kernel_other
         )
         coded = [shape(NB, z.rows, KS * 128), shape(*frame), shape(*frame, dtype=F32)]
-        taps, code, slope, pay = call(
+        taps, code, slope, pay, banded = call(
             inner_kernel,
             "inner",
-            coded + [shape(4, 128, dtype=F32)],
+            coded + [shape(4, 128, dtype=F32), shape(KS * 128, 256)],
             [VMEM] * 4,
             [pltpu.VMEM((NB, z.own // 2 + 16, 256), F32)],
             cost=heavy,
@@ -857,16 +862,16 @@
             ],
             out_specs=[VMEM] * 4 + [HBM],
             alias={6: 0, 7: 1, 8: 2},
-        )(pixels, in_mask, halo, weights, aux, pay, taps, code, slope)
+        )(pixels, in_mask, halo, banded, aux, pay, taps, code, slope)
         stats = lax.all_to_all(pay, ("section", "wide"), 0, 0)
-        recon, sent, decode_pay = call(
+        sent, decode_pay = call(
             decode_kernel,
             "decode",
-            [shape(z.own, NB * 128), shape(*frame), shape(CCODE, 128, dtype=F32)],
-            [VMEM] * 5,
+            [shape(*frame), shape(CCODE, 128, dtype=F32)],
+            [VMEM] * 6,
             [framed, framed],
             cost=heavy,
-        )(code, own_cot, halo_cot, weights, aux)
+        )(whole[2], code, in_mask, halo_cot, weights, aux)
         grad, pay, moments = call(
             whiten_kernel,
             "whiten",
@@ -881,12 +886,20 @@
             alias={3: 0},
         )(stats, code, slope, sent, taps, decode_pay, aux)
         parts = lax.all_to_all(pay, ("section", "wide"), 0, 0)
-        half_done, sending, onehot, new_mean, new_cov = call(
-            spread_kernel,
-            "spread",
+        (sending,) = call(
+            send_kernel,
+            "send",
+            [shape(z.mb, z.band, z.span)],
+            [VMEM] * 5,
+            [framed],
+            cost=heavy,
+        )(grad, code, in_mask, weights, aux)
+        arrived = lax.ppermute(sending, "section", swap)
+        half_done, onehot, new_mean, new_cov = call(
+            keep_kernel,
+            "keep",
             [
                 shape(1, z.micro, z.band, z.span),
-                shape(z.mb, z.band, z.span),
                 shape(128, NK),
                 shape(1, CCODE, dtype=F32),
                 shape(CCODE, CCODE, dtype=F32),
@@ -899,10 +912,9 @@
                 pltpu.VMEM((CCODE, CCODE), F32),
                 DMA((3,)),
             ],
-            out_specs=[HBM, VMEM, VMEM, HBM, HBM],
+            out_specs=[HBM, VMEM, HBM, HBM],
             cost=heavy,
-        )(grad, mask, weights, recon, aux, moments)
-        arrived = lax.ppermute(sending, "section", swap)
+        )(grad, code, in_mask, weights, aux, moments)
         (sums,) = call(
             total_kernel,
             "total",

time: 36.5 us -> 36 us (0.986)
  waiting for transfers between devices: 10.8 us -> 9.28 us
  Pallas kernels: 13.3 us -> 14.4 us
    pallas_call x3 -> x4, Pallas kernels: 5.52 us -> 7.32 us  [the longest x1 2.42 us: run(): call(keep_kernel, 'keep', [shape(1, z.micro, z.band, z.span), shape(128,...]
    all_to_all x1, waiting for transfers between devices: 5.41 us -> 3.75 us  [run(): parts = lax.all_to_all(pay, ('section', 'wide'), 0, 0)]
where the time goes in v4:
time: 36 us; the launch traced here: 35.7 us
  Pallas kernels  14.4 us (40%)
  starting transfers between devices  11.2 us (31%)
  waiting for transfers between devices  9.28 us (26%)
  between operations  0.77 us (2%)
    all_to_all x1, starting transfers between devices, run(): stats = lax.all_to_all(pay, ('section', 'wide'), 0, 0)  5.45 us
    all_to_all x1, waiting for transfers between devices, run(): stats = lax.all_to_all(pay, ('section', 'wide'), 0, 0)  5.21 us
    all_to_all x1, waiting for transfers between devices, run(): parts = lax.all_to_all(pay, ('section', 'wide'), 0, 0)  3.75 us
    ppermute x1, starting transfers between devices, run(): halo = lax.ppermute(halo, 'wide', pair)  3 us
    all_to_all x1, starting transfers between devices, run(): parts = lax.all_to_all(pay, ('section', 'wide'), 0, 0)  2.59 us
    pallas_call x1, Pallas kernels, run(): call(keep_kernel, 'keep', [shape(1, z.micro, z.band, z.span), shape(128,...  2.42 us
    pallas_call x1, Pallas kernels, run(): call(decode_kernel, 'decode', [shape(*frame), shape(CCODE, 128, dtype=F32...  2.09 us
    pallas_call x1, Pallas kernels, run(): call(whiten_kernel, 'whiten', [shape(*frame), shape(sections * wides, CCO...  2.04 us
  transfers between devices with their start and end apart: 5, of which 3 were waited for; matrix products, arithmetic and copies ran while one was open for 0% of the time, Pallas kernels for 20%

profile of v4, /device:TPU:0, one launch (start us, length us, event | category | flops | bytes accessed | tf_op | source)
XLA Modules:
  0.0 35.7 jit_solution(5187413303673687219)
XLA Ops:
  0.6 0.0 copy-start.2
  0.6 0.0 copy-start
  0.7 1.1 %edge.1 = (bf16[48,640]{1,0:T(8,128)(2,1)S(1)}, bf16[32,1600]{1,0:T(8,128)(2,1)S(1)}) custom-call(bf16[8,64,512]{2,1,0:T(8,128)(2,1)} %refs_0_.4, s32[8,64,128]{2,1,0:T(8,128)} %refs_1_.3, bf16[8,64,512]{2,1,0:T(8,128)(2,1)} %refs_0_.5, bf16[1,1600]{1,0:T(2,128)(2,1)} %refs_3_.3), custom_call_target="tpu_custom_call" | custom-call | tf_op jit(solution)/shard_map/edge/pallas_call | solution.py:807
  1.8 3.0 %collective-permute-start = (bf16[48,640]{1,0:T(8,128)(2,1)S(1)}, bf16[48,640]{1,0:T(8,128)(2,1)S(1)}, u32[]{:S(2)}, u32[]{:S(2)}) collective-permute-start(bf16[48,640]{1,0:T(8,128)(2,1)S(1)} %get-tuple-element.36), channel_id=1, source_target_pairs={{0,1},{1,0},{2,3},{3,2},{4,5},{5,4},{6,7},{7,6},{8,9},{9,8},{10,11... | collective-permute-start | bytes 184328 | tf_op jit(solution)/shard_map/ppermute | solution.py:820
  4.8 0.0 collective-permute-start.1
  4.8 0.0 copy-done.2
  4.8 0.0 copy-done
  4.8 1.0 %prepare.1 = (bf16[256,640]{1,0:T(8,128)(2,1)S(1)}, bf16[256,640]{1,0:T(8,128)(2,1)S(1)}, f32[56,128]{1,0:T(8,128)S(1)}) custom-call(bf16[8,64,512]{2,1,0:T(8,128)(2,1)S(1)} %copy-done, s32[8,64,128]{2,1,0:T(8,128)S(1)} %copy-done.2, s32[8,8]{1,0:T(8,128)} %refs_2_.2, f32[16]{0:T(128)} %refs_3_.2, f32[4]{0:T(128)} %refs_4_.1, f32[16]{0:T(128)} %refs_5_.1, ...), custom_call_target="tpu_custom_call" | custom-call | flops 4000000000 | bytes 4000000 | tf_op jit(solution)/shard_map/prepare/pallas_call | solution.py:822
  5.8 0.3 collective-permute-done.1.refs_1_
  6.1 0.5 %taps.1.refs_2_.refs_4_.refs_3_ = bf16[128,512]{1,0:T(8,128)(2,1)S(1)} custom-call(bf16[32,1600]{1,0:T(8,128)(2,1)S(1)} %get-tuple-element.37.refs_0_, bf16[32,1600]{1,0:T(8,128)(2,1)S(1)} %collective-permute-done.1.refs_1_), custom_call_target="tpu_custom_call" | custom-call | tf_op jit(solution)/shard_map/taps/pallas_call | solution.py:841
  6.6 1.3 %inner.1 = (bf16[5,144,640]{2,1,0:T(8,128)(2,1)S(1)}, bf16[5,144,256]{2,1,0:T(8,128)(2,1)S(1)}, f32[5,144,256]{2,1,0:T(8,128)S(1)}, f32[4,128]{1,0:T(4,128)S(1)}, bf16[640,256]{1,0:T(8,128)(2,1)S(1)}) custom-call(bf16[256,640]{1,0:T(8,128)(2,1)S(1)} %get-tuple-element.34.refs_0_, bf16[256,640]{1,0:T(8,128)(2,1)S(1)} %get-tuple-element.35.refs_1_.refs_2_, ...), custom_call_target="tpu_custom_call" | custom-call | flops 4000000000 | bytes 4000000 | tf_op jit(solution)/shard_map/inner/pallas_call | solution.py:845
  7.9 0.0 collective-permute-done.refs_2_
  7.9 0.0 copy-start.1
  7.9 1.6 %encode.1 = (bf16[5,144,640]{2,1,0:T(8,128)(2,1)S(1)}, bf16[5,144,256]{2,1,0:T(8,128)(2,1)S(1)}, f32[5,144,256]{2,1,0:T(8,128)S(1)}, bf16[32,640]{1,0:T(8,128)(2,1)S(1)}, f32[32,4,128]{2,1,0:T(4,128)}) custom-call(bf16[256,640]{1,0:T(8,128)(2,1)S(1)} %get-tuple-element.34.refs_0_, ...), custom_call_target="tpu_custom_call", output_to_operand_aliasing={{0}: (6, {}), {1}: (7, {}), {2}: (8, {})} | custom-call | tf_op jit(solution)/shard_map/encode/pallas_call | solution.py:853
  9.5 5.5 %all-to-all-start = ((f32[32,4,128]{2,1,0:T(4,128)}), f32[32,4,128]{2,1,0:T(4,128)S(1)}, u32[]{:S(2)}, u32[]{:S(2)}) async-start(f32[32,4,128]{2,1,0:T(4,128)} %get-tuple-element.44), calls=%async_computation | async-start | bytes 131072 | tf_op jit(solution)/shard_map/all_to_all | solution.py:866
  14.9 0.0 copy-done.1
  14.9 2.1 %decode.1 = (bf16[5,144,256]{2,1,0:T(8,128)(2,1)S(1)}, f32[16,128]{1,0:T(8,128)S(1)}) custom-call(bf16[8,64,512]{2,1,0:T(8,128)(2,1)S(1)} %copy-done.1, bf16[5,144,256]{2,1,0:T(8,128)(2,1)S(1)} %get-tuple-element.45.refs_1_, bf16[256,640]{1,0:T(8,128)(2,1)S(1)} %get-tuple-element.35.refs_1_.refs_2_, bf16[32,640]{1,0:T(8,128)(2,1)S(1)} %get-tuple-element.47.refs_3_, ...), custom_call_target="tpu_custom_call" | custom-call | flops 4000000000 | bytes 4000000 | tf_op jit(solution)/shard_map/decode/pallas_call | solution.py:867
  17.0 5.2 %all-to-all-done.refs_0_ = f32[32,4,128]{2,1,0:T(4,128)S(1)} async-done(((f32[32,4,128]{2,1,0:T(4,128)}), f32[32,4,128]{2,1,0:T(4,128)S(1)}, u32[]{:S(2)}, u32[]{:S(2)}) %all-to-all-start) | async-done | bytes 65568 | tf_op jit(solution)/shard_map/all_to_all | solution.py:866
  22.2 2.0 %whiten.1 = (bf16[5,144,256]{2,1,0:T(8,128)(2,1)S(1)}, bf16[32,16,128]{2,1,0:T(8,128)(2,1)}, f32[24,128]{1,0:T(8,128)S(1)}) custom-call(f32[32,4,128]{2,1,0:T(4,128)S(1)} %all-to-all-done.refs_0_, bf16[5,144,256]{2,1,0:T(8,128)(2,1)S(1)} %get-tuple-element.45.refs_1_, f32[5,144,256]{2,1,0:T(8,128)S(1)} %get-tuple-element.46.refs_2_, ...), custom_call_target="tpu_custom_call", output_to_operand_aliasing={{0}: (3, {})} | custom-call | tf_op jit(solution)/shard_map/whiten/pallas_call | solution.py:875
  24.3 2.6 %all-to-all-start.1 = ((bf16[32,16,128]{2,1,0:T(8,128)(2,1)}), bf16[32,16,128]{2,1,0:T(8,128)(2,1)S(1)}, u32[]{:S(2)}, u32[]{:S(2)}) async-start(bf16[32,16,128]{2,1,0:T(8,128)(2,1)} %get-tuple-element.51), calls=%async_computation.1 | async-start | bytes 262144 | tf_op jit(solution)/shard_map/all_to_all | solution.py:888
  26.9 1.5 %send.1 = bf16[4,64,512]{2,1,0:T(8,128)(2,1)S(1)} custom-call(bf16[5,144,256]{2,1,0:T(8,128)(2,1)S(1)} %get-tuple-element.52.refs_0_, bf16[5,144,256]{2,1,0:T(8,128)(2,1)S(1)} %get-tuple-element.45.refs_1_, bf16[256,640]{1,0:T(8,128)(2,1)S(1)} %get-tuple-element.35.refs_1_.refs_2_, bf16[128,512]{1,0:T(8,128)(2,1)S(1)} %taps.1.refs_2_.refs_4_.refs_3_, ...), custom_call_target="tpu_custom_call" | custom-call | flops 4000000000 | bytes 4000000 | tf_op jit(solution)/shard_map/send/pallas_call | solution.py:889
  28.4 0.2 collective-permute-start.2
  28.6 2.4 %keep.1 = (bf16[1,8,64,512]{3,2,1,0:T(8,128)(2,1)}, bf16[128,1600]{1,0:T(8,128)(2,1)S(1)}, f32[1,16]{1,0:T(1,128)}, f32[16,16]{1,0:T(8,128)}) custom-call(bf16[5,144,256]{2,1,0:T(8,128)(2,1)S(1)} %get-tuple-element.52.refs_0_, bf16[5,144,256]{2,1,0:T(8,128)(2,1)S(1)} %get-tuple-element.45.refs_1_, bf16[256,640]{1,0:T(8,128)(2,1)S(1)} %get-tuple-element.35.refs_1_.refs_2_, ...), custom_call_target="tpu_custom_call" | custom-call | flops 4000000000 | bytes 4000000 | tf_op jit(solution)/shard_map/keep/pallas_call | solution.py:898
  31.0 3.8 %all-to-all-done.1.refs_0_ = bf16[32,16,128]{2,1,0:T(8,128)(2,1)S(1)} async-done(((bf16[32,16,128]{2,1,0:T(8,128)(2,1)}), bf16[32,16,128]{2,1,0:T(8,128)(2,1)S(1)}, u32[]{:S(2)}, u32[]{:S(2)}) %all-to-all-start.1) | async-done | bytes 131104 | tf_op jit(solution)/shard_map/all_to_all | solution.py:888
  34.8 0.0 collective-permute-done.2.refs_1_
  34.8 0.9 %finish.1 = (bf16[1,8,64,512]{3,2,1,0:T(8,128)(2,1)}, f32[1,1600]{1,0:T(1,128)}, f32[1,16]{1,0:T(1,128)}, f32[1,4]{1,0:T(1,128)}) custom-call(f32[16,128]{1,0:T(8,128)S(1)} %total.1.refs_0_, bf16[4,64,512]{2,1,0:T(8,128)(2,1)S(1)} %collective-permute-done.2.refs_1_, ...), custom_call_target="tpu_custom_call", output_to_operand_aliasing={{0}: (3, {})} | custom-call | tf_op jit(solution)/shard_map/finish/pallas_call | solution.py:926
  (1 shorter events, 0.0 us)
Async XLA Ops:
  0.6 4.1 %copy-start.2 = (s32[8,64,128]{2,1,0:T(8,128)S(1)}, s32[8,64,128]{2,1,0:T(8,128)}, u32[]{:S(2)}) copy-start(s32[8,64,128]{2,1,0:T(8,128)} %refs_1_.3) | copy-start | bytes 786436
  0.6 4.1 %copy-start = (bf16[8,64,512]{2,1,0:T(8,128)(2,1)S(1)}, bf16[8,64,512]{2,1,0:T(8,128)(2,1)}, u32[]{:S(2)}) copy-start(bf16[8,64,512]{2,1,0:T(8,128)(2,1)} %refs_0_.4) | copy-start | bytes 1572868
  1.8 6.1 %collective-permute-start = (bf16[48,640]{1,0:T(8,128)(2,1)S(1)}, bf16[48,640]{1,0:T(8,128)(2,1)S(1)}, u32[]{:S(2)}, u32[]{:S(2)}) collective-permute-start(bf16[48,640]{1,0:T(8,128)(2,1)S(1)} %get-tuple-element.36), channel_id=1, source_target_pairs={{0,1},{1,0},{2,3},{3,2},{4,5},{5,4},{6,7},{7,6},{8,9},{9,8},{10,11... | collective-permute-start | bytes 184328 | tf_op jit(solution)/shard_map/ppermute | solution.py:820
  4.8 1.3 %collective-permute-start.1 = (bf16[32,1600]{1,0:T(8,128)(2,1)S(1)}, bf16[32,1600]{1,0:T(8,128)(2,1)S(1)}, u32[]{:S(2)}, u32[]{:S(2)}) collective-permute-start(bf16[32,1600]{1,0:T(8,128)(2,1)S(1)} %get-tuple-element.37.refs_0_), channel_id=1, source_target_pairs={{0,16},{16,0},{1,17},{17,1},{2,18},{18,2},{3,19},{19,3},{4,20},{20... | collective-permute-start | bytes 307208 | tf_op jit(solution)/shard_map/ppermute | solution.py:821
  7.9 7.1 %copy-start.1 = (bf16[8,64,512]{2,1,0:T(8,128)(2,1)S(1)}, bf16[8,64,512]{2,1,0:T(8,128)(2,1)}, u32[]{:S(2)}) copy-start(bf16[8,64,512]{2,1,0:T(8,128)(2,1)} %refs_0_.5) | copy-start | bytes 1572868
  9.5 12.8 %all-to-all-start = ((f32[32,4,128]{2,1,0:T(4,128)}), f32[32,4,128]{2,1,0:T(4,128)S(1)}, u32[]{:S(2)}, u32[]{:S(2)}) async-start(f32[32,4,128]{2,1,0:T(4,128)} %get-tuple-element.44), calls=%async_computation | async-start | bytes 131072 | tf_op jit(solution)/shard_map/all_to_all | solution.py:866
  24.3 10.5 %all-to-all-start.1 = ((bf16[32,16,128]{2,1,0:T(8,128)(2,1)}), bf16[32,16,128]{2,1,0:T(8,128)(2,1)S(1)}, u32[]{:S(2)}, u32[]{:S(2)}) async-start(bf16[32,16,128]{2,1,0:T(8,128)(2,1)} %get-tuple-element.51), calls=%async_computation.1 | async-start | bytes 262144 | tf_op jit(solution)/shard_map/all_to_all | solution.py:888
  28.4 6.4 %collective-permute-start.2 = (bf16[4,64,512]{2,1,0:T(8,128)(2,1)S(1)}, bf16[4,64,512]{2,1,0:T(8,128)(2,1)S(1)}, u32[]{:S(2)}, u32[]{:S(2)}) collective-permute-start(bf16[4,64,512]{2,1,0:T(8,128)(2,1)S(1)} %send.1), channel_id=1, source_target_pairs={{0,16},{16,0},{1,17},{17,1},{2,18},{18,2},{3,19},{19,3},{4,20},{20... | collective-permute-start | bytes 786440 | tf_op jit(solution)/shard_map/ppermute | solution.py:897

commit v5 on v4

--- a/solution.py
+++ b/solution.py
@@ -60,7 +60,8 @@
         self.halo = self.mb * HALO
         self.shift = self.mb.bit_length() - 1
         self.frame = NB * self.rows
-        self.sent = self.halo + self.halo // 2
+        self.near = self.halo // 2
+        self.sent = CIN * (self.halo + self.near) + self.near
 
 
 def tap_target(n):
@@ -273,15 +274,36 @@
     return flat.astype(BF16)
 
 
+def kernel_rows(flat):
+    taps = CIN * KS * KS
+    pad = jnp.zeros((1, 256 - NK % 128), F32)
+    flat = jnp.concatenate([flat, pad], axis=1)
+    lane = iota((1, 128), 1)
+    row = iota((CCODE, 128), 0)
+    rows = jnp.zeros((CCODE, 128), F32)
+    for o in range(CCODE):
+        chunk, shift = divmod(o * taps, 128)
+        x = flat[:, chunk * 128 : chunk * 128 + 128]
+        if shift:
+            after = flat[:, chunk * 128 + 128 : chunk * 128 + 256]
+            x = jnp.where(
+                lane < 128 - shift,
+                pltpu.roll(x, 128 - shift, 1),
+                pltpu.roll(after, 128 - shift, 1),
+            )
+        rows = jnp.where(row == o, jnp.broadcast_to(x, (CCODE, 128)), rows)
+    return rows
+
+
 def spread_taps(kernel_pair):
-    row = iota((2 * CCODE, NK), 0)
-    _, o = tap_target(iota((1, NK), 1))
-    values = jnp.where(row < CCODE, kernel_pair[0], kernel_pair[1])
-    spreaded = jnp.where((row & (CCODE - 1)) == o, values, 0.0).astype(BF16)
-    taps = dot(spreaded, tap_onehot(), ((1,), (1,))).astype(BF16)
-    lane = iota((2 * CCODE, 512), 1)
-    repeat = hot(iota((2 * CCODE, 512), 0) == ((lane >> 8) * CCODE + (lane & 15)))
-    return dot(taps, repeat, ((0,), (0,))).astype(BF16)
+    taps = CIN * KS * KS
+    rows = jnp.concatenate([kernel_rows(x) for x in kernel_pair for _ in range(8)], axis=0)
+    lane = iota((1, 128), 1)
+    target, _ = tap_target(jnp.minimum(lane, taps - 1))
+    slots = hot(iota((128, 128), 0) == jnp.where(lane < taps, target, -1))
+    wide = dot(slots, rows.T.astype(BF16)).astype(BF16)
+    halves = [wide[:, 0:128], wide[:, 128:256]]
+    return jnp.concatenate([x for x in halves for _ in range(2)], axis=1)
 
 
 def band_weights(wide_taps):
@@ -319,7 +341,6 @@
     copies.append(pltpu.make_async_copy(kernel, kernel_buf, sems.at[3]))
     for copy in copies:
         copy.start()
-    out[z.halo : z.sent, z.span : z.span + HW] = jnp.zeros((z.sent - z.halo, HW), BF16)
     for copy in copies:
         copy.wait()
     kernel_out[...] = jnp.broadcast_to(kernel_buf[...].astype(F32), (COPIES, NK)).astype(BF16)
@@ -336,11 +357,16 @@
     mask_rows = beside(mask_buf)
     allowed = jnp.concatenate([mask_rows] * CIN, axis=2)
     every, half = range(0, HALO, 2), range(0, HALO // 2, 2)
-    out[0 : z.halo, 0 : z.span] = ordered(beside(field_buf) * allowed, every)
-    out[0 : z.halo, z.span : z.span + HW] = ordered(mask_rows, every)
     near = beside(cot_buf) * allowed
     near = jnp.where(odd == 1, near[:, : HALO // 2], near[:, HALO // 2 :])
-    out[z.halo : z.sent, 0 : z.span] = ordered(near, half)
+    pieces = ordered(beside(field_buf) * allowed, every), ordered(near, half)
+    start = 0
+    for piece in pieces:
+        count = piece.shape[0]
+        for c in range(CIN):
+            out[start : start + count, :] = piece[:, c * HW : c * HW + HW]
+            start += count
+    out[start : z.sent, :] = ordered(mask_rows, every)[0 : z.near]
 
 
 def prepare_kernel(
@@ -370,11 +396,10 @@
     columns = window_columns()
     mask_columns = window_mask_columns()
     pixel_mask = mask[mine_rows].astype(F32).astype(BF16).reshape(z.own, HW)
-    framed_mask = dot(gather, pixel_mask).astype(BF16)
-    in_mask = dot(framed_mask, mask_columns)
-    windowed = dot(
-        dot(gather, fields[mine_rows].reshape(z.own, z.span)).astype(BF16), columns
-    )
+    pixels = fields[mine_rows].reshape(z.own, z.span)
+    framed = dot(gather, jnp.concatenate([pixel_mask, pixels], axis=1)).astype(BF16)
+    in_mask = dot(framed[:, 0:HW], mask_columns)
+    windowed = dot(framed[:, HW:], columns)
     for copy in copies:
         copy.wait()
     lane = iota((8, 128), 1)
@@ -442,13 +467,6 @@
     for s in sums:
         pay.append(fold(jnp.broadcast_to(s[:, :128] + s[:, 128:], (8, 128)), 16)[0:1])
     return code, slope, jnp.concatenate(pay, axis=0)
-
-
-def put_codes(blocks, count, start, code_out):
-    rows = pl.ds(start, count)
-    for b, (low, high) in enumerate(mend_coarse(blocks)):
-        code_out[b, rows, 0:128] = low.astype(BF16)
-        code_out[b, rows, 128:256] = high.astype(BF16)
 
 
 def inner_kernel(
@@ -486,14 +504,19 @@
 def encode_kernel(
     z, pixels, own_mask, halo, banded, aux, inner_pay, taps_in, code_in, slope_in,
     taps_out, code_out, slope_out, cot_out, pay_out,
-    sh, pays, sem,
+    sh,
 ):
     odd = lax.rem(lax.axis_index("wide"), 2)
     half = z.own // 2
     count = 32
     channel_ok = jnp.tile(aux[40:56], (1, NB))
-    halo_mask = dot(halo[0:16, z.span : z.span + HW], window_mask_columns())
-    halo_pixels = dot(halo[:, 0 : z.span], window_columns())
+    middle, end = CIN * z.halo, CIN * (z.halo + z.near)
+    halo_mask = dot(halo[end : z.sent, :], window_mask_columns())
+    halo_rows = [
+        jnp.concatenate([halo[i : i + count, :] for i in range(start, stop, count)], axis=1)
+        for start, stop, count in ((0, middle, z.halo), (middle, end, z.near))
+    ]
+    halo_pixels = dot(jnp.concatenate(halo_rows, axis=0), window_columns())
     halo_x = halo_pixels[0 : z.halo] * jnp.tile(channel_ok, (2, 1))
     zeros = jnp.zeros((NB, 16, 256), F32)
     sh[:, 0:16, :] = zeros
@@ -521,26 +544,17 @@
     mine = ((iota((NB * count, 1), 0) >> 4) & 1) == odd
     code, slope, pay = encode_rows(jnp.concatenate(taps, axis=0), banded[...], bias, masks, mine)
     pay = pay + inner_pay[...]
-    for i in range(pays.shape[0]):
-        pays[i] = pay
-    copy = pltpu.make_async_copy(pays, pay_out, sem.at[0])
-    copy.start()
+    pay_out[...] = pay
     for b in range(NB):
-        slope_out[b, pl.ds(start, count), :] = slope[b * count : b * count + count]
-    put_codes([code[b * count : b * count + count] for b in range(NB)], count, start, code_out)
-    inner = z.rows - count
-    inner_start = pl.multiple_of(odd * count, 16)
-    put_codes(
-        [code_in[b, pl.ds(inner_start, inner), :].astype(F32) for b in range(NB)],
-        inner, inner_start, code_out,
-    )
-    near = halo_pixels[z.halo : z.sent] * channel_ok
+        rs = slice(b * count, b * count + count)
+        code_out[b, pl.ds(start, count), :] = code[rs].astype(BF16)
+        slope_out[b, pl.ds(start, count), :] = slope[rs]
+    near = halo_pixels[z.halo : z.halo + z.near] * channel_ok
     nothing = jnp.zeros((8, NB * 128), F32)
     for h in range(2):
         rows = near[h * 8 : h * 8 + 8]
         rows = [jnp.where(odd == 1, nothing, rows), jnp.where(odd == 1, rows, nothing)]
         cot_out[h * 16 : h * 16 + 16, :] = jnp.concatenate(rows, axis=0).astype(BF16)
-    copy.wait()
 
 
 def decode_kernel(
@@ -551,9 +565,7 @@
     odd = lax.rem(lax.axis_index("wide"), 2)
     mine = pl.ds(lax.axis_index("section") * z.mb, z.mb)
     rows = z.rows
-    put_frame(
-        z, sh, [(code[b, :, 0:128].astype(F32), code[b, :, 128:256].astype(F32)) for b in range(NB)]
-    )
+    put_frame(z, sh, mend_coarse([code[b].astype(F32) for b in range(NB)]))
     banded = band_weights(weights[:, 256:512])
     raws = spread(z, sh, banded)
     gather = gather_rows(z)
@@ -577,8 +589,14 @@
     put_frame(z, sh, mend_fine([(grads[b], grads[NB + b]) for b in range(NB)]))
     taps = jnp.concatenate([fine_taps(z, sh, b) for b in range(NB)], axis=0)
     sent_out[...] = dot(taps, banded).astype(BF16).reshape(NB, rows, 256)
+    last = HW // 2 - (NB - 1) * (UW - 2)
+    within = mine_rows & ((iota((1, 256), 1) >> 4) <= last)
     mine = jnp.concatenate(
-        [jnp.where(mine_rows, code[b].astype(F32), 0.0).astype(BF16) for b in range(NB)], axis=0
+        [
+            jnp.where(within if b == NB - 1 else mine_rows, code[b].astype(F32), 0.0).astype(BF16)
+            for b in range(NB)
+        ],
+        axis=0,
     )
     pay = pick_taps(dot(mine, taps, ((0,), (0,))))
     bias_sum = fold(jnp.broadcast_to(bias_sum, (16, 128)), 8)
@@ -591,7 +609,6 @@
 def whiten_kernel(
     z, stats, code, slope, sent, taps, decode_pay, aux,
     grad_out, pay_out, moments_out,
-    pays, sem,
 ):
     odd = lax.rem(lax.axis_index("wide"), 2)
     rows = z.rows
@@ -653,16 +670,11 @@
     biases = jnp.where((lane & 2) == 0, coarse, biases - coarse)
     encode_pay = jnp.where(lane >= 120, biases, encode_pay)
     decoded = jnp.where(lane >= 120, biases, decoded)
-    half = pays.shape[0] // 2
-    for i in range(half):
-        pays[i] = encode_pay.astype(BF16)
-        pays[half + i] = decoded.astype(BF16)
-    copy = pltpu.make_async_copy(pays, pay_out, sem.at[0])
-    copy.start()
+    pay_out[0] = encode_pay.astype(BF16)
+    pay_out[1] = decoded.astype(BF16)
     for b, (low, high) in enumerate(mend_coarse(blocks)):
         grad_out[b, :, 0:128] = low.astype(BF16)
         grad_out[b, :, 128:256] = high.astype(BF16)
-    copy.wait()
 
 
 def picture(z, decodes, grad, code, in_mask, weights, aux, sh):
@@ -671,7 +683,7 @@
     frames = [
         jnp.where(decodes, code[b].astype(F32), grad[b].astype(F32)) for b in range(NB)
     ]
-    put_frame(z, sh, [(x[:, 0:128], x[:, 128:256]) for x in frames])
+    put_frame(z, sh, mend_coarse(frames))
     chosen = jnp.where(decodes, weights[:, 256:512].astype(F32), weights[:, 0:256].astype(F32))
     raws = spread(z, sh, band_weights(chosen))
     for h in range(2):
@@ -807,7 +819,7 @@
         halo, kernel_own = call(
             edge_kernel,
             "edge",
-            [shape(z.sent, z.span + HW), shape(COPIES, NK)],
+            [shape(z.sent, HW), shape(COPIES, NK)],
             [HBM] * 4,
             [
                 edge_buf,
@@ -853,16 +865,12 @@
         taps, code, slope, halo_cot, pay = call(
             encode_kernel,
             "encode",
-            coded + [shape(z.halo, NB * 128), shape(sections * wides, 4, 128, dtype=F32)],
+            coded + [shape(z.halo, NB * 128), shape(4, 128, dtype=F32)],
             [VMEM] * 9,
-            [
-                pltpu.VMEM((NB, 64, 256), F32),
-                pltpu.VMEM((sections * wides, 4, 128), F32),
-                DMA((1,)),
-            ],
-            out_specs=[VMEM] * 4 + [HBM],
+            [pltpu.VMEM((NB, 64, 256), F32)],
             alias={6: 0, 7: 1, 8: 2},
         )(pixels, in_mask, halo, banded, aux, pay, taps, code, slope)
+        pay = jnp.broadcast_to(pay[None], (sections * wides, 4, 128))
         stats = lax.all_to_all(pay, ("section", "wide"), 0, 0)
         sent, decode_pay = call(
             decode_kernel,
@@ -877,14 +885,15 @@
             "whiten",
             [
                 shape(*frame),
-                shape(sections * wides, CCODE, 128),
+                shape(sections, CCODE, 128),
                 shape(CCODE + 8, 128, dtype=F32),
             ],
             [VMEM] * 7,
-            [pltpu.VMEM((sections * wides, CCODE, 128), BF16), DMA((1,))],
-            out_specs=[VMEM, HBM, VMEM],
+            [],
             alias={3: 0},
         )(stats, code, slope, sent, taps, decode_pay, aux)
+        pay = jnp.broadcast_to(pay[:, None], (sections, wides, CCODE, 128))
+        pay = pay.reshape(sections * wides, CCODE, 128)
         parts = lax.all_to_all(pay, ("section", "wide"), 0, 0)
         (sending,) = call(
             send_kernel,

time: 36 us -> 35.9 us (level)
  local copies, waits for them, and re-layouts: 0.01 us -> 1.33 us
  Pallas kernels: 14.4 us -> 13.1 us
    pallas_call x3, Pallas kernels: 4.7 us -> 3.35 us  [the longest x1 1.37 us: run(): call(whiten_kernel, 'whiten', [shape(*frame), shape(sections, CCODE, 128)...]
    broadcast_in_dim x0 -> x2, local copies, waits for them, and re-layouts: none -> 1.31 us  [the longest x1 0.67 us: run(): pay = jnp.broadcast_to(pay[:, None], (sections, wides, CCODE, 128))]
where the time goes in v5:
time: 35.9 us; the launch traced here: 35.6 us
  Pallas kernels  13.1 us (36%)
  starting transfers between devices  11.3 us (31%)
  waiting for transfers between devices  9.1 us (25%)
  local copies, waits for them, and re-layouts  1.33 us (4%)
  between operations  0.76 us (2%)
    all_to_all x1, starting transfers between devices, run(): stats = lax.all_to_all(pay, ('section', 'wide'), 0, 0)  5.55 us
    all_to_all x1, waiting for transfers between devices, run(): stats = lax.all_to_all(pay, ('section', 'wide'), 0, 0)  5.19 us
    all_to_all x1, waiting for transfers between devices, run(): parts = lax.all_to_all(pay, ('section', 'wide'), 0, 0)  3.56 us
    ppermute x1, starting transfers between devices, run(): halo = lax.ppermute(halo, 'wide', pair)  3 us
    all_to_all x1, starting transfers between devices, run(): parts = lax.all_to_all(pay, ('section', 'wide'), 0, 0)  2.57 us
    pallas_call x1, Pallas kernels, run(): call(keep_kernel, 'keep', [shape(1, z.micro, z.band, z.span), shape(128,...  2.52 us
    pallas_call x1, Pallas kernels, run(): call(decode_kernel, 'decode', [shape(*frame), shape(CCODE, 128, dtype=F32...  2.11 us
    pallas_call x1, Pallas kernels, run(): call(send_kernel, 'send', [shape(z.mb, z.band, z.span)], [VMEM] * 5, [fra...  1.64 us
  transfers between devices with their start and end apart: 5, of which 3 were waited for; matrix products, arithmetic and copies ran while one was open for 0% of the time, Pallas kernels for 20%

profile of v5, /device:TPU:0, one launch (start us, length us, event | category | flops | bytes accessed | tf_op | source)
XLA Modules:
  0.0 35.6 jit_solution(12265778793083801243)
XLA Ops:
  0.6 0.0 copy-start.2
  0.6 0.0 copy-start
  0.7 1.1 %edge.1 = (bf16[208,128]{1,0:T(8,128)(2,1)S(1)}, bf16[32,1600]{1,0:T(8,128)(2,1)S(1)}) custom-call(bf16[8,64,512]{2,1,0:T(8,128)(2,1)} %refs_0_.4, s32[8,64,128]{2,1,0:T(8,128)} %refs_1_.3, bf16[8,64,512]{2,1,0:T(8,128)(2,1)} %refs_0_.5, bf16[1,1600]{1,0:T(2,128)(2,1)} %refs_3_.3), custom_call_target="tpu_custom_call" | custom-call | tf_op jit(solution)/shard_map/edge/pallas_call | solution.py:819
  1.7 3.0 %collective-permute-start = (bf16[208,128]{1,0:T(8,128)(2,1)S(1)}, bf16[208,128]{1,0:T(8,128)(2,1)S(1)}, u32[]{:S(2)}, u32[]{:S(2)}) collective-permute-start(bf16[208,128]{1,0:T(8,128)(2,1)S(1)} %get-tuple-element.36), channel_id=1, source_target_pairs={{0,1},{1,0},{2,3},{3,2},{4,5},{5,4},{6,7},{7,6},{8,9},{9,8},{10,11... | collective-permute-start | bytes 159752 | tf_op jit(solution)/shard_map/ppermute | solution.py:832
  4.8 0.0 collective-permute-start.1
  4.8 0.0 copy-done.2
  4.8 0.0 copy-done
  4.8 0.9 %prepare.1 = (bf16[256,640]{1,0:T(8,128)(2,1)S(1)}, bf16[256,640]{1,0:T(8,128)(2,1)S(1)}, f32[56,128]{1,0:T(8,128)S(1)}) custom-call(bf16[8,64,512]{2,1,0:T(8,128)(2,1)S(1)} %copy-done, s32[8,64,128]{2,1,0:T(8,128)S(1)} %copy-done.2, s32[8,8]{1,0:T(8,128)} %refs_2_.2, f32[16]{0:T(128)} %refs_3_.2, f32[4]{0:T(128)} %refs_4_.1, f32[16]{0:T(128)} %refs_5_.1, ...), custom_call_target="tpu_custom_call" | custom-call | flops 4000000000 | bytes 4000000 | tf_op jit(solution)/shard_map/prepare/pallas_call | solution.py:834
  5.7 0.4 collective-permute-done.1.refs_1_
  6.1 0.3 taps.1.refs_2_.refs_4_.refs_3_
  6.4 1.3 %inner.1 = (bf16[5,144,640]{2,1,0:T(8,128)(2,1)S(1)}, bf16[5,144,256]{2,1,0:T(8,128)(2,1)S(1)}, f32[5,144,256]{2,1,0:T(8,128)S(1)}, f32[4,128]{1,0:T(4,128)S(1)}, bf16[640,256]{1,0:T(8,128)(2,1)S(1)}) custom-call(bf16[256,640]{1,0:T(8,128)(2,1)S(1)} %get-tuple-element.34.refs_0_, bf16[256,640]{1,0:T(8,128)(2,1)S(1)} %get-tuple-element.35.refs_1_.refs_2_, ...), custom_call_target="tpu_custom_call" | custom-call | flops 4000000000 | bytes 4000000 | tf_op jit(solution)/shard_map/inner/pallas_call | solution.py:857
  7.7 0.0 collective-permute-done.refs_2_
  7.7 0.0 copy-start.1
  7.7 0.9 %encode.1 = (bf16[5,144,640]{2,1,0:T(8,128)(2,1)S(1)}, bf16[5,144,256]{2,1,0:T(8,128)(2,1)S(1)}, f32[5,144,256]{2,1,0:T(8,128)S(1)}, bf16[32,640]{1,0:T(8,128)(2,1)S(1)}, f32[4,128]{1,0:T(4,128)S(1)}) custom-call(bf16[256,640]{1,0:T(8,128)(2,1)S(1)} %get-tuple-element.34.refs_0_, ...), custom_call_target="tpu_custom_call", output_to_operand_aliasing={{0}: (6, {}), {1}: (7, {}), {2}: (8, {})} | custom-call | tf_op jit(solution)/shard_map/encode/pallas_call | solution.py:865
  8.6 0.6 %broadcast_in_dim.4 = f32[32,4,128]{2,1,0:T(4,128)} broadcast(f32[4,128]{1,0:T(4,128)S(1)} %get-tuple-element.44), dimensions={1,2} | broadcast | bytes 67584 | tf_op jit(solution)/shard_map/broadcast_in_dim | solution.py:873
  9.2 5.5 %all-to-all-start = ((f32[32,4,128]{2,1,0:T(4,128)}), f32[32,4,128]{2,1,0:T(4,128)S(1)}, u32[]{:S(2)}, u32[]{:S(2)}) async-start(f32[32,4,128]{2,1,0:T(4,128)} %broadcast_in_dim.4), calls=%async_computation | async-start | bytes 131072 | tf_op jit(solution)/shard_map/all_to_all | solution.py:874
  14.8 0.0 copy-done.1
  14.8 2.1 %decode.1 = (bf16[5,144,256]{2,1,0:T(8,128)(2,1)S(1)}, f32[16,128]{1,0:T(8,128)S(1)}) custom-call(bf16[8,64,512]{2,1,0:T(8,128)(2,1)S(1)} %copy-done.1, bf16[5,144,256]{2,1,0:T(8,128)(2,1)S(1)} %get-tuple-element.45.refs_1_, bf16[256,640]{1,0:T(8,128)(2,1)S(1)} %get-tuple-element.35.refs_1_.refs_2_, bf16[32,640]{1,0:T(8,128)(2,1)S(1)} %get-tuple-element.47.refs_3_, ...), custom_call_target="tpu_custom_call" | custom-call | flops 4000000000 | bytes 4000000 | tf_op jit(solution)/shard_map/decode/pallas_call | solution.py:875
  16.9 5.2 %all-to-all-done.refs_0_ = f32[32,4,128]{2,1,0:T(4,128)S(1)} async-done(((f32[32,4,128]{2,1,0:T(4,128)}), f32[32,4,128]{2,1,0:T(4,128)S(1)}, u32[]{:S(2)}, u32[]{:S(2)}) %all-to-all-start) | async-done | bytes 65568 | tf_op jit(solution)/shard_map/all_to_all | solution.py:874
  22.1 1.4 %whiten.1 = (bf16[5,144,256]{2,1,0:T(8,128)(2,1)S(1)}, bf16[2,16,128]{2,1,0:T(8,128)(2,1)S(1)}, f32[24,128]{1,0:T(8,128)S(1)}) custom-call(f32[32,4,128]{2,1,0:T(4,128)S(1)} %all-to-all-done.refs_0_, bf16[5,144,256]{2,1,0:T(8,128)(2,1)S(1)} %get-tuple-element.45.refs_1_, ...), custom_call_target="tpu_custom_call", output_to_operand_aliasing={{0}: (3, {})} | custom-call | tf_op jit(solution)/shard_map/whiten/pallas_call | solution.py:883
  23.5 0.7 %broadcast_in_dim.5 = bf16[2,16,16,128]{3,2,1,0:T(8,128)(2,1)} broadcast(bf16[2,16,128]{2,1,0:T(8,128)(2,1)S(1)} %get-tuple-element.51), dimensions={0,2,3} | broadcast | bytes 139264 | tf_op jit(solution)/shard_map/broadcast_in_dim | solution.py:895
  24.2 2.6 %all-to-all-start.1 = ((bf16[32,16,128]{2,1,0:T(8,128)(2,1)}), bf16[32,16,128]{2,1,0:T(8,128)(2,1)S(1)}, u32[]{:S(2)}, u32[]{:S(2)}) async-start(bf16[32,16,128]{2,1,0:T(8,128)(2,1)} %bitcast), calls=%async_computation.1 | async-start | bytes 262144 | tf_op jit(solution)/shard_map/all_to_all | solution.py:897
  26.7 1.6 %send.1 = bf16[4,64,512]{2,1,0:T(8,128)(2,1)S(1)} custom-call(bf16[5,144,256]{2,1,0:T(8,128)(2,1)S(1)} %get-tuple-element.52.refs_0_, bf16[5,144,256]{2,1,0:T(8,128)(2,1)S(1)} %get-tuple-element.45.refs_1_, bf16[256,640]{1,0:T(8,128)(2,1)S(1)} %get-tuple-element.35.refs_1_.refs_2_, bf16[128,512]{1,0:T(8,128)(2,1)S(1)} %taps.1.refs_2_.refs_4_.refs_3_, ...), custom_call_target="tpu_custom_call" | custom-call | flops 4000000000 | bytes 4000000 | tf_op jit(solution)/shard_map/send/pallas_call | solution.py:898
  28.4 0.2 collective-permute-start.2
  28.6 2.5 %keep.1 = (bf16[1,8,64,512]{3,2,1,0:T(8,128)(2,1)}, bf16[128,1600]{1,0:T(8,128)(2,1)S(1)}, f32[1,16]{1,0:T(1,128)}, f32[16,16]{1,0:T(8,128)}) custom-call(bf16[5,144,256]{2,1,0:T(8,128)(2,1)S(1)} %get-tuple-element.52.refs_0_, bf16[5,144,256]{2,1,0:T(8,128)(2,1)S(1)} %get-tuple-element.45.refs_1_, bf16[256,640]{1,0:T(8,128)(2,1)S(1)} %get-tuple-element.35.refs_1_.refs_2_, ...), custom_call_target="tpu_custom_call" | custom-call | flops 4000000000 | bytes 4000000 | tf_op jit(solution)/shard_map/keep/pallas_call | solution.py:907
  31.1 3.6 %all-to-all-done.1.refs_0_ = bf16[32,16,128]{2,1,0:T(8,128)(2,1)S(1)} async-done(((bf16[32,16,128]{2,1,0:T(8,128)(2,1)}), bf16[32,16,128]{2,1,0:T(8,128)(2,1)S(1)}, u32[]{:S(2)}, u32[]{:S(2)}) %all-to-all-start.1) | async-done | bytes 131104 | tf_op jit(solution)/shard_map/all_to_all | solution.py:897
  34.7 0.0 collective-permute-done.2.refs_1_
  34.7 0.9 %finish.1 = (bf16[1,8,64,512]{3,2,1,0:T(8,128)(2,1)}, f32[1,1600]{1,0:T(1,128)}, f32[1,16]{1,0:T(1,128)}, f32[1,4]{1,0:T(1,128)}) custom-call(f32[16,128]{1,0:T(8,128)S(1)} %total.1.refs_0_, bf16[4,64,512]{2,1,0:T(8,128)(2,1)S(1)} %collective-permute-done.2.refs_1_, ...), custom_call_target="tpu_custom_call", output_to_operand_aliasing={{0}: (3, {})} | custom-call | tf_op jit(solution)/shard_map/finish/pallas_call | solution.py:935
  (1 shorter events, 0.0 us)
Async XLA Ops:
  0.6 4.1 %copy-start.2 = (s32[8,64,128]{2,1,0:T(8,128)S(1)}, s32[8,64,128]{2,1,0:T(8,128)}, u32[]{:S(2)}) copy-start(s32[8,64,128]{2,1,0:T(8,128)} %refs_1_.3) | copy-start | bytes 786436
  0.6 4.1 %copy-start = (bf16[8,64,512]{2,1,0:T(8,128)(2,1)S(1)}, bf16[8,64,512]{2,1,0:T(8,128)(2,1)}, u32[]{:S(2)}) copy-start(bf16[8,64,512]{2,1,0:T(8,128)(2,1)} %refs_0_.4) | copy-start | bytes 1572868
  1.7 5.9 %collective-permute-start = (bf16[208,128]{1,0:T(8,128)(2,1)S(1)}, bf16[208,128]{1,0:T(8,128)(2,1)S(1)}, u32[]{:S(2)}, u32[]{:S(2)}) collective-permute-start(bf16[208,128]{1,0:T(8,128)(2,1)S(1)} %get-tuple-element.36), channel_id=1, source_target_pairs={{0,1},{1,0},{2,3},{3,2},{4,5},{5,4},{6,7},{7,6},{8,9},{9,8},{10,11... | collective-permute-start | bytes 159752 | tf_op jit(solution)/shard_map/ppermute | solution.py:832
  4.8 1.3 %collective-permute-start.1 = (bf16[32,1600]{1,0:T(8,128)(2,1)S(1)}, bf16[32,1600]{1,0:T(8,128)(2,1)S(1)}, u32[]{:S(2)}, u32[]{:S(2)}) collective-permute-start(bf16[32,1600]{1,0:T(8,128)(2,1)S(1)} %get-tuple-element.37.refs_0_), channel_id=1, source_target_pairs={{0,16},{16,0},{1,17},{17,1},{2,18},{18,2},{3,19},{19,3},{4,20},{20... | collective-permute-start | bytes 307208 | tf_op jit(solution)/shard_map/ppermute | solution.py:833
  7.7 7.1 %copy-start.1 = (bf16[8,64,512]{2,1,0:T(8,128)(2,1)S(1)}, bf16[8,64,512]{2,1,0:T(8,128)(2,1)}, u32[]{:S(2)}) copy-start(bf16[8,64,512]{2,1,0:T(8,128)(2,1)} %refs_0_.5) | copy-start | bytes 1572868
  9.2 12.9 %all-to-all-start = ((f32[32,4,128]{2,1,0:T(4,128)}), f32[32,4,128]{2,1,0:T(4,128)S(1)}, u32[]{:S(2)}, u32[]{:S(2)}) async-start(f32[32,4,128]{2,1,0:T(4,128)} %broadcast_in_dim.4), calls=%async_computation | async-start | bytes 131072 | tf_op jit(solution)/shard_map/all_to_all | solution.py:874
  24.2 10.5 %all-to-all-start.1 = ((bf16[32,16,128]{2,1,0:T(8,128)(2,1)}), bf16[32,16,128]{2,1,0:T(8,128)(2,1)S(1)}, u32[]{:S(2)}, u32[]{:S(2)}) async-start(bf16[32,16,128]{2,1,0:T(8,128)(2,1)} %bitcast), calls=%async_computation.1 | async-start | bytes 262144 | tf_op jit(solution)/shard_map/all_to_all | solution.py:897
  28.4 6.3 %collective-permute-start.2 = (bf16[4,64,512]{2,1,0:T(8,128)(2,1)S(1)}, bf16[4,64,512]{2,1,0:T(8,128)(2,1)S(1)}, u32[]{:S(2)}, u32[]{:S(2)}) collective-permute-start(bf16[4,64,512]{2,1,0:T(8,128)(2,1)S(1)} %send.1), channel_id=1, source_target_pairs={{0,16},{16,0},{1,17},{17,1},{2,18},{18,2},{3,19},{19,3},{4,20},{20... | collective-permute-start | bytes 786440 | tf_op jit(solution)/shard_map/ppermute | solution.py:906

commit v6 on v5

--- a/solution.py
+++ b/solution.py
@@ -40,6 +40,10 @@
     while len(rolled) > 1:
         rolled = [sum(rolled[i : i + 2]) for i in range(0, len(rolled), 2)]
     return rolled[0]
+
+
+def lanes_from(x, source):
+    return jnp.take_along_axis(x, source, axis=1, mode="promise_in_bounds")
 
 
 def split(x):
@@ -464,8 +468,14 @@
         jnp.sum(jnp.where(diagonal, total[h * 8 : h * 8 + 8], 0.0), axis=0, keepdims=True)
         for h in range(2)
     ]
-    for s in sums:
-        pay.append(fold(jnp.broadcast_to(s[:, :128] + s[:, 128:], (8, 128)), 16)[0:1])
+    first, count = (
+        fold(jnp.broadcast_to(x[:, :128] + x[:, 128:], (8, 128)), 16) for x in sums
+    )
+    lane = iota((8, 128), 1)
+    inner, group = lane & 15, lane >> 4
+    first = lanes_from(first, jnp.where(inner == 0, group, group + 8))
+    spare = jnp.where(inner == 2, count, first)[0:1]
+    pay[1] = jnp.where(inner[0:1] < 8, spare, pay[1])
     return code, slope, jnp.concatenate(pay, axis=0)
 
 
@@ -613,21 +623,23 @@
     odd = lax.rem(lax.axis_index("wide"), 2)
     rows = z.rows
     pay = jnp.sum(stats[...], axis=0)
-    count = pay[3:4]
-    mean = pay[2:3] / count
-    diagonal = (iota((8, 128), 1) >> 4) == iota((8, 128), 0)
-    second = jnp.concatenate(
-        [
-            fold(jnp.where(diagonal, jnp.broadcast_to(pay[h : h + 1], (8, 128)), 0.0), 16)
-            for h in range(2)
-        ],
-        axis=0,
-    )
+    lane = iota((8, 128), 1)
+    inner, step = lane & 15, iota((8, 128), 0)
+    low, high = (jnp.broadcast_to(pay[h : h + 1], (8, 128)) for h in range(2))
+    count = lanes_from(high, jnp.full((8, 128), 2, jnp.int32))[0:1]
+    first = lanes_from(high, jnp.where(inner < 8, 16 * inner, 16 * (inner - 8) + 1))[0:1]
+    mean = first / count
+    columns = jnp.concatenate([lanes_from(high, 16 * step + h) for h in range(2)], axis=0)
+    diagonal = (lane >> 4) == step
+    mirrored = lanes_from(low, jnp.where(inner < 8, 16 * inner + 8 + step, 0))
+    low, high = (fold(jnp.where(diagonal, x, 0.0), 16) for x in (low, high))
+    second = jnp.concatenate([low, jnp.where(inner < 8, mirrored, high)], axis=0)
     lane = iota((16, 128), 1)
     row = iota((16, 128), 0)
     wide_mean = jnp.broadcast_to(mean, (16, 128))
-    mean_column = jnp.sum(jnp.where(lane == row, wide_mean, 0.0), axis=1, keepdims=True)
-    cov = second / jnp.broadcast_to(count, (16, 128)) - mean_column * wide_mean
+    total = jnp.broadcast_to(count, (16, 128))
+    mean_column = columns / total
+    cov = second / total - mean_column * wide_mean
     moments_out[0:CCODE] = cov
     moments_out[CCODE:] = jnp.broadcast_to(mean, (8, 128))
     offset = cov - jnp.where((lane & 15) == row, 1.0, 0.0)
@@ -857,7 +869,7 @@
         taps, code, slope, pay, banded = call(
             inner_kernel,
             "inner",
-            coded + [shape(4, 128, dtype=F32), shape(KS * 128, 256)],
+            coded + [shape(2, 128, dtype=F32), shape(KS * 128, 256)],
             [VMEM] * 4,
             [pltpu.VMEM((NB, z.own // 2 + 16, 256), F32)],
             cost=heavy,
@@ -865,12 +877,12 @@
         taps, code, slope, halo_cot, pay = call(
             encode_kernel,
             "encode",
-            coded + [shape(z.halo, NB * 128), shape(4, 128, dtype=F32)],
+            coded + [shape(z.halo, NB * 128), shape(2, 128, dtype=F32)],
             [VMEM] * 9,
             [pltpu.VMEM((NB, 64, 256), F32)],
             alias={6: 0, 7: 1, 8: 2},
         )(pixels, in_mask, halo, banded, aux, pay, taps, code, slope)
-        pay = jnp.broadcast_to(pay[None], (sections * wides, 4, 128))
+        pay = jnp.broadcast_to(pay[None], (sections * wides, 2, 128))
         stats = lax.all_to_all(pay, ("section", "wide"), 0, 0)
         sent, decode_pay = call(
             decode_kernel,

time: 35.9 us -> 35.7 us (level)
  no operation moved by 1% of the time
where the time goes in v6:
time: 35.7 us; the launch traced here: 35.4 us
  Pallas kernels  13 us (36%)
  starting transfers between devices  11.3 us (32%)
  waiting for transfers between devices  8.99 us (25%)
  local copies, waits for them, and re-layouts  1.31 us (4%)
  between operations  0.76 us (2%)
    all_to_all x1, starting transfers between devices, run(): stats = lax.all_to_all(pay, ('section', 'wide'), 0, 0)  5.56 us
    all_to_all x1, waiting for transfers between devices, run(): stats = lax.all_to_all(pay, ('section', 'wide'), 0, 0)  5.07 us
    all_to_all x1, waiting for transfers between devices, run(): parts = lax.all_to_all(pay, ('section', 'wide'), 0, 0)  3.56 us
    ppermute x1, starting transfers between devices, run(): halo = lax.ppermute(halo, 'wide', pair)  3 us
    all_to_all x1, starting transfers between devices, run(): parts = lax.all_to_all(pay, ('section', 'wide'), 0, 0)  2.57 us
    pallas_call x1, Pallas kernels, run(): call(keep_kernel, 'keep', [shape(1, z.micro, z.band, z.span), shape(128,...  2.52 us
    pallas_call x1, Pallas kernels, run(): call(decode_kernel, 'decode', [shape(*frame), shape(CCODE, 128, dtype=F32...  2.12 us
    pallas_call x1, Pallas kernels, run(): call(send_kernel, 'send', [shape(z.mb, z.band, z.span)], [VMEM] * 5, [fra...  1.64 us
  transfers between devices with their start and end apart: 5, of which 3 were waited for; matrix products, arithmetic and copies ran while one was open for 0% of the time, Pallas kernels for 20%

profile of v6, /device:TPU:0, one launch (start us, length us, event | category | flops | bytes accessed | tf_op | source)
XLA Modules:
  0.0 35.4 jit_solution(16127426977771702558)
XLA Ops:
  0.6 0.0 copy-start.2
  0.6 0.0 copy-start
  0.7 1.1 %edge.1 = (bf16[208,128]{1,0:T(8,128)(2,1)S(1)}, bf16[32,1600]{1,0:T(8,128)(2,1)S(1)}) custom-call(bf16[8,64,512]{2,1,0:T(8,128)(2,1)} %refs_0_.4, s32[8,64,128]{2,1,0:T(8,128)} %refs_1_.3, bf16[8,64,512]{2,1,0:T(8,128)(2,1)} %refs_0_.5, bf16[1,1600]{1,0:T(2,128)(2,1)} %refs_3_.3), custom_call_target="tpu_custom_call" | custom-call | tf_op jit(solution)/shard_map/edge/pallas_call | solution.py:831
  1.7 3.0 %collective-permute-start = (bf16[208,128]{1,0:T(8,128)(2,1)S(1)}, bf16[208,128]{1,0:T(8,128)(2,1)S(1)}, u32[]{:S(2)}, u32[]{:S(2)}) collective-permute-start(bf16[208,128]{1,0:T(8,128)(2,1)S(1)} %get-tuple-element.36), channel_id=1, source_target_pairs={{0,1},{1,0},{2,3},{3,2},{4,5},{5,4},{6,7},{7,6},{8,9},{9,8},{10,11... | collective-permute-start | bytes 159752 | tf_op jit(solution)/shard_map/ppermute | solution.py:844
  4.8 0.0 collective-permute-start.1
  4.8 0.0 copy-done.2
  4.8 0.0 copy-done
  4.8 0.9 %prepare.1 = (bf16[256,640]{1,0:T(8,128)(2,1)S(1)}, bf16[256,640]{1,0:T(8,128)(2,1)S(1)}, f32[56,128]{1,0:T(8,128)S(1)}) custom-call(bf16[8,64,512]{2,1,0:T(8,128)(2,1)S(1)} %copy-done, s32[8,64,128]{2,1,0:T(8,128)S(1)} %copy-done.2, s32[8,8]{1,0:T(8,128)} %refs_2_.2, f32[16]{0:T(128)} %refs_3_.2, f32[4]{0:T(128)} %refs_4_.1, f32[16]{0:T(128)} %refs_5_.1, ...), custom_call_target="tpu_custom_call" | custom-call | flops 4000000000 | bytes 4000000 | tf_op jit(solution)/shard_map/prepare/pallas_call | solution.py:846
  5.7 0.4 collective-permute-done.1.refs_1_
  6.1 0.3 taps.1.refs_2_.refs_4_.refs_3_
  6.4 1.2 %inner.1 = (bf16[5,144,640]{2,1,0:T(8,128)(2,1)S(1)}, bf16[5,144,256]{2,1,0:T(8,128)(2,1)S(1)}, f32[5,144,256]{2,1,0:T(8,128)S(1)}, f32[2,128]{1,0:T(2,128)S(1)}, bf16[640,256]{1,0:T(8,128)(2,1)S(1)}) custom-call(bf16[256,640]{1,0:T(8,128)(2,1)S(1)} %get-tuple-element.34.refs_0_, bf16[256,640]{1,0:T(8,128)(2,1)S(1)} %get-tuple-element.35.refs_1_.refs_2_, ...), custom_call_target="tpu_custom_call" | custom-call | flops 4000000000 | bytes 4000000 | tf_op jit(solution)/shard_map/inner/pallas_call | solution.py:869
  7.7 0.0 collective-permute-done.refs_2_
  7.7 0.0 copy-start.1
  7.7 0.9 %encode.1 = (bf16[5,144,640]{2,1,0:T(8,128)(2,1)S(1)}, bf16[5,144,256]{2,1,0:T(8,128)(2,1)S(1)}, f32[5,144,256]{2,1,0:T(8,128)S(1)}, bf16[32,640]{1,0:T(8,128)(2,1)S(1)}, f32[2,128]{1,0:T(2,128)S(1)}) custom-call(bf16[256,640]{1,0:T(8,128)(2,1)S(1)} %get-tuple-element.34.refs_0_, ...), custom_call_target="tpu_custom_call", output_to_operand_aliasing={{0}: (6, {}), {1}: (7, {}), {2}: (8, {})} | custom-call | tf_op jit(solution)/shard_map/encode/pallas_call | solution.py:877
  8.6 0.6 %broadcast_in_dim.4 = f32[32,2,128]{2,1,0:T(2,128)} broadcast(f32[2,128]{1,0:T(2,128)S(1)} %get-tuple-element.44), dimensions={1,2} | broadcast | bytes 33792 | tf_op jit(solution)/shard_map/broadcast_in_dim | solution.py:885
  9.2 5.6 %all-to-all-start = ((f32[32,2,128]{2,1,0:T(2,128)}), f32[32,2,128]{2,1,0:T(2,128)S(1)}, u32[]{:S(2)}, u32[]{:S(2)}) async-start(f32[32,2,128]{2,1,0:T(2,128)} %broadcast_in_dim.4), calls=%async_computation | async-start | bytes 65536 | tf_op jit(solution)/shard_map/all_to_all | solution.py:886
  14.8 0.0 copy-done.1
  14.8 2.1 %decode.1 = (bf16[5,144,256]{2,1,0:T(8,128)(2,1)S(1)}, f32[16,128]{1,0:T(8,128)S(1)}) custom-call(bf16[8,64,512]{2,1,0:T(8,128)(2,1)S(1)} %copy-done.1, bf16[5,144,256]{2,1,0:T(8,128)(2,1)S(1)} %get-tuple-element.45.refs_1_, bf16[256,640]{1,0:T(8,128)(2,1)S(1)} %get-tuple-element.35.refs_1_.refs_2_, bf16[32,640]{1,0:T(8,128)(2,1)S(1)} %get-tuple-element.47.refs_3_, ...), custom_call_target="tpu_custom_call" | custom-call | flops 4000000000 | bytes 4000000 | tf_op jit(solution)/shard_map/decode/pallas_call | solution.py:887
  16.9 5.1 %all-to-all-done.refs_0_ = f32[32,2,128]{2,1,0:T(2,128)S(1)} async-done(((f32[32,2,128]{2,1,0:T(2,128)}), f32[32,2,128]{2,1,0:T(2,128)S(1)}, u32[]{:S(2)}, u32[]{:S(2)}) %all-to-all-start) | async-done | bytes 32800 | tf_op jit(solution)/shard_map/all_to_all | solution.py:886
  22.0 1.4 %whiten.1 = (bf16[5,144,256]{2,1,0:T(8,128)(2,1)S(1)}, bf16[2,16,128]{2,1,0:T(8,128)(2,1)S(1)}, f32[24,128]{1,0:T(8,128)S(1)}) custom-call(f32[32,2,128]{2,1,0:T(2,128)S(1)} %all-to-all-done.refs_0_, bf16[5,144,256]{2,1,0:T(8,128)(2,1)S(1)} %get-tuple-element.45.refs_1_, ...), custom_call_target="tpu_custom_call", output_to_operand_aliasing={{0}: (3, {})} | custom-call | tf_op jit(solution)/shard_map/whiten/pallas_call | solution.py:895
  23.4 0.7 %broadcast_in_dim.5 = bf16[2,16,16,128]{3,2,1,0:T(8,128)(2,1)} broadcast(bf16[2,16,128]{2,1,0:T(8,128)(2,1)S(1)} %get-tuple-element.51), dimensions={0,2,3} | broadcast | bytes 139264 | tf_op jit(solution)/shard_map/broadcast_in_dim | solution.py:907
  24.0 2.6 %all-to-all-start.1 = ((bf16[32,16,128]{2,1,0:T(8,128)(2,1)}), bf16[32,16,128]{2,1,0:T(8,128)(2,1)S(1)}, u32[]{:S(2)}, u32[]{:S(2)}) async-start(bf16[32,16,128]{2,1,0:T(8,128)(2,1)} %bitcast), calls=%async_computation.1 | async-start | bytes 262144 | tf_op jit(solution)/shard_map/all_to_all | solution.py:909
  26.6 1.6 %send.1 = bf16[4,64,512]{2,1,0:T(8,128)(2,1)S(1)} custom-call(bf16[5,144,256]{2,1,0:T(8,128)(2,1)S(1)} %get-tuple-element.52.refs_0_, bf16[5,144,256]{2,1,0:T(8,128)(2,1)S(1)} %get-tuple-element.45.refs_1_, bf16[256,640]{1,0:T(8,128)(2,1)S(1)} %get-tuple-element.35.refs_1_.refs_2_, bf16[128,512]{1,0:T(8,128)(2,1)S(1)} %taps.1.refs_2_.refs_4_.refs_3_, ...), custom_call_target="tpu_custom_call" | custom-call | flops 4000000000 | bytes 4000000 | tf_op jit(solution)/shard_map/send/pallas_call | solution.py:910
  28.3 0.2 collective-permute-start.2
  28.4 2.5 %keep.1 = (bf16[1,8,64,512]{3,2,1,0:T(8,128)(2,1)}, bf16[128,1600]{1,0:T(8,128)(2,1)S(1)}, f32[1,16]{1,0:T(1,128)}, f32[16,16]{1,0:T(8,128)}) custom-call(bf16[5,144,256]{2,1,0:T(8,128)(2,1)S(1)} %get-tuple-element.52.refs_0_, bf16[5,144,256]{2,1,0:T(8,128)(2,1)S(1)} %get-tuple-element.45.refs_1_, bf16[256,640]{1,0:T(8,128)(2,1)S(1)} %get-tuple-element.35.refs_1_.refs_2_, ...), custom_call_target="tpu_custom_call" | custom-call | flops 4000000000 | bytes 4000000 | tf_op jit(solution)/shard_map/keep/pallas_call | solution.py:919
  31.0 3.6 %all-to-all-done.1.refs_0_ = bf16[32,16,128]{2,1,0:T(8,128)(2,1)S(1)} async-done(((bf16[32,16,128]{2,1,0:T(8,128)(2,1)}), bf16[32,16,128]{2,1,0:T(8,128)(2,1)S(1)}, u32[]{:S(2)}, u32[]{:S(2)}) %all-to-all-start.1) | async-done | bytes 131104 | tf_op jit(solution)/shard_map/all_to_all | solution.py:909
  34.6 0.0 collective-permute-done.2.refs_1_
  34.6 0.9 %finish.1 = (bf16[1,8,64,512]{3,2,1,0:T(8,128)(2,1)}, f32[1,1600]{1,0:T(1,128)}, f32[1,16]{1,0:T(1,128)}, f32[1,4]{1,0:T(1,128)}) custom-call(f32[16,128]{1,0:T(8,128)S(1)} %total.1.refs_0_, bf16[4,64,512]{2,1,0:T(8,128)(2,1)S(1)} %collective-permute-done.2.refs_1_, ...), custom_call_target="tpu_custom_call", output_to_operand_aliasing={{0}: (3, {})} | custom-call | tf_op jit(solution)/shard_map/finish/pallas_call | solution.py:947
  (1 shorter events, 0.0 us)
Async XLA Ops:
  0.6 4.1 %copy-start.2 = (s32[8,64,128]{2,1,0:T(8,128)S(1)}, s32[8,64,128]{2,1,0:T(8,128)}, u32[]{:S(2)}) copy-start(s32[8,64,128]{2,1,0:T(8,128)} %refs_1_.3) | copy-start | bytes 786436
  0.6 4.1 %copy-start = (bf16[8,64,512]{2,1,0:T(8,128)(2,1)S(1)}, bf16[8,64,512]{2,1,0:T(8,128)(2,1)}, u32[]{:S(2)}) copy-start(bf16[8,64,512]{2,1,0:T(8,128)(2,1)} %refs_0_.4) | copy-start | bytes 1572868
  1.7 5.9 %collective-permute-start = (bf16[208,128]{1,0:T(8,128)(2,1)S(1)}, bf16[208,128]{1,0:T(8,128)(2,1)S(1)}, u32[]{:S(2)}, u32[]{:S(2)}) collective-permute-start(bf16[208,128]{1,0:T(8,128)(2,1)S(1)} %get-tuple-element.36), channel_id=1, source_target_pairs={{0,1},{1,0},{2,3},{3,2},{4,5},{5,4},{6,7},{7,6},{8,9},{9,8},{10,11... | collective-permute-start | bytes 159752 | tf_op jit(solution)/shard_map/ppermute | solution.py:844
  4.8 1.3 %collective-permute-start.1 = (bf16[32,1600]{1,0:T(8,128)(2,1)S(1)}, bf16[32,1600]{1,0:T(8,128)(2,1)S(1)}, u32[]{:S(2)}, u32[]{:S(2)}) collective-permute-start(bf16[32,1600]{1,0:T(8,128)(2,1)S(1)} %get-tuple-element.37.refs_0_), channel_id=1, source_target_pairs={{0,16},{16,0},{1,17},{17,1},{2,18},{18,2},{3,19},{19,3},{4,20},{20... | collective-permute-start | bytes 307208 | tf_op jit(solution)/shard_map/ppermute | solution.py:845
  7.7 7.1 %copy-start.1 = (bf16[8,64,512]{2,1,0:T(8,128)(2,1)S(1)}, bf16[8,64,512]{2,1,0:T(8,128)(2,1)}, u32[]{:S(2)}) copy-start(bf16[8,64,512]{2,1,0:T(8,128)(2,1)} %refs_0_.5) | copy-start | bytes 1572868
  9.2 12.8 %all-to-all-start = ((f32[32,2,128]{2,1,0:T(2,128)}), f32[32,2,128]{2,1,0:T(2,128)S(1)}, u32[]{:S(2)}, u32[]{:S(2)}) async-start(f32[32,2,128]{2,1,0:T(2,128)} %broadcast_in_dim.4), calls=%async_computation | async-start | bytes 65536 | tf_op jit(solution)/shard_map/all_to_all | solution.py:886
  24.0 10.5 %all-to-all-start.1 = ((bf16[32,16,128]{2,1,0:T(8,128)(2,1)}), bf16[32,16,128]{2,1,0:T(8,128)(2,1)S(1)}, u32[]{:S(2)}, u32[]{:S(2)}) async-start(bf16[32,16,128]{2,1,0:T(8,128)(2,1)} %bitcast), calls=%async_computation.1 | async-start | bytes 262144 | tf_op jit(solution)/shard_map/all_to_all | solution.py:909
  28.3 6.3 %collective-permute-start.2 = (bf16[4,64,512]{2,1,0:T(8,128)(2,1)S(1)}, bf16[4,64,512]{2,1,0:T(8,128)(2,1)S(1)}, u32[]{:S(2)}, u32[]{:S(2)}) collective-permute-start(bf16[4,64,512]{2,1,0:T(8,128)(2,1)S(1)} %send.1), channel_id=1, source_target_pairs={{0,16},{16,0},{1,17},{17,1},{2,18},{18,2},{3,19},{19,3},{4,20},{20... | collective-permute-start | bytes 786440 | tf_op jit(solution)/shard_map/ppermute | solution.py:918

commit v7 on v6

--- a/solution.py
+++ b/solution.py
@@ -44,13 +44,6 @@
 
 def lanes_from(x, source):
     return jnp.take_along_axis(x, source, axis=1, mode="promise_in_bounds")
-
-
-def split(x):
-    high = x.astype(BF16)
-    rest = x - high.astype(F32)
-    mid = rest.astype(BF16)
-    return high, mid, (rest - mid.astype(F32)).astype(BF16)
 
 
 class Sizes:
@@ -76,11 +69,6 @@
     k = (t * 205) >> 10
     l = t - 5 * k
     return (3 * k + (l >> 1)) * 8 + 2 * c + (l & 1), o
-
-
-def tap_onehot():
-    target, _ = tap_target(iota((1, NK), 1))
-    return hot(iota((128, NK), 0) == target)
 
 
 def row_target(z, row):
@@ -716,7 +704,7 @@
 
 def keep_kernel(
     z, grad, code, in_mask, weights, aux, moments,
-    pixels_out, onehot_out, mean_out, cov_out,
+    pixels_out, mean_out, cov_out,
     sh, mine, means, covs, sems,
 ):
     section = lax.axis_index("section")
@@ -735,7 +723,6 @@
     ]
     for copy in copies:
         copy.start()
-    onehot_out[...] = tap_onehot()
     for copy in copies:
         copy.wait()
 
@@ -745,7 +732,7 @@
 
 
 def finish_kernel(
-    z, sums, arrived, onehot, half_done, pixels_out, kernel_out, enc_out, dec_out,
+    z, sums, arrived, half_done, pixels_out, kernel_out, enc_out, dec_out,
     kernels, encs, decs, sems,
 ):
     there = z.micro - z.mb - lax.axis_index("section") * z.mb
@@ -762,10 +749,19 @@
     ]
     copies[0].start()
     total = sums[...]
-    chosen = dot(jnp.concatenate(split(total), axis=0), onehot[...])
-    chosen = chosen[0:16] + chosen[16:32] + chosen[32:48]
-    _, o = tap_target(iota((1, NK), 1))
-    kernels[...] = jnp.sum(jnp.where(iota((16, NK), 0) == o, chosen, 0.0), axis=0, keepdims=True)
+    taps = CIN * KS * KS
+    tap = (iota((CCODE, 128), 1) - taps * iota((CCODE, 128), 0)) & 127
+    slot, _ = tap_target(jnp.minimum(tap, taps - 1))
+    moved = lanes_from(total, slot)
+    place = iota((1, 128), 1)
+    for chunk in range((NK + 127) // 128):
+        out = jnp.zeros((1, 128), F32)
+        for o in range(CCODE):
+            start = o * taps - chunk * 128
+            if -taps < start < 128:
+                out = jnp.where((place >= start) & (place < start + taps), moved[o : o + 1], out)
+        width = min(128, NK - chunk * 128)
+        kernels[:, chunk * 128 : chunk * 128 + width] = out[:, 0:width]
     copies[3].start()
     lane = iota((16, 128), 1)
     row = iota((16, 128), 0)
@@ -916,12 +912,11 @@
             cost=heavy,
         )(grad, code, in_mask, weights, aux)
         arrived = lax.ppermute(sending, "section", swap)
-        half_done, onehot, new_mean, new_cov = call(
+        half_done, new_mean, new_cov = call(
             keep_kernel,
             "keep",
             [
                 shape(1, z.micro, z.band, z.span),
-                shape(128, NK),
                 shape(1, CCODE, dtype=F32),
                 shape(CCODE, CCODE, dtype=F32),
             ],
@@ -933,7 +928,7 @@
                 pltpu.VMEM((CCODE, CCODE), F32),
                 DMA((3,)),
             ],
-            out_specs=[HBM, VMEM, HBM, HBM],
+            out_specs=[HBM] * 3,
             cost=heavy,
         )(grad, code, in_mask, weights, aux, moments)
         (sums,) = call(
@@ -953,7 +948,7 @@
                 shape(1, CCODE, dtype=F32),
                 shape(1, CIN, dtype=F32),
             ],
-            [VMEM] * 3 + [HBM],
+            [VMEM] * 2 + [HBM],
             [
                 pltpu.VMEM((1, NK), F32),
                 pltpu.VMEM((1, CCODE), F32),
@@ -961,8 +956,8 @@
                 DMA((4,)),
             ],
             out_specs=[HBM] * 4,
-            alias={3: 0},
-        )(sums, arrived, onehot, half_done)
+            alias={2: 0},
+        )(sums, arrived, half_done)
         return (
             pixels_out,
             kernel_grads,

time: 35.7 us -> 35.6 us (level)
  no operation moved by 1% of the time
where the time goes in v7:
time: 35.6 us; the launch traced here: 35.3 us
  Pallas kernels  12.8 us (36%)
  starting transfers between devices  11.3 us (32%)
  waiting for transfers between devices  9.13 us (26%)
  local copies, waits for them, and re-layouts  1.31 us (4%)
  between operations  0.76 us (2%)
    all_to_all x1, starting transfers between devices, run(): stats = lax.all_to_all(pay, ('section', 'wide'), 0, 0)  5.56 us
    all_to_all x1, waiting for transfers between devices, run(): stats = lax.all_to_all(pay, ('section', 'wide'), 0, 0)  5.07 us
    all_to_all x1, waiting for transfers between devices, run(): parts = lax.all_to_all(pay, ('section', 'wide'), 0, 0)  3.7 us
    ppermute x1, starting transfers between devices, run(): halo = lax.ppermute(halo, 'wide', pair)  3 us
    all_to_all x1, starting transfers between devices, run(): parts = lax.all_to_all(pay, ('section', 'wide'), 0, 0)  2.57 us
    pallas_call x1, Pallas kernels, run(): call(keep_kernel, 'keep', [shape(1, z.micro, z.band, z.span), shape(1, CC...  2.38 us
    pallas_call x1, Pallas kernels, run(): call(decode_kernel, 'decode', [shape(*frame), shape(CCODE, 128, dtype=F32...  2.12 us
    pallas_call x1, Pallas kernels, run(): call(send_kernel, 'send', [shape(z.mb, z.band, z.span)], [VMEM] * 5, [fra...  1.64 us
  transfers between devices with their start and end apart: 5, of which 3 were waited for; matrix products, arithmetic and copies ran while one was open for 0% of the time, Pallas kernels for 20%

profile of v7, /device:TPU:0, one launch (start us, length us, event | category | flops | bytes accessed | tf_op | source)
XLA Modules:
  0.0 35.3 jit_solution(7596749073436657431)
XLA Ops:
  0.6 0.0 copy-start.2
  0.6 0.0 copy-start
  0.7 1.1 %edge.1 = (bf16[208,128]{1,0:T(8,128)(2,1)S(1)}, bf16[32,1600]{1,0:T(8,128)(2,1)S(1)}) custom-call(bf16[8,64,512]{2,1,0:T(8,128)(2,1)} %refs_0_.4, s32[8,64,128]{2,1,0:T(8,128)} %refs_1_.3, bf16[8,64,512]{2,1,0:T(8,128)(2,1)} %refs_0_.5, bf16[1,1600]{1,0:T(2,128)(2,1)} %refs_3_.3), custom_call_target="tpu_custom_call" | custom-call | tf_op jit(solution)/shard_map/edge/pallas_call | solution.py:827
  1.7 3.0 %collective-permute-start = (bf16[208,128]{1,0:T(8,128)(2,1)S(1)}, bf16[208,128]{1,0:T(8,128)(2,1)S(1)}, u32[]{:S(2)}, u32[]{:S(2)}) collective-permute-start(bf16[208,128]{1,0:T(8,128)(2,1)S(1)} %get-tuple-element.35), channel_id=1, source_target_pairs={{0,1},{1,0},{2,3},{3,2},{4,5},{5,4},{6,7},{7,6},{8,9},{9,8},{10,11... | collective-permute-start | bytes 159752 | tf_op jit(solution)/shard_map/ppermute | solution.py:840
  4.8 0.0 collective-permute-start.1
  4.8 0.0 copy-done.2
  4.8 0.0 copy-done
  4.8 0.9 %prepare.1 = (bf16[256,640]{1,0:T(8,128)(2,1)S(1)}, bf16[256,640]{1,0:T(8,128)(2,1)S(1)}, f32[56,128]{1,0:T(8,128)S(1)}) custom-call(bf16[8,64,512]{2,1,0:T(8,128)(2,1)S(1)} %copy-done, s32[8,64,128]{2,1,0:T(8,128)S(1)} %copy-done.2, s32[8,8]{1,0:T(8,128)} %refs_2_.2, f32[16]{0:T(128)} %refs_3_.2, f32[4]{0:T(128)} %refs_4_.1, f32[16]{0:T(128)} %refs_5_.1, ...), custom_call_target="tpu_custom_call" | custom-call | flops 4000000000 | bytes 4000000 | tf_op jit(solution)/shard_map/prepare/pallas_call | solution.py:842
  5.7 0.4 collective-permute-done.1.refs_1_
  6.1 0.3 taps.1.refs_2_.refs_4_.refs_3_
  6.4 1.2 %inner.1 = (bf16[5,144,640]{2,1,0:T(8,128)(2,1)S(1)}, bf16[5,144,256]{2,1,0:T(8,128)(2,1)S(1)}, f32[5,144,256]{2,1,0:T(8,128)S(1)}, f32[2,128]{1,0:T(2,128)S(1)}, bf16[640,256]{1,0:T(8,128)(2,1)S(1)}) custom-call(bf16[256,640]{1,0:T(8,128)(2,1)S(1)} %get-tuple-element.33.refs_0_, bf16[256,640]{1,0:T(8,128)(2,1)S(1)} %get-tuple-element.34.refs_1_.refs_2_, ...), custom_call_target="tpu_custom_call" | custom-call | flops 4000000000 | bytes 4000000 | tf_op jit(solution)/shard_map/inner/pallas_call | solution.py:865
  7.7 0.0 collective-permute-done.refs_2_
  7.7 0.0 copy-start.1
  7.7 0.9 %encode.1 = (bf16[5,144,640]{2,1,0:T(8,128)(2,1)S(1)}, bf16[5,144,256]{2,1,0:T(8,128)(2,1)S(1)}, f32[5,144,256]{2,1,0:T(8,128)S(1)}, bf16[32,640]{1,0:T(8,128)(2,1)S(1)}, f32[2,128]{1,0:T(2,128)S(1)}) custom-call(bf16[256,640]{1,0:T(8,128)(2,1)S(1)} %get-tuple-element.33.refs_0_, ...), custom_call_target="tpu_custom_call", output_to_operand_aliasing={{0}: (6, {}), {1}: (7, {}), {2}: (8, {})} | custom-call | tf_op jit(solution)/shard_map/encode/pallas_call | solution.py:873
  8.6 0.6 %broadcast_in_dim.4 = f32[32,2,128]{2,1,0:T(2,128)} broadcast(f32[2,128]{1,0:T(2,128)S(1)} %get-tuple-element.43), dimensions={1,2} | broadcast | bytes 33792 | tf_op jit(solution)/shard_map/broadcast_in_dim | solution.py:881
  9.2 5.6 %all-to-all-start = ((f32[32,2,128]{2,1,0:T(2,128)}), f32[32,2,128]{2,1,0:T(2,128)S(1)}, u32[]{:S(2)}, u32[]{:S(2)}) async-start(f32[32,2,128]{2,1,0:T(2,128)} %broadcast_in_dim.4), calls=%async_computation | async-start | bytes 65536 | tf_op jit(solution)/shard_map/all_to_all | solution.py:882
  14.8 0.0 copy-done.1
  14.8 2.1 %decode.1 = (bf16[5,144,256]{2,1,0:T(8,128)(2,1)S(1)}, f32[16,128]{1,0:T(8,128)S(1)}) custom-call(bf16[8,64,512]{2,1,0:T(8,128)(2,1)S(1)} %copy-done.1, bf16[5,144,256]{2,1,0:T(8,128)(2,1)S(1)} %get-tuple-element.44.refs_1_, bf16[256,640]{1,0:T(8,128)(2,1)S(1)} %get-tuple-element.34.refs_1_.refs_2_, bf16[32,640]{1,0:T(8,128)(2,1)S(1)} %get-tuple-element.46.refs_3_, ...), custom_call_target="tpu_custom_call" | custom-call | flops 4000000000 | bytes 4000000 | tf_op jit(solution)/shard_map/decode/pallas_call | solution.py:883
  16.9 5.1 %all-to-all-done.refs_0_ = f32[32,2,128]{2,1,0:T(2,128)S(1)} async-done(((f32[32,2,128]{2,1,0:T(2,128)}), f32[32,2,128]{2,1,0:T(2,128)S(1)}, u32[]{:S(2)}, u32[]{:S(2)}) %all-to-all-start) | async-done | bytes 32800 | tf_op jit(solution)/shard_map/all_to_all | solution.py:882
  22.0 1.4 %whiten.1 = (bf16[5,144,256]{2,1,0:T(8,128)(2,1)S(1)}, bf16[2,16,128]{2,1,0:T(8,128)(2,1)S(1)}, f32[24,128]{1,0:T(8,128)S(1)}) custom-call(f32[32,2,128]{2,1,0:T(2,128)S(1)} %all-to-all-done.refs_0_, bf16[5,144,256]{2,1,0:T(8,128)(2,1)S(1)} %get-tuple-element.44.refs_1_, ...), custom_call_target="tpu_custom_call", output_to_operand_aliasing={{0}: (3, {})} | custom-call | tf_op jit(solution)/shard_map/whiten/pallas_call | solution.py:891
  23.4 0.7 %broadcast_in_dim.5 = bf16[2,16,16,128]{3,2,1,0:T(8,128)(2,1)} broadcast(bf16[2,16,128]{2,1,0:T(8,128)(2,1)S(1)} %get-tuple-element.50), dimensions={0,2,3} | broadcast | bytes 139264 | tf_op jit(solution)/shard_map/broadcast_in_dim | solution.py:903
  24.0 2.6 %all-to-all-start.1 = ((bf16[32,16,128]{2,1,0:T(8,128)(2,1)}), bf16[32,16,128]{2,1,0:T(8,128)(2,1)S(1)}, u32[]{:S(2)}, u32[]{:S(2)}) async-start(bf16[32,16,128]{2,1,0:T(8,128)(2,1)} %bitcast), calls=%async_computation.1 | async-start | bytes 262144 | tf_op jit(solution)/shard_map/all_to_all | solution.py:905
  26.6 1.6 %send.1 = bf16[4,64,512]{2,1,0:T(8,128)(2,1)S(1)} custom-call(bf16[5,144,256]{2,1,0:T(8,128)(2,1)S(1)} %get-tuple-element.51.refs_0_, bf16[5,144,256]{2,1,0:T(8,128)(2,1)S(1)} %get-tuple-element.44.refs_1_, bf16[256,640]{1,0:T(8,128)(2,1)S(1)} %get-tuple-element.34.refs_1_.refs_2_, bf16[128,512]{1,0:T(8,128)(2,1)S(1)} %taps.1.refs_2_.refs_4_.refs_3_, ...), custom_call_target="tpu_custom_call" | custom-call | flops 4000000000 | bytes 4000000 | tf_op jit(solution)/shard_map/send/pallas_call | solution.py:906
  28.3 0.2 collective-permute-start.2
  28.4 2.4 %keep.1 = (bf16[1,8,64,512]{3,2,1,0:T(8,128)(2,1)}, f32[1,16]{1,0:T(1,128)}, f32[16,16]{1,0:T(8,128)}) custom-call(bf16[5,144,256]{2,1,0:T(8,128)(2,1)S(1)} %get-tuple-element.51.refs_0_, bf16[5,144,256]{2,1,0:T(8,128)(2,1)S(1)} %get-tuple-element.44.refs_1_, bf16[256,640]{1,0:T(8,128)(2,1)S(1)} %get-tuple-element.34.refs_1_.refs_2_, ...), custom_call_target="tpu_custom_call" | custom-call | flops 4000000000 | bytes 4000000 | tf_op jit(solution)/shard_map/keep/pallas_call | solution.py:915
  30.8 3.7 %all-to-all-done.1.refs_0_ = bf16[32,16,128]{2,1,0:T(8,128)(2,1)S(1)} async-done(((bf16[32,16,128]{2,1,0:T(8,128)(2,1)}), bf16[32,16,128]{2,1,0:T(8,128)(2,1)S(1)}, u32[]{:S(2)}, u32[]{:S(2)}) %all-to-all-start.1) | async-done | bytes 131104 | tf_op jit(solution)/shard_map/all_to_all | solution.py:905
  34.6 0.0 collective-permute-done.2.refs_1_
  34.6 0.8 %finish.1 = (bf16[1,8,64,512]{3,2,1,0:T(8,128)(2,1)}, f32[1,1600]{1,0:T(1,128)}, f32[1,16]{1,0:T(1,128)}, f32[1,4]{1,0:T(1,128)}) custom-call(f32[16,128]{1,0:T(8,128)S(1)} %total.1.refs_0_, bf16[4,64,512]{2,1,0:T(8,128)(2,1)S(1)} %collective-permute-done.2.refs_1_, bf16[1,8,64,512]{3,2,1,0:T(8,128)(2,1)} %get-tuple-element.53.refs_2_), custom_call_target="tpu_custom_call", output_to_operand_aliasing={{0}: (2, {})} | custom-call | tf_op jit(solution)/shard_map/finish/pallas_call | solution.py:942
  (1 shorter events, 0.0 us)
Async XLA Ops:
  0.6 4.1 %copy-start.2 = (s32[8,64,128]{2,1,0:T(8,128)S(1)}, s32[8,64,128]{2,1,0:T(8,128)}, u32[]{:S(2)}) copy-start(s32[8,64,128]{2,1,0:T(8,128)} %refs_1_.3) | copy-start | bytes 786436
  0.6 4.1 %copy-start = (bf16[8,64,512]{2,1,0:T(8,128)(2,1)S(1)}, bf16[8,64,512]{2,1,0:T(8,128)(2,1)}, u32[]{:S(2)}) copy-start(bf16[8,64,512]{2,1,0:T(8,128)(2,1)} %refs_0_.4) | copy-start | bytes 1572868
  1.7 5.9 %collective-permute-start = (bf16[208,128]{1,0:T(8,128)(2,1)S(1)}, bf16[208,128]{1,0:T(8,128)(2,1)S(1)}, u32[]{:S(2)}, u32[]{:S(2)}) collective-permute-start(bf16[208,128]{1,0:T(8,128)(2,1)S(1)} %get-tuple-element.35), channel_id=1, source_target_pairs={{0,1},{1,0},{2,3},{3,2},{4,5},{5,4},{6,7},{7,6},{8,9},{9,8},{10,11... | collective-permute-start | bytes 159752 | tf_op jit(solution)/shard_map/ppermute | solution.py:840
  4.8 1.3 %collective-permute-start.1 = (bf16[32,1600]{1,0:T(8,128)(2,1)S(1)}, bf16[32,1600]{1,0:T(8,128)(2,1)S(1)}, u32[]{:S(2)}, u32[]{:S(2)}) collective-permute-start(bf16[32,1600]{1,0:T(8,128)(2,1)S(1)} %get-tuple-element.36.refs_0_), channel_id=1, source_target_pairs={{0,16},{16,0},{1,17},{17,1},{2,18},{18,2},{3,19},{19,3},{4,20},{20... | collective-permute-start | bytes 307208 | tf_op jit(solution)/shard_map/ppermute | solution.py:841
  7.7 7.1 %copy-start.1 = (bf16[8,64,512]{2,1,0:T(8,128)(2,1)S(1)}, bf16[8,64,512]{2,1,0:T(8,128)(2,1)}, u32[]{:S(2)}) copy-start(bf16[8,64,512]{2,1,0:T(8,128)(2,1)} %refs_0_.5) | copy-start | bytes 1572868
  9.2 12.8 %all-to-all-start = ((f32[32,2,128]{2,1,0:T(2,128)}), f32[32,2,128]{2,1,0:T(2,128)S(1)}, u32[]{:S(2)}, u32[]{:S(2)}) async-start(f32[32,2,128]{2,1,0:T(2,128)} %broadcast_in_dim.4), calls=%async_computation | async-start | bytes 65536 | tf_op jit(solution)/shard_map/all_to_all | solution.py:882
  24.0 10.5 %all-to-all-start.1 = ((bf16[32,16,128]{2,1,0:T(8,128)(2,1)}), bf16[32,16,128]{2,1,0:T(8,128)(2,1)S(1)}, u32[]{:S(2)}, u32[]{:S(2)}) async-start(bf16[32,16,128]{2,1,0:T(8,128)(2,1)} %bitcast), calls=%async_computation.1 | async-start | bytes 262144 | tf_op jit(solution)/shard_map/all_to_all | solution.py:905
  28.3 6.3 %collective-permute-start.2 = (bf16[4,64,512]{2,1,0:T(8,128)(2,1)S(1)}, bf16[4,64,512]{2,1,0:T(8,128)(2,1)S(1)}, u32[]{:S(2)}, u32[]{:S(2)}) collective-permute-start(bf16[4,64,512]{2,1,0:T(8,128)(2,1)S(1)} %send.1), channel_id=1, source_target_pairs={{0,16},{16,0},{1,17},{17,1},{2,18},{18,2},{3,19},{19,3},{4,20},{20... | collective-permute-start | bytes 786440 | tf_op jit(solution)/shard_map/ppermute | solution.py:914

commit v8 on v7

--- a/solution.py
+++ b/solution.py
@@ -14,7 +14,8 @@
 NB = 5
 HALO = 8
 NK = CCODE * CIN * KS * KS
-COPIES = 32
+COPIES = 16
+PADDED = NK + 192
 
 decay_rate = 0.9
 whiten_weight = 0.25
@@ -335,7 +336,9 @@
         copy.start()
     for copy in copies:
         copy.wait()
-    kernel_out[...] = jnp.broadcast_to(kernel_buf[...].astype(F32), (COPIES, NK)).astype(BF16)
+    kernel_row = kernel_buf[...].astype(F32)
+    kernel_out[:, 0:NK] = jnp.broadcast_to(kernel_row, (COPIES, NK)).astype(BF16)
+    kernel_out[:, NK:] = jnp.zeros((COPIES, PADDED - NK), BF16)
 
     def beside(buf):
         rows = buf[...].astype(F32)
@@ -421,7 +424,7 @@
 
 
 def taps_kernel(z, kernel_own, kernel_other, weights_out):
-    mine, other = (x[0:16].astype(F32)[0:1] for x in (kernel_own, kernel_other))
+    mine, other = (x[:, 0:NK].astype(F32)[0:1] for x in (kernel_own, kernel_other))
     leads = lax.axis_index("section") == 0
     weights_out[...] = spread_taps((jnp.where(leads, mine, other), jnp.where(leads, other, mine)))
 
@@ -501,7 +504,7 @@
 
 def encode_kernel(
     z, pixels, own_mask, halo, banded, aux, inner_pay, taps_in, code_in, slope_in,
-    taps_out, code_out, slope_out, cot_out, pay_out,
+    taps_out, code_out, slope_out, pay_out,
     sh,
 ):
     odd = lax.rem(lax.axis_index("wide"), 2)
@@ -510,12 +513,9 @@
     channel_ok = jnp.tile(aux[40:56], (1, NB))
     middle, end = CIN * z.halo, CIN * (z.halo + z.near)
     halo_mask = dot(halo[end : z.sent, :], window_mask_columns())
-    halo_rows = [
-        jnp.concatenate([halo[i : i + count, :] for i in range(start, stop, count)], axis=1)
-        for start, stop, count in ((0, middle, z.halo), (middle, end, z.near))
-    ]
-    halo_pixels = dot(jnp.concatenate(halo_rows, axis=0), window_columns())
-    halo_x = halo_pixels[0 : z.halo] * jnp.tile(channel_ok, (2, 1))
+    halo_rows = [halo[i : i + z.halo, :] for i in range(0, middle, z.halo)]
+    halo_pixels = dot(jnp.concatenate(halo_rows, axis=1), window_columns())
+    halo_x = halo_pixels * jnp.tile(channel_ok, (2, 1))
     zeros = jnp.zeros((NB, 16, 256), F32)
     sh[:, 0:16, :] = zeros
     sh[:, 48:64, :] = zeros
@@ -547,16 +547,10 @@
         rs = slice(b * count, b * count + count)
         code_out[b, pl.ds(start, count), :] = code[rs].astype(BF16)
         slope_out[b, pl.ds(start, count), :] = slope[rs]
-    near = halo_pixels[z.halo : z.halo + z.near] * channel_ok
-    nothing = jnp.zeros((8, NB * 128), F32)
-    for h in range(2):
-        rows = near[h * 8 : h * 8 + 8]
-        rows = [jnp.where(odd == 1, nothing, rows), jnp.where(odd == 1, rows, nothing)]
-        cot_out[h * 16 : h * 16 + 16, :] = jnp.concatenate(rows, axis=0).astype(BF16)
 
 
 def decode_kernel(
-    z, cotangent, code, in_mask, halo_cot, weights, aux,
+    z, cotangent, code, in_mask, halo, weights, aux,
     sent_out, pay_out,
     sh, cot_frame,
 ):
@@ -568,8 +562,19 @@
     raws = spread(z, sh, banded)
     gather = gather_rows(z)
     columns = window_columns()
-    own_cot = dot(dot(gather, cotangent[mine].reshape(z.own, z.span)).astype(BF16), columns)
-    put_pixels(z, cot_frame, odd, own_cot * in_mask[...].astype(F32), halo_cot[...].astype(F32))
+    own_cot = dot(gather, cotangent[mine].reshape(z.own, z.span)).astype(BF16)
+    near = [
+        halo[i : i + z.near, :] for i in range(CIN * z.halo, CIN * (z.halo + z.near), z.near)
+    ]
+    cots = dot(jnp.concatenate([own_cot, jnp.concatenate(near, axis=1)], axis=0), columns)
+    near = cots[z.own : z.own + z.near] * jnp.tile(aux[40:56], (1, NB))
+    nothing = jnp.zeros((8, NB * 128), F32)
+    beside = []
+    for h in range(2):
+        part = near[h * 8 : h * 8 + 8]
+        beside += [jnp.where(odd == 1, nothing, part), jnp.where(odd == 1, part, nothing)]
+    own_cot = cots[0 : z.own] * in_mask[...].astype(F32)
+    put_pixels(z, cot_frame, odd, own_cot, jnp.concatenate(beside, axis=0))
     mine_rows = own_rows(z, odd)
     u_local = (iota((1, 128), 1) >> 3) & (UW - 1)
     inner = mine_rows & (u_local >= 1) & (u_local <= UW - 2)
@@ -827,7 +832,7 @@
         halo, kernel_own = call(
             edge_kernel,
             "edge",
-            [shape(z.sent, HW), shape(COPIES, NK)],
+            [shape(z.sent, HW), shape(COPIES, PADDED)],
             [HBM] * 4,
             [
                 edge_buf,
@@ -870,10 +875,10 @@
             [pltpu.VMEM((NB, z.own // 2 + 16, 256), F32)],
             cost=heavy,
         )(pixels, in_mask, weights, aux)
-        taps, code, slope, halo_cot, pay = call(
+        taps, code, slope, pay = call(
             encode_kernel,
             "encode",
-            coded + [shape(z.halo, NB * 128), shape(2, 128, dtype=F32)],
+            coded + [shape(2, 128, dtype=F32)],
             [VMEM] * 9,
             [pltpu.VMEM((NB, 64, 256), F32)],
             alias={6: 0, 7: 1, 8: 2},
@@ -887,7 +892,7 @@
             [VMEM] * 6,
             [framed, framed],
             cost=heavy,
-        )(whole[2], code, in_mask, halo_cot, weights, aux)
+        )(whole[2], code, in_mask, halo, weights, aux)
         grad, pay, moments = call(
             whiten_kernel,
             "whiten",

time: 35.6 us -> 35.6 us (level)
  no operation moved by 1% of the time
where the time goes in v8:
time: 35.6 us; the launch traced here: 35.3 us
  Pallas kernels  12.8 us (36%)
  starting transfers between devices  11.4 us (32%)
  waiting for transfers between devices  9.07 us (25%)
  local copies, waits for them, and re-layouts  1.31 us (4%)
  between operations  0.76 us (2%)
    all_to_all x1, starting transfers between devices, run(): stats = lax.all_to_all(pay, ('section', 'wide'), 0, 0)  5.63 us
    all_to_all x1, waiting for transfers between devices, run(): stats = lax.all_to_all(pay, ('section', 'wide'), 0, 0)  5.08 us
    all_to_all x1, waiting for transfers between devices, run(): parts = lax.all_to_all(pay, ('section', 'wide'), 0, 0)  3.7 us
    ppermute x1, starting transfers between devices, run(): halo = lax.ppermute(halo, 'wide', pair)  3 us
    all_to_all x1, starting transfers between devices, run(): parts = lax.all_to_all(pay, ('section', 'wide'), 0, 0)  2.57 us
    pallas_call x1, Pallas kernels, run(): call(keep_kernel, 'keep', [shape(1, z.micro, z.band, z.span), shape(1, CC...  2.38 us
    pallas_call x1, Pallas kernels, run(): call(decode_kernel, 'decode', [shape(*frame), shape(CCODE, 128, dtype=F32...  2.11 us
    pallas_call x1, Pallas kernels, run(): call(send_kernel, 'send', [shape(z.mb, z.band, z.span)], [VMEM] * 5, [fra...  1.64 us
  transfers between devices with their start and end apart: 5, of which 3 were waited for; matrix products, arithmetic and copies ran while one was open for 0% of the time, Pallas kernels for 20%

profile of v8, /device:TPU:0, one launch (start us, length us, event | category | flops | bytes accessed | tf_op | source)
XLA Modules:
  0.0 35.3 jit_solution(12817012478649110903)
XLA Ops:
  0.6 0.0 copy-start.2
  0.6 0.0 copy-start
  0.7 1.1 %edge.1 = (bf16[208,128]{1,0:T(8,128)(2,1)S(1)}, bf16[16,1792]{1,0:T(8,128)(2,1)S(1)}) custom-call(bf16[8,64,512]{2,1,0:T(8,128)(2,1)} %refs_0_.4, s32[8,64,128]{2,1,0:T(8,128)} %refs_1_.3, bf16[8,64,512]{2,1,0:T(8,128)(2,1)} %refs_0_.5, bf16[1,1600]{1,0:T(2,128)(2,1)} %refs_3_.3), custom_call_target="tpu_custom_call" | custom-call | tf_op jit(solution)/shard_map/edge/pallas_call | solution.py:832
  1.7 3.0 %collective-permute-start = (bf16[208,128]{1,0:T(8,128)(2,1)S(1)}, bf16[208,128]{1,0:T(8,128)(2,1)S(1)}, u32[]{:S(2)}, u32[]{:S(2)}) collective-permute-start(bf16[208,128]{1,0:T(8,128)(2,1)S(1)} %get-tuple-element.34), channel_id=1, source_target_pairs={{0,1},{1,0},{2,3},{3,2},{4,5},{5,4},{6,7},{7,6},{8,9},{9,8},{10,11... | collective-permute-start | bytes 159752 | tf_op jit(solution)/shard_map/ppermute | solution.py:845
  4.8 0.0 collective-permute-start.1
  4.8 0.0 copy-done.2
  4.8 0.0 copy-done
  4.8 0.9 %prepare.1 = (bf16[256,640]{1,0:T(8,128)(2,1)S(1)}, bf16[256,640]{1,0:T(8,128)(2,1)S(1)}, f32[56,128]{1,0:T(8,128)S(1)}) custom-call(bf16[8,64,512]{2,1,0:T(8,128)(2,1)S(1)} %copy-done, s32[8,64,128]{2,1,0:T(8,128)S(1)} %copy-done.2, s32[8,8]{1,0:T(8,128)} %refs_2_.2, f32[16]{0:T(128)} %refs_3_.2, f32[4]{0:T(128)} %refs_4_.1, f32[16]{0:T(128)} %refs_5_.1, ...), custom_call_target="tpu_custom_call" | custom-call | flops 4000000000 | bytes 4000000 | tf_op jit(solution)/shard_map/prepare/pallas_call | solution.py:847
  5.7 0.3 collective-permute-done.1.refs_1_
  6.0 0.3 taps.1.refs_2_.refs_4_.refs_3_
  6.3 1.2 %inner.1 = (bf16[5,144,640]{2,1,0:T(8,128)(2,1)S(1)}, bf16[5,144,256]{2,1,0:T(8,128)(2,1)S(1)}, f32[5,144,256]{2,1,0:T(8,128)S(1)}, f32[2,128]{1,0:T(2,128)S(1)}, bf16[640,256]{1,0:T(8,128)(2,1)S(1)}) custom-call(bf16[256,640]{1,0:T(8,128)(2,1)S(1)} %get-tuple-element.32.refs_0_, bf16[256,640]{1,0:T(8,128)(2,1)S(1)} %get-tuple-element.33.refs_1_.refs_2_, ...), custom_call_target="tpu_custom_call" | custom-call | flops 4000000000 | bytes 4000000 | tf_op jit(solution)/shard_map/inner/pallas_call | solution.py:870
  7.6 0.0 collective-permute-done.refs_2_.refs_3_
  7.6 0.0 copy-start.1
  7.6 0.9 %encode.1 = (bf16[5,144,640]{2,1,0:T(8,128)(2,1)S(1)}, bf16[5,144,256]{2,1,0:T(8,128)(2,1)S(1)}, f32[5,144,256]{2,1,0:T(8,128)S(1)}, f32[2,128]{1,0:T(2,128)S(1)}) custom-call(bf16[256,640]{1,0:T(8,128)(2,1)S(1)} %get-tuple-element.32.refs_0_, ...), custom_call_target="tpu_custom_call", output_to_operand_aliasing={{0}: (6, {}), {1}: (7, {}), {2}: (8, {})} | custom-call | tf_op jit(solution)/shard_map/encode/pallas_call | solution.py:878
  8.5 0.6 %broadcast_in_dim.4 = f32[32,2,128]{2,1,0:T(2,128)} broadcast(f32[2,128]{1,0:T(2,128)S(1)} %get-tuple-element.42), dimensions={1,2} | broadcast | bytes 33792 | tf_op jit(solution)/shard_map/broadcast_in_dim | solution.py:886
  9.1 5.6 %all-to-all-start = ((f32[32,2,128]{2,1,0:T(2,128)}), f32[32,2,128]{2,1,0:T(2,128)S(1)}, u32[]{:S(2)}, u32[]{:S(2)}) async-start(f32[32,2,128]{2,1,0:T(2,128)} %broadcast_in_dim.4), calls=%async_computation | async-start | bytes 65536 | tf_op jit(solution)/shard_map/all_to_all | solution.py:887
  14.8 0.0 copy-done.1
  14.8 2.1 %decode.1 = (bf16[5,144,256]{2,1,0:T(8,128)(2,1)S(1)}, f32[16,128]{1,0:T(8,128)S(1)}) custom-call(bf16[8,64,512]{2,1,0:T(8,128)(2,1)S(1)} %copy-done.1, bf16[5,144,256]{2,1,0:T(8,128)(2,1)S(1)} %get-tuple-element.43.refs_1_, bf16[256,640]{1,0:T(8,128)(2,1)S(1)} %get-tuple-element.33.refs_1_.refs_2_, ...), custom_call_target="tpu_custom_call" | custom-call | flops 4000000000 | bytes 4000000 | tf_op jit(solution)/shard_map/decode/pallas_call | solution.py:888
  16.9 5.1 %all-to-all-done.refs_0_ = f32[32,2,128]{2,1,0:T(2,128)S(1)} async-done(((f32[32,2,128]{2,1,0:T(2,128)}), f32[32,2,128]{2,1,0:T(2,128)S(1)}, u32[]{:S(2)}, u32[]{:S(2)}) %all-to-all-start) | async-done | bytes 32800 | tf_op jit(solution)/shard_map/all_to_all | solution.py:887
  22.0 1.4 %whiten.1 = (bf16[5,144,256]{2,1,0:T(8,128)(2,1)S(1)}, bf16[2,16,128]{2,1,0:T(8,128)(2,1)S(1)}, f32[24,128]{1,0:T(8,128)S(1)}) custom-call(f32[32,2,128]{2,1,0:T(2,128)S(1)} %all-to-all-done.refs_0_, bf16[5,144,256]{2,1,0:T(8,128)(2,1)S(1)} %get-tuple-element.43.refs_1_, ...), custom_call_target="tpu_custom_call", output_to_operand_aliasing={{0}: (3, {})} | custom-call | tf_op jit(solution)/shard_map/whiten/pallas_call | solution.py:896
  23.3 0.7 %broadcast_in_dim.5 = bf16[2,16,16,128]{3,2,1,0:T(8,128)(2,1)} broadcast(bf16[2,16,128]{2,1,0:T(8,128)(2,1)S(1)} %get-tuple-element.48), dimensions={0,2,3} | broadcast | bytes 139264 | tf_op jit(solution)/shard_map/broadcast_in_dim | solution.py:908
  24.0 2.6 %all-to-all-start.1 = ((bf16[32,16,128]{2,1,0:T(8,128)(2,1)}), bf16[32,16,128]{2,1,0:T(8,128)(2,1)S(1)}, u32[]{:S(2)}, u32[]{:S(2)}) async-start(bf16[32,16,128]{2,1,0:T(8,128)(2,1)} %bitcast), calls=%async_computation.1 | async-start | bytes 262144 | tf_op jit(solution)/shard_map/all_to_all | solution.py:910
  26.6 1.6 %send.1 = bf16[4,64,512]{2,1,0:T(8,128)(2,1)S(1)} custom-call(bf16[5,144,256]{2,1,0:T(8,128)(2,1)S(1)} %get-tuple-element.49.refs_0_, bf16[5,144,256]{2,1,0:T(8,128)(2,1)S(1)} %get-tuple-element.43.refs_1_, bf16[256,640]{1,0:T(8,128)(2,1)S(1)} %get-tuple-element.33.refs_1_.refs_2_, bf16[128,512]{1,0:T(8,128)(2,1)S(1)} %taps.1.refs_2_.refs_4_.refs_3_, ...), custom_call_target="tpu_custom_call" | custom-call | flops 4000000000 | bytes 4000000 | tf_op jit(solution)/shard_map/send/pallas_call | solution.py:911
  28.2 0.2 collective-permute-start.2
  28.4 2.4 %keep.1 = (bf16[1,8,64,512]{3,2,1,0:T(8,128)(2,1)}, f32[1,16]{1,0:T(1,128)}, f32[16,16]{1,0:T(8,128)}) custom-call(bf16[5,144,256]{2,1,0:T(8,128)(2,1)S(1)} %get-tuple-element.49.refs_0_, bf16[5,144,256]{2,1,0:T(8,128)(2,1)S(1)} %get-tuple-element.43.refs_1_, bf16[256,640]{1,0:T(8,128)(2,1)S(1)} %get-tuple-element.33.refs_1_.refs_2_, ...), custom_call_target="tpu_custom_call" | custom-call | flops 4000000000 | bytes 4000000 | tf_op jit(solution)/shard_map/keep/pallas_call | solution.py:920
  30.8 3.7 %all-to-all-done.1.refs_0_ = bf16[32,16,128]{2,1,0:T(8,128)(2,1)S(1)} async-done(((bf16[32,16,128]{2,1,0:T(8,128)(2,1)}), bf16[32,16,128]{2,1,0:T(8,128)(2,1)S(1)}, u32[]{:S(2)}, u32[]{:S(2)}) %all-to-all-start.1) | async-done | bytes 131104 | tf_op jit(solution)/shard_map/all_to_all | solution.py:910
  34.5 0.0 collective-permute-done.2.refs_1_
  34.5 0.8 %finish.1 = (bf16[1,8,64,512]{3,2,1,0:T(8,128)(2,1)}, f32[1,1600]{1,0:T(1,128)}, f32[1,16]{1,0:T(1,128)}, f32[1,4]{1,0:T(1,128)}) custom-call(f32[16,128]{1,0:T(8,128)S(1)} %total.1.refs_0_, bf16[4,64,512]{2,1,0:T(8,128)(2,1)S(1)} %collective-permute-done.2.refs_1_, bf16[1,8,64,512]{3,2,1,0:T(8,128)(2,1)} %get-tuple-element.51.refs_2_), custom_call_target="tpu_custom_call", output_to_operand_aliasing={{0}: (2, {})} | custom-call | tf_op jit(solution)/shard_map/finish/pallas_call | solution.py:947
  (1 shorter events, 0.0 us)
Async XLA Ops:
  0.6 4.1 %copy-start.2 = (s32[8,64,128]{2,1,0:T(8,128)S(1)}, s32[8,64,128]{2,1,0:T(8,128)}, u32[]{:S(2)}) copy-start(s32[8,64,128]{2,1,0:T(8,128)} %refs_1_.3) | copy-start | bytes 786436
  0.6 4.1 %copy-start = (bf16[8,64,512]{2,1,0:T(8,128)(2,1)S(1)}, bf16[8,64,512]{2,1,0:T(8,128)(2,1)}, u32[]{:S(2)}) copy-start(bf16[8,64,512]{2,1,0:T(8,128)(2,1)} %refs_0_.4) | copy-start | bytes 1572868
  1.7 5.8 %collective-permute-start = (bf16[208,128]{1,0:T(8,128)(2,1)S(1)}, bf16[208,128]{1,0:T(8,128)(2,1)S(1)}, u32[]{:S(2)}, u32[]{:S(2)}) collective-permute-start(bf16[208,128]{1,0:T(8,128)(2,1)S(1)} %get-tuple-element.34), channel_id=1, source_target_pairs={{0,1},{1,0},{2,3},{3,2},{4,5},{5,4},{6,7},{7,6},{8,9},{9,8},{10,11... | collective-permute-start | bytes 159752 | tf_op jit(solution)/shard_map/ppermute | solution.py:845
  4.8 1.2 %collective-permute-start.1 = (bf16[16,1792]{1,0:T(8,128)(2,1)S(1)}, bf16[16,1792]{1,0:T(8,128)(2,1)S(1)}, u32[]{:S(2)}, u32[]{:S(2)}) collective-permute-start(bf16[16,1792]{1,0:T(8,128)(2,1)S(1)} %get-tuple-element.35.refs_0_), channel_id=1, source_target_pairs={{0,16},{16,0},{1,17},{17,1},{2,18},{18,2},{3,19},{19,3},{4,20},{20... | collective-permute-start | bytes 172040 | tf_op jit(solution)/shard_map/ppermute | solution.py:846
  7.6 7.2 %copy-start.1 = (bf16[8,64,512]{2,1,0:T(8,128)(2,1)S(1)}, bf16[8,64,512]{2,1,0:T(8,128)(2,1)}, u32[]{:S(2)}) copy-start(bf16[8,64,512]{2,1,0:T(8,128)(2,1)} %refs_0_.5) | copy-start | bytes 1572868
  9.1 12.8 %all-to-all-start = ((f32[32,2,128]{2,1,0:T(2,128)}), f32[32,2,128]{2,1,0:T(2,128)S(1)}, u32[]{:S(2)}, u32[]{:S(2)}) async-start(f32[32,2,128]{2,1,0:T(2,128)} %broadcast_in_dim.4), calls=%async_computation | async-start | bytes 65536 | tf_op jit(solution)/shard_map/all_to_all | solution.py:887
  24.0 10.5 %all-to-all-start.1 = ((bf16[32,16,128]{2,1,0:T(8,128)(2,1)}), bf16[32,16,128]{2,1,0:T(8,128)(2,1)S(1)}, u32[]{:S(2)}, u32[]{:S(2)}) async-start(bf16[32,16,128]{2,1,0:T(8,128)(2,1)} %bitcast), calls=%async_computation.1 | async-start | bytes 262144 | tf_op jit(solution)/shard_map/all_to_all | solution.py:910
  28.2 6.3 %collective-permute-start.2 = (bf16[4,64,512]{2,1,0:T(8,128)(2,1)S(1)}, bf16[4,64,512]{2,1,0:T(8,128)(2,1)S(1)}, u32[]{:S(2)}, u32[]{:S(2)}) collective-permute-start(bf16[4,64,512]{2,1,0:T(8,128)(2,1)S(1)} %send.1), channel_id=1, source_target_pairs={{0,16},{16,0},{1,17},{17,1},{2,18},{18,2},{3,19},{19,3},{4,20},{20... | collective-permute-start | bytes 786440 | tf_op jit(solution)/shard_map/ppermute | solution.py:919

commit v9 on v8

--- a/solution.py
+++ b/solution.py
@@ -436,16 +436,16 @@
     return jnp.concatenate([up, here, down], axis=1).astype(BF16)
 
 
-def encode_rows(taps, banded, bias, masks, mine):
+def encode_rows(taps, banded, bias, masks, counted):
     code_mask = dot(masks, code_mask_lanes())
     pre = dot(taps, banded) + bias
     slope = jnp.exp(jnp.minimum(pre, 0.0))
     code = jnp.where(pre > 0, pre, slope - 1.0).astype(BF16).astype(F32)
     slope = jnp.where(code_mask > 0.5, slope, -slope)
-    allowed = code_mask if mine is None else jnp.where(mine, code_mask, 0.0)
-    weighted = code * allowed
+    allowed, seen = counted(code_mask), counted(code)
+    weighted = seen * allowed
     halves = [
-        jnp.concatenate([x[:, 0:128], x[:, 128:256]], axis=0).astype(BF16) for x in (weighted, code)
+        jnp.concatenate([x[:, 0:128], x[:, 128:256]], axis=0).astype(BF16) for x in (weighted, seen)
     ]
     second = dot(*halves, ((0,), (0,)))
     sums = [jnp.sum(x, axis=0, keepdims=True) for x in (weighted, allowed)]
@@ -494,7 +494,9 @@
     bias = jnp.concatenate([aux[8:9], aux[8:9]], axis=1)
     banded = band_weights(weights[:, 0:256])
     band_out[...] = banded
-    code, slope, pay = encode_rows(jnp.concatenate(taps, axis=0), banded, bias, masks, None)
+    code, slope, pay = encode_rows(
+        jnp.concatenate(taps, axis=0), banded, bias, masks, lambda x: x
+    )
     pay_out[...] = pay
     for b in range(NB):
         rs = slice(b * count, b * count + count)
@@ -539,8 +541,16 @@
         [x[:, b * 128 : b * 128 + 128] for b in range(NB) for x in (first, later)], axis=0
     ).astype(BF16)
     bias = jnp.concatenate([aux[8:9], aux[8:9]], axis=1)
-    mine = ((iota((NB * count, 1), 0) >> 4) & 1) == odd
-    code, slope, pay = encode_rows(jnp.concatenate(taps, axis=0), banded[...], bias, masks, mine)
+
+    def own_part(x):
+        parts = [x[i * 16 : i * 16 + 16] for i in range(2 * NB)]
+        return jnp.concatenate(
+            [jnp.where(odd == 1, y, x) for x, y in zip(parts[::2], parts[1::2])], axis=0
+        )
+
+    code, slope, pay = encode_rows(
+        jnp.concatenate(taps, axis=0), banded[...], bias, masks, own_part
+    )
     pay = pay + inner_pay[...]
     pay_out[...] = pay
     for b in range(NB):

time: 35.6 us -> 35.6 us (level)
  no operation moved by 1% of the time
where the time goes in v9:
time: 35.6 us; the launch traced here: 35.3 us
  Pallas kernels  12.7 us (36%)
  starting transfers between devices  11.4 us (32%)
  waiting for transfers between devices  9.07 us (25%)
  local copies, waits for them, and re-layouts  1.31 us (4%)
  between operations  0.76 us (2%)
    all_to_all x1, starting transfers between devices, run(): stats = lax.all_to_all(pay, ('section', 'wide'), 0, 0)  5.63 us
    all_to_all x1, waiting for transfers between devices, run(): stats = lax.all_to_all(pay, ('section', 'wide'), 0, 0)  5.08 us
    all_to_all x1, waiting for transfers between devices, run(): parts = lax.all_to_all(pay, ('section', 'wide'), 0, 0)  3.7 us
    ppermute x1, starting transfers between devices, run(): halo = lax.ppermute(halo, 'wide', pair)  3 us
    all_to_all x1, starting transfers between devices, run(): parts = lax.all_to_all(pay, ('section', 'wide'), 0, 0)  2.57 us
    pallas_call x1, Pallas kernels, run(): call(keep_kernel, 'keep', [shape(1, z.micro, z.band, z.span), shape(1, CC...  2.38 us
    pallas_call x1, Pallas kernels, run(): call(decode_kernel, 'decode', [shape(*frame), shape(CCODE, 128, dtype=F32...  2.11 us
    pallas_call x1, Pallas kernels, run(): call(send_kernel, 'send', [shape(z.mb, z.band, z.span)], [VMEM] * 5, [fra...  1.64 us
  transfers between devices with their start and end apart: 5, of which 3 were waited for; matrix products, arithmetic and copies ran while one was open for 0% of the time, Pallas kernels for 20%

profile of v9, /device:TPU:0, one launch (start us, length us, event | category | flops | bytes accessed | tf_op | source)
XLA Modules:
  0.0 35.3 jit_solution(2761158552671637778)
XLA Ops:
  0.6 0.0 copy-start.2
  0.6 0.0 copy-start
  0.7 1.1 %edge.1 = (bf16[208,128]{1,0:T(8,128)(2,1)S(1)}, bf16[16,1792]{1,0:T(8,128)(2,1)S(1)}) custom-call(bf16[8,64,512]{2,1,0:T(8,128)(2,1)} %refs_0_.4, s32[8,64,128]{2,1,0:T(8,128)} %refs_1_.3, bf16[8,64,512]{2,1,0:T(8,128)(2,1)} %refs_0_.5, bf16[1,1600]{1,0:T(2,128)(2,1)} %refs_3_.3), custom_call_target="tpu_custom_call" | custom-call | tf_op jit(solution)/shard_map/edge/pallas_call | solution.py:842
  1.7 3.0 %collective-permute-start = (bf16[208,128]{1,0:T(8,128)(2,1)S(1)}, bf16[208,128]{1,0:T(8,128)(2,1)S(1)}, u32[]{:S(2)}, u32[]{:S(2)}) collective-permute-start(bf16[208,128]{1,0:T(8,128)(2,1)S(1)} %get-tuple-element.34), channel_id=1, source_target_pairs={{0,1},{1,0},{2,3},{3,2},{4,5},{5,4},{6,7},{7,6},{8,9},{9,8},{10,11... | collective-permute-start | bytes 159752 | tf_op jit(solution)/shard_map/ppermute | solution.py:855
  4.8 0.0 collective-permute-start.1
  4.8 0.0 copy-done.2
  4.8 0.0 copy-done
  4.8 0.9 %prepare.1 = (bf16[256,640]{1,0:T(8,128)(2,1)S(1)}, bf16[256,640]{1,0:T(8,128)(2,1)S(1)}, f32[56,128]{1,0:T(8,128)S(1)}) custom-call(bf16[8,64,512]{2,1,0:T(8,128)(2,1)S(1)} %copy-done, s32[8,64,128]{2,1,0:T(8,128)S(1)} %copy-done.2, s32[8,8]{1,0:T(8,128)} %refs_2_.2, f32[16]{0:T(128)} %refs_3_.2, f32[4]{0:T(128)} %refs_4_.1, f32[16]{0:T(128)} %refs_5_.1, ...), custom_call_target="tpu_custom_call" | custom-call | flops 4000000000 | bytes 4000000 | tf_op jit(solution)/shard_map/prepare/pallas_call | solution.py:857
  5.7 0.3 collective-permute-done.1.refs_1_
  6.0 0.3 taps.1.refs_2_.refs_4_.refs_3_
  6.3 1.2 %inner.1 = (bf16[5,144,640]{2,1,0:T(8,128)(2,1)S(1)}, bf16[5,144,256]{2,1,0:T(8,128)(2,1)S(1)}, f32[5,144,256]{2,1,0:T(8,128)S(1)}, f32[2,128]{1,0:T(2,128)S(1)}, bf16[640,256]{1,0:T(8,128)(2,1)S(1)}) custom-call(bf16[256,640]{1,0:T(8,128)(2,1)S(1)} %get-tuple-element.32.refs_0_, bf16[256,640]{1,0:T(8,128)(2,1)S(1)} %get-tuple-element.33.refs_1_.refs_2_, ...), custom_call_target="tpu_custom_call" | custom-call | flops 4000000000 | bytes 4000000 | tf_op jit(solution)/shard_map/inner/pallas_call | solution.py:880
  7.6 0.0 collective-permute-done.refs_2_.refs_3_
  7.6 0.0 copy-start.1
  7.6 0.8 %encode.1 = (bf16[5,144,640]{2,1,0:T(8,128)(2,1)S(1)}, bf16[5,144,256]{2,1,0:T(8,128)(2,1)S(1)}, f32[5,144,256]{2,1,0:T(8,128)S(1)}, f32[2,128]{1,0:T(2,128)S(1)}) custom-call(bf16[256,640]{1,0:T(8,128)(2,1)S(1)} %get-tuple-element.32.refs_0_, ...), custom_call_target="tpu_custom_call", output_to_operand_aliasing={{0}: (6, {}), {1}: (7, {}), {2}: (8, {})} | custom-call | tf_op jit(solution)/shard_map/encode/pallas_call | solution.py:888
  8.5 0.6 %broadcast_in_dim.4 = f32[32,2,128]{2,1,0:T(2,128)} broadcast(f32[2,128]{1,0:T(2,128)S(1)} %get-tuple-element.42), dimensions={1,2} | broadcast | bytes 33792 | tf_op jit(solution)/shard_map/broadcast_in_dim | solution.py:896
  9.1 5.6 %all-to-all-start = ((f32[32,2,128]{2,1,0:T(2,128)}), f32[32,2,128]{2,1,0:T(2,128)S(1)}, u32[]{:S(2)}, u32[]{:S(2)}) async-start(f32[32,2,128]{2,1,0:T(2,128)} %broadcast_in_dim.4), calls=%async_computation | async-start | bytes 65536 | tf_op jit(solution)/shard_map/all_to_all | solution.py:897
  14.7 0.0 copy-done.1
  14.7 2.1 %decode.1 = (bf16[5,144,256]{2,1,0:T(8,128)(2,1)S(1)}, f32[16,128]{1,0:T(8,128)S(1)}) custom-call(bf16[8,64,512]{2,1,0:T(8,128)(2,1)S(1)} %copy-done.1, bf16[5,144,256]{2,1,0:T(8,128)(2,1)S(1)} %get-tuple-element.43.refs_1_, bf16[256,640]{1,0:T(8,128)(2,1)S(1)} %get-tuple-element.33.refs_1_.refs_2_, ...), custom_call_target="tpu_custom_call" | custom-call | flops 4000000000 | bytes 4000000 | tf_op jit(solution)/shard_map/decode/pallas_call | solution.py:898
  16.8 5.1 %all-to-all-done.refs_0_ = f32[32,2,128]{2,1,0:T(2,128)S(1)} async-done(((f32[32,2,128]{2,1,0:T(2,128)}), f32[32,2,128]{2,1,0:T(2,128)S(1)}, u32[]{:S(2)}, u32[]{:S(2)}) %all-to-all-start) | async-done | bytes 32800 | tf_op jit(solution)/shard_map/all_to_all | solution.py:897
  21.9 1.4 %whiten.1 = (bf16[5,144,256]{2,1,0:T(8,128)(2,1)S(1)}, bf16[2,16,128]{2,1,0:T(8,128)(2,1)S(1)}, f32[24,128]{1,0:T(8,128)S(1)}) custom-call(f32[32,2,128]{2,1,0:T(2,128)S(1)} %all-to-all-done.refs_0_, bf16[5,144,256]{2,1,0:T(8,128)(2,1)S(1)} %get-tuple-element.43.refs_1_, ...), custom_call_target="tpu_custom_call", output_to_operand_aliasing={{0}: (3, {})} | custom-call | tf_op jit(solution)/shard_map/whiten/pallas_call | solution.py:906
  23.3 0.7 %broadcast_in_dim.5 = bf16[2,16,16,128]{3,2,1,0:T(8,128)(2,1)} broadcast(bf16[2,16,128]{2,1,0:T(8,128)(2,1)S(1)} %get-tuple-element.48), dimensions={0,2,3} | broadcast | bytes 139264 | tf_op jit(solution)/shard_map/broadcast_in_dim | solution.py:918
  24.0 2.6 %all-to-all-start.1 = ((bf16[32,16,128]{2,1,0:T(8,128)(2,1)}), bf16[32,16,128]{2,1,0:T(8,128)(2,1)S(1)}, u32[]{:S(2)}, u32[]{:S(2)}) async-start(bf16[32,16,128]{2,1,0:T(8,128)(2,1)} %bitcast), calls=%async_computation.1 | async-start | bytes 262144 | tf_op jit(solution)/shard_map/all_to_all | solution.py:920
  26.5 1.6 %send.1 = bf16[4,64,512]{2,1,0:T(8,128)(2,1)S(1)} custom-call(bf16[5,144,256]{2,1,0:T(8,128)(2,1)S(1)} %get-tuple-element.49.refs_0_, bf16[5,144,256]{2,1,0:T(8,128)(2,1)S(1)} %get-tuple-element.43.refs_1_, bf16[256,640]{1,0:T(8,128)(2,1)S(1)} %get-tuple-element.33.refs_1_.refs_2_, bf16[128,512]{1,0:T(8,128)(2,1)S(1)} %taps.1.refs_2_.refs_4_.refs_3_, ...), custom_call_target="tpu_custom_call" | custom-call | flops 4000000000 | bytes 4000000 | tf_op jit(solution)/shard_map/send/pallas_call | solution.py:921
  28.2 0.2 collective-permute-start.2
  28.4 2.4 %keep.1 = (bf16[1,8,64,512]{3,2,1,0:T(8,128)(2,1)}, f32[1,16]{1,0:T(1,128)}, f32[16,16]{1,0:T(8,128)}) custom-call(bf16[5,144,256]{2,1,0:T(8,128)(2,1)S(1)} %get-tuple-element.49.refs_0_, bf16[5,144,256]{2,1,0:T(8,128)(2,1)S(1)} %get-tuple-element.43.refs_1_, bf16[256,640]{1,0:T(8,128)(2,1)S(1)} %get-tuple-element.33.refs_1_.refs_2_, ...), custom_call_target="tpu_custom_call" | custom-call | flops 4000000000 | bytes 4000000 | tf_op jit(solution)/shard_map/keep/pallas_call | solution.py:930
  30.8 3.7 %all-to-all-done.1.refs_0_ = bf16[32,16,128]{2,1,0:T(8,128)(2,1)S(1)} async-done(((bf16[32,16,128]{2,1,0:T(8,128)(2,1)}), bf16[32,16,128]{2,1,0:T(8,128)(2,1)S(1)}, u32[]{:S(2)}, u32[]{:S(2)}) %all-to-all-start.1) | async-done | bytes 131104 | tf_op jit(solution)/shard_map/all_to_all | solution.py:920
  34.5 0.0 collective-permute-done.2.refs_1_
  34.5 0.8 %finish.1 = (bf16[1,8,64,512]{3,2,1,0:T(8,128)(2,1)}, f32[1,1600]{1,0:T(1,128)}, f32[1,16]{1,0:T(1,128)}, f32[1,4]{1,0:T(1,128)}) custom-call(f32[16,128]{1,0:T(8,128)S(1)} %total.1.refs_0_, bf16[4,64,512]{2,1,0:T(8,128)(2,1)S(1)} %collective-permute-done.2.refs_1_, bf16[1,8,64,512]{3,2,1,0:T(8,128)(2,1)} %get-tuple-element.51.refs_2_), custom_call_target="tpu_custom_call", output_to_operand_aliasing={{0}: (2, {})} | custom-call | tf_op jit(solution)/shard_map/finish/pallas_call | solution.py:957
  (1 shorter events, 0.0 us)
Async XLA Ops:
  0.6 4.1 %copy-start.2 = (s32[8,64,128]{2,1,0:T(8,128)S(1)}, s32[8,64,128]{2,1,0:T(8,128)}, u32[]{:S(2)}) copy-start(s32[8,64,128]{2,1,0:T(8,128)} %refs_1_.3) | copy-start | bytes 786436
  0.6 4.1 %copy-start = (bf16[8,64,512]{2,1,0:T(8,128)(2,1)S(1)}, bf16[8,64,512]{2,1,0:T(8,128)(2,1)}, u32[]{:S(2)}) copy-start(bf16[8,64,512]{2,1,0:T(8,128)(2,1)} %refs_0_.4) | copy-start | bytes 1572868
  1.7 5.8 %collective-permute-start = (bf16[208,128]{1,0:T(8,128)(2,1)S(1)}, bf16[208,128]{1,0:T(8,128)(2,1)S(1)}, u32[]{:S(2)}, u32[]{:S(2)}) collective-permute-start(bf16[208,128]{1,0:T(8,128)(2,1)S(1)} %get-tuple-element.34), channel_id=1, source_target_pairs={{0,1},{1,0},{2,3},{3,2},{4,5},{5,4},{6,7},{7,6},{8,9},{9,8},{10,11... | collective-permute-start | bytes 159752 | tf_op jit(solution)/shard_map/ppermute | solution.py:855
  4.8 1.2 %collective-permute-start.1 = (bf16[16,1792]{1,0:T(8,128)(2,1)S(1)}, bf16[16,1792]{1,0:T(8,128)(2,1)S(1)}, u32[]{:S(2)}, u32[]{:S(2)}) collective-permute-start(bf16[16,1792]{1,0:T(8,128)(2,1)S(1)} %get-tuple-element.35.refs_0_), channel_id=1, source_target_pairs={{0,16},{16,0},{1,17},{17,1},{2,18},{18,2},{3,19},{19,3},{4,20},{20... | collective-permute-start | bytes 172040 | tf_op jit(solution)/shard_map/ppermute | solution.py:856
  7.6 7.1 %copy-start.1 = (bf16[8,64,512]{2,1,0:T(8,128)(2,1)S(1)}, bf16[8,64,512]{2,1,0:T(8,128)(2,1)}, u32[]{:S(2)}) copy-start(bf16[8,64,512]{2,1,0:T(8,128)(2,1)} %refs_0_.5) | copy-start | bytes 1572868
  9.1 12.8 %all-to-all-start = ((f32[32,2,128]{2,1,0:T(2,128)}), f32[32,2,128]{2,1,0:T(2,128)S(1)}, u32[]{:S(2)}, u32[]{:S(2)}) async-start(f32[32,2,128]{2,1,0:T(2,128)} %broadcast_in_dim.4), calls=%async_computation | async-start | bytes 65536 | tf_op jit(solution)/shard_map/all_to_all | solution.py:897
  24.0 10.5 %all-to-all-start.1 = ((bf16[32,16,128]{2,1,0:T(8,128)(2,1)}), bf16[32,16,128]{2,1,0:T(8,128)(2,1)S(1)}, u32[]{:S(2)}, u32[]{:S(2)}) async-start(bf16[32,16,128]{2,1,0:T(8,128)(2,1)} %bitcast), calls=%async_computation.1 | async-start | bytes 262144 | tf_op jit(solution)/shard_map/all_to_all | solution.py:920
  28.2 6.3 %collective-permute-start.2 = (bf16[4,64,512]{2,1,0:T(8,128)(2,1)S(1)}, bf16[4,64,512]{2,1,0:T(8,128)(2,1)S(1)}, u32[]{:S(2)}, u32[]{:S(2)}) collective-permute-start(bf16[4,64,512]{2,1,0:T(8,128)(2,1)S(1)} %send.1), channel_id=1, source_target_pairs={{0,16},{16,0},{1,17},{17,1},{2,18},{18,2},{3,19},{19,3},{4,20},{20... | collective-permute-start | bytes 786440 | tf_op jit(solution)/shard_map/ppermute | solution.py:929
